TPU v7x, 32 devices: a whole 2x2x4 slice. The times are simulated.
32 devices in a mesh: grp: 2 (over y), sec: 4 (over z), mpo: 4 (over x, core).
Axes of the slice: x: 2, y: 2, z: 4, core: 2. Of those that a mesh axis runs over, the one named last changes fastest.
Arguments:
- psi: bfloat16 [64, 128, 3, 128], P(('grp', 'sec')), parts along dimension 0, may hold values from -6 to 6
- left_env: bfloat16 [16, 32, 128, 128], P(('grp', 'mpo'), 'sec'), parts along dimension 0, may hold values from -0.5 to 0.5
- right_env: bfloat16 [16, 32, 128, 128], P(('grp', 'mpo'), 'sec'), parts along dimension 0, may hold values from -0.1875 to 0.1875
- site_op: bfloat16 [16, 32, 3, 3], P(('grp', 'mpo'), 'sec'), parts along dimension 0, may hold values from -3.5 to 3.5
- source: int32 [4, 32], P('mpo'), may hold values from 0 to 31, as said below
Outputs:
- product: bfloat16 [128, 64, 3, 128], P('mpo', ('grp', 'sec')), parts along dimension 1
There are 2 independent parts, one for each index of `grp`. A program takes and returns all parts, laid end to end along the dimension named above; an argument that names none is the same for every part. Nothing has to cross between parts.
Inputs may be any that keep to these rules, and one draw needn't show every extreme that they name: `source`: within each bond-charge group g and each aligned block of 8 output sectors, at most 2 entries name input sectors of one aligned block of 8 input sectors, and exactly 2 do for some block.
All inputs are finite; a program needn't handle non-finite values.
Results may differ from a plain program's by a relative error of at most 0.0058.
Values may be sent and summed in bfloat16 or wider, within the bound.
No kernel may reach another device: no remote copies, remote signals or barrier semaphores. Data moves between devices by JAX's collectives and lax.ppermute only.
A program may use at most 64 MiB of HBM per device.

v0:
```python
import jax
import jax.numpy as jnp
from jax import lax
from jax.sharding import PartitionSpec as P


def shards(psi, left_env, right_env, site_op, source):
    me_sec = lax.axis_index("sec")
    nsec = lax.axis_size("sec")
    sdev = psi.shape[0]
    blk = psi.shape[1]
    phys = psi.shape[2]
    slots = max(2, (sdev + nsec - 1) // nsec)
    table = source[0]
    owners = (table // sdev).reshape(nsec, sdev)
    mine = owners == me_sec
    ranked = jnp.cumsum(mine.astype(jnp.int32), axis=1) - 1
    picked = mine[:, None, :] & (
        ranked[:, None, :] == jnp.arange(slots, dtype=jnp.int32)[None, :, None]
    )
    local_rows = (table % sdev).reshape(nsec, sdev)
    chosen = jnp.sum(jnp.where(picked, local_rows[:, None, :], 0), axis=2)
    outgoing = jnp.take(psi, chosen.reshape(-1), axis=0).reshape(nsec, slots, blk, phys, blk)
    arrived = lax.all_to_all(outgoing, "sec", split_axis=0, concat_axis=0, tiled=True)
    my_sources = lax.dynamic_slice_in_dim(table, me_sec * sdev, sdev)
    sender = my_sources // sdev
    onehot = (sender[:, None] == jnp.arange(nsec, dtype=jnp.int32)[None, :]).astype(jnp.int32)
    slot_index = jnp.sum(jnp.cumsum(onehot, axis=0) * onehot, axis=1) - 1
    position = sender * slots + slot_index
    taken = jnp.take(arrived.reshape(nsec * slots, blk, phys, blk), position, axis=0)
    left = jnp.einsum(
        "wtab,tbpc->wtapc", left_env, taken, preferred_element_type=jnp.float32
    ).astype(jnp.bfloat16)
    mixed = jnp.einsum(
        "wtapc,wtpq->wtaqc", left, site_op, preferred_element_type=jnp.float32
    ).astype(jnp.bfloat16)
    partial_value = jnp.einsum(
        "wtaqc,wtcd->atqd", mixed, right_env, preferred_element_type=jnp.float32
    )
    summed = lax.psum_scatter(partial_value, "mpo", scatter_dimension=0, tiled=True)
    return summed.astype(jnp.bfloat16)


def solution(mesh):
    placed = (
        P(("grp", "sec"), None, None, None),
        P(("grp", "mpo"), "sec", None, None),
        P(("grp", "mpo"), "sec", None, None),
        P(("grp", "mpo"), "sec", None, None),
        P("mpo", None),
    )
    return jax.shard_map(
        shards,
        mesh=mesh,
        in_specs=placed,
        out_specs=P("mpo", ("grp", "sec"), None, None),
        check_vma=False,
    )
```

profile of v0, /device:TPU:0, one launch (start us, length us, event | category | flops | bytes accessed | tf_op | source)
XLA Modules:
  0.0 83.1 jit_solution(16464623839848542808)
XLA Ops:
  6.5 0.0 copy-start
  6.5 0.5 broadcast.215
  7.0 1.3 %reduce.3 = s32[32]{0:T(128)S(1)} reduce(s32[1,32]{1,0:T(1,128)} %param.11, s32[]{:T(128)} %broadcast.215), dimensions={0}, to_apply=%param.11.reduce_sub_computation.3 | reduce | bytes 260 | tf_op args[4]
  8.4 0.1 squeeze.3
  8.5 0.2 reduce_window_sum.22
  8.7 0.1 select_reduce_fusion
  8.8 0.1 copy.17
  8.9 0.1 reshape.131
  9.0 0.0 copy-done
  9.0 0.7 gather_fusion
  9.7 0.0 copy-start.3
  9.8 0.0 copy-start.2
  9.8 1.0 %broadcast_select_fusion = bf16[8,128,3,128]{3,1,2,0:T(8,128)(2,1)} fusion(bf16[8,128,3,128]{3,1,2,0:T(8,128)(2,1)S(1)} %gather_fusion, pred[8]{0:T(512)(128)(4,1)S(1)} %compare_and_fusion.1), kind=kLoop, calls=%fused_computation.11 | loop fusion | flops 393216 | bytes 1572872 | tf_op jit(solution)/shard_map/jit(_take)/select_n | solution.py:23
  10.8 6.3 %all-to-all-start = ((bf16[4,2,128,3,128]{4,2,3,1,0:T(8,128)(2,1)}), bf16[4,2,128,3,128]{4,2,3,1,0:T(8,128)(2,1)S(1)}, u32[]{:S(2)}, u32[]{:S(2)}) async-start(bf16[4,2,128,3,128]{4,2,3,1,0:T(8,128)(2,1)} %bitcast.1), calls=%async_computation | async-start | bytes 1572864 | tf_op jit(solution)/shard_map/all_to_all | solution.py:24
  17.1 0.0 reduce-scatter.2.cloned.1.call-start
  17.1 0.0 copy-done.3
  17.1 0.1 and_select_fusion
  17.2 0.2 reduce_window_sum.23
  17.4 0.0 copy-done.2
  17.4 0.1 copy.27
  17.5 0.1 compare_and_fusion
  17.6 19.6 %all-to-all-done = bf16[4,2,128,3,128]{4,2,3,1,0:T(8,128)(2,1)S(1)} async-done(((bf16[4,2,128,3,128]{4,2,3,1,0:T(8,128)(2,1)}), bf16[4,2,128,3,128]{4,2,3,1,0:T(8,128)(2,1)S(1)}, u32[]{:S(2)}, u32[]{:S(2)}) %all-to-all-start) | async-done | bytes 786464 | tf_op jit(solution)/shard_map/all_to_all | solution.py:24
  37.2 0.7 gather_fusion.1
  37.9 1.9 %fusion.2 = bf16[2,8,128,3,128]{2,4,0,3,1:T(8,128)(2,1)S(1)} fusion(bf16[8,128,3,128]{3,1,2,0:T(8,128)(2,1)S(1)} %gather_fusion.1, pred[8]{0:T(512)(128)(4,1)S(1)} %get-tuple-element.6, bf16[2,8,128,128]{3,2,1,0:T(8,128)(2,1)} %param.8), kind=kOutput, calls=%fused_computation.6 | convolution fusion | flops 202506240 | bytes 2883592 | tf_op jit(solution)/shard_map/wtab,tbpc->wtapc/dot_general | solution.py:31
  39.8 2.5 %copy.20 = bf16[2,8,128,3,128]{4,3,2,1,0:T(4,128)(2,1)} copy(bf16[2,8,128,3,128]{2,4,0,3,1:T(8,128)(2,1)S(1)} %fusion.2) | data formatting | bytes 3145728 | tf_op jit(solution)/shard_map/convert_element_type | solution.py:33
  42.4 0.0 copy-start.1
  42.4 2.9 %convert_bitcast_fusion = bf16[2,8,128,3,128]{4,3,2,1,0:T(4,128)(2,1)S(1)} fusion(bf16[2,8,128,3,128]{4,3,2,1,0:T(4,128)(2,1)} %copy.20, bf16[2,8,3,3,1]{2,3,4,1,0:T(4,128)(2,1)S(1)} %copy.27), kind=kOutput, calls=%fused_computation.2 | convolution fusion | flops 5505024 | bytes 3146016 | tf_op jit(solution)/shard_map/wtapc,wtpq->wtaqc/dot_general | solution.py:34
  45.2 0.0 copy-done.1
  45.2 1.8 %fusion.3 = f32[128,8,3,128]{3,0,2,1:T(8,128)} fusion(bf16[2,8,128,3,128]{4,3,2,1,0:T(4,128)(2,1)S(1)} %convert_bitcast_fusion, bf16[2,8,128,128]{3,2,1,0:T(8,128)(2,1)S(1)} %copy-done.1), kind=kOutput, calls=%fused_computation.7 | convolution fusion | flops 201326592 | bytes 3670016 | tf_op jit(solution)/shard_map/wtaqc,wtcd->atqd/dot_general | solution.py:37
  47.0 0.0 reduce-scatter.2.cloned.1.call-update
  47.0 27.4 %reduce-scatter.2.cloned.1.call-done = f32[32,8,3,128]{3,0,2,1:T(8,128)} async-done(((f32[128,8,3,128]{3,0,2,1:T(8,128)}), f32[32,8,3,128]{3,0,2,1:T(8,128)}) %reduce-scatter.2.cloned.1.call-update) | async-done | bytes 393232 | tf_op jit(solution)/shard_map/reduce_scatter | solution.py:40
  74.4 1.0 %convert_element_type.31 = bf16[32,8,3,128]{3,0,2,1:T(8,128)(2,1)S(1)} convert(f32[32,8,3,128]{3,0,2,1:T(8,128)} %reduce-scatter.2.cloned.1.call-done) | non-fusion elementwise | flops 98304 | bytes 589824 | tf_op jit(solution)/shard_map/convert_element_type | solution.py:41
  75.5 0.8 copy.24
  (8 shorter events, 0.1 us)
Async XLA Ops:
  6.5 2.5 %copy-start = (bf16[8,128,3,128]{3,1,2,0:T(8,128)(2,1)S(1)}, bf16[8,128,3,128]{3,1,2,0:T(8,128)(2,1)}, u32[]{:S(2)}) copy-start(bf16[8,128,3,128]{3,1,2,0:T(8,128)(2,1)} %param.7) | copy-start | bytes 2359300
  9.7 7.4 %copy-start.3 = (s32[1,32]{1,0:T(1,128)S(1)}, s32[1,32]{1,0:T(1,128)}, u32[]{:S(2)}) copy-start(s32[1,32]{1,0:T(1,128)} %param.11) | copy-start | bytes 388
  9.8 7.6 %copy-start.2 = (bf16[2,8,3,3]{1,0,3,2:T(2,128)(2,1)S(1)}, bf16[2,8,3,3]{1,0,3,2:T(2,128)(2,1)}, u32[]{:S(2)}) copy-start(bf16[2,8,3,3]{1,0,3,2:T(2,128)(2,1)} %param.10) | copy-start | bytes 868
  10.8 26.4 %all-to-all-start = ((bf16[4,2,128,3,128]{4,2,3,1,0:T(8,128)(2,1)}), bf16[4,2,128,3,128]{4,2,3,1,0:T(8,128)(2,1)S(1)}, u32[]{:S(2)}, u32[]{:S(2)}) async-start(bf16[4,2,128,3,128]{4,2,3,1,0:T(8,128)(2,1)} %bitcast.1), calls=%async_computation | async-start | bytes 1572864 | tf_op jit(solution)/shard_map/all_to_all | solution.py:24
  17.1 57.3 %reduce-scatter.2.cloned.1.call-start = ((), (), s32[]{:S(2)}) async-start(), calls=%async_computation.2 | async-start | bytes 1966080 | tf_op jit(solution)/shard_map/reduce_scatter | solution.py:40
  42.4 2.9 %copy-start.1 = (bf16[2,8,128,128]{3,2,1,0:T(8,128)(2,1)S(1)}, bf16[2,8,128,128]{3,2,1,0:T(8,128)(2,1)}, u32[]{:S(2)}) copy-start(bf16[2,8,128,128]{3,2,1,0:T(8,128)(2,1)} %param.9) | copy-start | bytes 1572868
Sparse Core Ops, SparseCore 0:
  47.1 27.2 reduce-scatter.1
where the time goes:
time: 83.4 us; the launch traced here: 83.1 us
  waiting for transfers between devices  47 us (56%)
  between operations  13.5 us (16%)
  matrix products  6.52 us (8%)
  starting transfers between devices  6.32 us (8%)
  local copies, waits for them, and re-layouts  5.61 us (7%)
  other arithmetic  4.12 us (5%)
    reduce_scatter x1, waiting for transfers between devices, shards(): lax.psum_scatter(partial_value, 'mpo', scatter_dimension=0, tiled=True)  27.4 us
    all_to_all x1, waiting for transfers between devices, shards(): lax.all_to_all(outgoing, 'sec', split_axis=0, concat_axis=0, tiled=True)  19.6 us
    all_to_all x1, starting transfers between devices, shards(): lax.all_to_all(outgoing, 'sec', split_axis=0, concat_axis=0, tiled=True)  6.32 us
    dot_general x1, matrix products, shards(): jnp.einsum('wtapc,wtpq->wtaqc', left, site_op, preferred_element_type=jnp...  2.88 us
    convert_element_type x1, local copies, waits for them, and re-layouts, shards(): left = jnp.einsum('wtab,tbpc->wtapc', left_env, taken, preferred_element_...  2.54 us
    dot_general x1, matrix products, shards(): jnp.einsum('wtab,tbpc->wtapc', left_env, taken, preferred_element_type=jn...  1.89 us
    dot_general x1, matrix products, shards(): jnp.einsum('wtaqc,wtcd->atqd', mixed, right_env, preferred_element_type=j...  1.75 us
  transfers between devices with their start and end apart: 2, of which 2 were waited for; matrix products, arithmetic and copies ran while one was open for 1% of the time, Pallas kernels for 0%

commit v1 on v0

--- a/solution.py
+++ b/solution.py
@@ -1,10 +1,220 @@
+import functools
+
 import jax
 import jax.numpy as jnp
 from jax import lax
+from jax.experimental import pallas as pl
+from jax.experimental.pallas import tpu as pltpu
 from jax.sharding import PartitionSpec as P
 
-
-def shards(psi, left_env, right_env, site_op, source):
+SLOTS = 2
+VMEM_BYTES = 8 * 1024 * 1024
+
+
+def space(kind):
+    return pl.BlockSpec(memory_space=kind)
+
+
+def params():
+    return pltpu.CompilerParams(vmem_limit_bytes=VMEM_BYTES)
+
+
+def pick(table, base, count, block):
+    zero = jnp.int32(0)
+    seen, places, rows = zero, [zero, zero], [zero, zero]
+    for t in range(count):
+        value = table[0, base + t]
+        owner = lax.div(value, jnp.int32(count))
+        hit = owner == block
+        row = value - owner * count
+        for j in range(SLOTS):
+            here = hit & (seen == j)
+            places[j] = jnp.where(here, jnp.int32(t), places[j])
+            rows[j] = jnp.where(here, row, rows[j])
+        seen = seen + hit.astype(jnp.int32)
+    return places, rows
+
+
+def route_kernel(nsec, sdev, table, psi, *refs):
+    outs, order, sems = refs[: nsec - 1], refs[nsec - 1], refs[nsec]
+    me = lax.axis_index("sec")
+    copies = []
+    for k in range(1, nsec):
+        other = jnp.bitwise_xor(me, k)
+        rows = pick(table, other * sdev, sdev, me)[1]
+        for j in range(SLOTS):
+            copy = pltpu.make_async_copy(psi.at[rows[j]], outs[k - 1].at[j], sems.at[k - 1, j])
+            copy.start()
+            copies.append(copy)
+    for k in range(nsec):
+        places, rows = pick(table, me * sdev, sdev, jnp.bitwise_xor(me, k))
+        for j in range(SLOTS):
+            order[k * SLOTS + j] = places[j]
+            if k == 0:
+                order[nsec * SLOTS + j] = rows[j]
+    for copy in copies:
+        copy.wait()
+
+
+def route(table, psi, nsec, sdev):
+    block = psi.shape[1:]
+    shapes = [jax.ShapeDtypeStruct((SLOTS,) + block, psi.dtype)] * (nsec - 1)
+    shapes.append(jax.ShapeDtypeStruct((nsec * SLOTS + SLOTS,), jnp.int32))
+    return pl.pallas_call(
+        functools.partial(route_kernel, nsec, sdev),
+        out_shape=shapes,
+        in_specs=[space(pltpu.SMEM), space(pl.ANY)],
+        out_specs=[space(pl.ANY)] * (nsec - 1) + [space(pltpu.SMEM)],
+        scratch_shapes=[pltpu.SemaphoreType.DMA((nsec - 1, SLOTS))],
+        compiler_params=params(),
+        name="route",
+    )(table, psi)
+
+
+def apply_kernel(classes, nsec, nmpo, order, ops, *refs):
+    ncls = len(classes)
+    blocks, left, right = refs[:ncls], refs[ncls], refs[ncls + 1]
+    keep = refs[ncls + 2]
+    sends = refs[ncls + 3 : ncls + 2 + nmpo]
+    xbuf, lbuf, rbuf, sems = refs[ncls + 2 + nmpo :]
+    wdev, sdev, blk = left.shape[0], left.shape[1], left.shape[2]
+    phys = xbuf.shape[1]
+    part = blk // nmpo
+    me = lax.axis_index("mpo")
+    places, copies = [], []
+    for i, k in enumerate(classes):
+        for j in range(SLOTS):
+            s = i * SLOTS + j
+            t = order[k * SLOTS + j]
+            row = order[nsec * SLOTS + j] if k == 0 else j
+            places.append(t)
+            mine = [
+                pltpu.make_async_copy(blocks[i].at[row], xbuf.at[s], sems.at[s, 0]),
+                pltpu.make_async_copy(left.at[:, t], lbuf.at[s], sems.at[s, 1]),
+                pltpu.make_async_copy(right.at[:, t], rbuf.at[s], sems.at[s, 2]),
+            ]
+            for copy in mine:
+                copy.start()
+            copies.append(mine)
+    for s in range(ncls * SLOTS):
+        for copy in copies[s]:
+            copy.wait()
+        rows = []
+        for w in range(wdev):
+            for m in range(nmpo):
+                start = pl.multiple_of(jnp.bitwise_xor(me, m) * part, part)
+                rows.append(lbuf[s, w, pl.ds(start, part), :])
+        lhs = jnp.concatenate(rows, axis=0)
+        lefts = []
+        for p in range(phys):
+            done = jnp.dot(lhs, xbuf[s, p], preferred_element_type=jnp.float32)
+            lefts.append(done.astype(jnp.bfloat16).astype(jnp.float32))
+        mixed = []
+        for q in range(phys):
+            across = []
+            for w in range(wdev):
+                base = ((w * sdev) + places[s]) * (phys * phys) + q
+                total = None
+                for p in range(phys):
+                    term = lefts[p][w * blk : (w + 1) * blk] * ops[base + p * phys]
+                    total = term if total is None else total + term
+                across.append(total.astype(jnp.bfloat16))
+            mixed.append(jnp.concatenate(across, axis=1))
+        rmat = rbuf[s].reshape(wdev * blk, blk)
+        for q in range(phys):
+            out = jnp.dot(mixed[q], rmat, preferred_element_type=jnp.float32)
+            keep[s, q] = out[:part]
+            for m in range(1, nmpo):
+                sends[m - 1][s, q] = out[m * part : (m + 1) * part].astype(jnp.bfloat16)
+
+
+def apply(classes, order, ops, blocks, left, right, nsec, nmpo):
+    wdev, sdev, blk = left.shape[:3]
+    phys = blocks[0].shape[1]
+    n = len(classes) * SLOTS
+    piece = (n, phys, blk // nmpo, blk)
+    shapes = [jax.ShapeDtypeStruct(piece, jnp.float32)]
+    shapes += [jax.ShapeDtypeStruct(piece, jnp.bfloat16)] * (nmpo - 1)
+    return pl.pallas_call(
+        functools.partial(apply_kernel, classes, nsec, nmpo),
+        out_shape=shapes,
+        in_specs=[space(pltpu.SMEM)] * 2 + [space(pl.ANY)] * (len(classes) + 2),
+        out_specs=[space(pltpu.VMEM)] * nmpo,
+        scratch_shapes=[
+            pltpu.VMEM((n, phys, blk, blk), jnp.bfloat16),
+            pltpu.VMEM((n, wdev, blk, blk), jnp.bfloat16),
+            pltpu.VMEM((n, wdev, blk, blk), jnp.bfloat16),
+            pltpu.SemaphoreType.DMA((n, 3)),
+        ],
+        compiler_params=params(),
+        cost_estimate=pl.CostEstimate(
+            flops=n * wdev * phys * blk**3 * 4,
+            bytes_accessed=n * (phys + 2 * wdev) * blk * blk * 2,
+            transcendentals=0,
+        ),
+        name="apply",
+    )(order, ops, *blocks, left, right)
+
+
+def merge_kernel(groups, nmpo, *refs):
+    orders = refs[:nmpo]
+    stages = refs[nmpo : nmpo + len(groups) * nmpo]
+    out, acc = refs[-2], refs[-1]
+    for m in range(nmpo):
+        for g, classes in enumerate(groups):
+            got = stages[g * nmpo + m]
+            for i, k in enumerate(classes):
+                for j in range(SLOTS):
+                    t = orders[m][k * SLOTS + j]
+                    value = got[i * SLOTS + j].astype(jnp.float32)
+                    acc[t] = value if m == 0 else acc[t] + value
+    for q in range(out.shape[1]):
+        out[:, q] = jnp.swapaxes(acc[:, q], 0, 1).astype(out.dtype)
+
+
+def merge(groups, orders, stages, sdev):
+    nmpo = len(orders)
+    phys, part, blk = stages[0][0].shape[1:]
+    flat = [array for stage in stages for array in stage]
+    return pl.pallas_call(
+        functools.partial(merge_kernel, groups, nmpo),
+        out_shape=jax.ShapeDtypeStruct((part, phys, sdev, blk), jnp.bfloat16),
+        in_specs=[space(pltpu.SMEM)] * nmpo + [space(pltpu.VMEM)] * len(flat),
+        out_specs=space(pltpu.VMEM),
+        scratch_shapes=[pltpu.VMEM((sdev, phys, part, blk), jnp.float32)],
+        compiler_params=params(),
+        name="merge",
+    )(*orders, *flat)
+
+
+def fast_shards(psi, left_env, right_env, site_op, source):
+    nsec = lax.axis_size("sec")
+    nmpo = lax.axis_size("mpo")
+    sdev = psi.shape[0]
+    blocks = jnp.transpose(psi, (0, 2, 1, 3))
+    ops = site_op.astype(jnp.float32).reshape(-1)
+    routed = route(source, blocks, nsec, sdev)
+    outgoing, order = routed[:-1], routed[-1]
+    arrived = [blocks]
+    for k in range(1, nsec):
+        arrived.append(lax.ppermute(outgoing[k - 1], "sec", [(i, i ^ k) for i in range(nsec)]))
+
+    def across(value, m):
+        return lax.ppermute(value, "mpo", [(i, i ^ m) for i in range(nmpo)])
+
+    orders = [order] + [across(order, m) for m in range(1, nmpo)]
+    groups = [tuple(range(0, nsec - 2)), (nsec - 2,), (nsec - 1,)]
+    stages = []
+    for classes in groups:
+        parts = apply(
+            classes, order, ops, [arrived[k] for k in classes], left_env, right_env, nsec, nmpo
+        )
+        stages.append([parts[0]] + [across(parts[m], m) for m in range(1, nmpo)])
+    out = merge(groups, orders, stages, sdev)
+    return jnp.transpose(out, (0, 2, 1, 3))
+
+
+def any_shards(psi, left_env, right_env, site_op, source):
     me_sec = lax.axis_index("sec")
     nsec = lax.axis_size("sec")
     sdev = psi.shape[0]
@@ -41,6 +251,14 @@
     return summed.astype(jnp.bfloat16)
 
 
+def shards(psi, left_env, right_env, site_op, source):
+    nsec = lax.axis_size("sec")
+    nmpo = lax.axis_size("mpo")
+    exact = psi.shape[0] == SLOTS * nsec and nsec == 4 and nmpo == 4
+    body = fast_shards if exact else any_shards
+    return body(psi, left_env, right_env, site_op, source)
+
+
 def solution(mesh):
     placed = (
         P(("grp", "sec"), None, None, None),

time: 83.4 us -> 46.7 us (0.56)
  waiting for transfers between devices: 47 us -> 17.5 us
  between operations: 13.5 us -> 0.1 us
  Pallas kernels: 0 us -> 10.7 us
  starting transfers between devices: 6.32 us -> 15.1 us
  matrix products: 6.52 us -> 0 us
  other arithmetic: 4.12 us -> 0 us
  local copies, waits for them, and re-layouts: 5.61 us -> 3.15 us
    reduce_scatter x1 -> x0, waiting for transfers between devices: 27.4 us -> none  [shards(): lax.psum_scatter(partial_value, 'mpo', scatter_dimension=0, tiled=True)]
    all_to_all x1 -> x0, waiting for transfers between devices: 19.6 us -> none  [shards(): lax.all_to_all(outgoing, 'sec', split_axis=0, concat_axis=0, tiled=True)]
    ppermute x0 -> x15, waiting for transfers between devices: none -> 17.5 us  [the longest x3 12.4 us: fast_shards(): lax.ppermute(outgoing[k - 1], 'sec', [(i, i ^ k) for i in range(nsec)])]
    ppermute x0 -> x15, starting transfers between devices: none -> 15.1 us  [the longest x12 9.46 us: across(): return lax.ppermute(value, 'mpo', [(i, i ^ m) for i in range(nmpo)])]
    pallas_call x0 -> x5, Pallas kernels: none -> 10.7 us  [the longest x3 6.97 us: apply(): pl.pallas_call(functools.partial(apply_kernel, classes, nsec, nmpo), out_...]
    dot_general x3 -> x0, matrix products: 6.52 us -> none  [the longest x1 2.88 us: shards(): jnp.einsum('wtapc,wtpq->wtaqc', left, site_op, preferred_element_type=jnp...]
    all_to_all x1 -> x0, starting transfers between devices: 6.32 us -> none  [shards(): lax.all_to_all(outgoing, 'sec', split_axis=0, concat_axis=0, tiled=True)]
    convert_element_type x2 -> x0, local copies, waits for them, and re-layouts: 3.29 us -> none  [the longest x1 2.54 us: shards(): left = jnp.einsum('wtab,tbpc->wtapc', left_env, taken, preferred_element_...]
  transfers between devices with their start and end apart: 2 -> 15, of which waited for: 2 -> 3; matrix products, arithmetic and copies ran while one was open for 1% -> 1% of each run, Pallas kernels for 0% -> 15%
where the time goes in v1:
time: 46.7 us; the launch traced here: 46.6 us
  waiting for transfers between devices  17.5 us (37%)
  starting transfers between devices  15.1 us (32%)
  Pallas kernels  10.7 us (23%)
  local copies, waits for them, and re-layouts  3.15 us (7%)
    ppermute x3, waiting for transfers between devices, fast_shards(): lax.ppermute(outgoing[k - 1], 'sec', [(i, i ^ k) for i in range(nsec)])  12.4 us
    ppermute x12, starting transfers between devices, across(): return lax.ppermute(value, 'mpo', [(i, i ^ m) for i in range(nmpo)])  9.46 us
    pallas_call x3, Pallas kernels, apply(): pl.pallas_call(functools.partial(apply_kernel, classes, nsec, nmpo), out_...  6.97 us
    ppermute x3, starting transfers between devices, fast_shards(): lax.ppermute(outgoing[k - 1], 'sec', [(i, i ^ k) for i in range(nsec)])  5.68 us
    ppermute x12, waiting for transfers between devices, across(): return lax.ppermute(value, 'mpo', [(i, i ^ m) for i in range(nmpo)])  5.08 us
    unnamed x14, local copies, waits for them, and re-layouts  2.91 us
    pallas_call x1, Pallas kernels, route(): pl.pallas_call(functools.partial(route_kernel, nsec, sdev), out_shape=sha...  2.24 us
    pallas_call x1, Pallas kernels, merge(): pl.pallas_call(functools.partial(merge_kernel, groups, nmpo), out_shape=j...  1.5 us
  transfers between devices with their start and end apart: 15, of which 3 were waited for; matrix products, arithmetic and copies ran while one was open for 1% of the time, Pallas kernels for 15%

profile of v1, /device:TPU:0, one launch (start us, length us, event | category | flops | bytes accessed | tf_op | source)
XLA Modules:
  0.0 46.6 jit_solution(865457106588055511)
XLA Ops:
  0.0 0.0 copy-start
  0.0 0.0 copy-start.3
  0.0 1.2 %copy-done.3 = bf16[8,128,3,128]{3,1,2,0:T(8,128)(2,1)S(1)} copy-done((bf16[8,128,3,128]{3,1,2,0:T(8,128)(2,1)S(1)}, bf16[8,128,3,128]{3,1,2,0:T(8,128)(2,1)}, u32[]{:S(2)}) %copy-start.3) | copy-done | bytes 786456
  1.2 0.7 %copy-done.5 = s32[1,32]{1,0:T(1,128)S(1)} copy-done((s32[1,32]{1,0:T(1,128)S(1)}, s32[1,32]{1,0:T(1,128)}, u32[]{:S(2)}) %copy-start.5) | copy-done | bytes 152
  1.9 2.2 %route.1 = (bf16[2,3,128,128]{3,2,1,0:T(8,128)(2,1)S(1)}, bf16[2,3,128,128]{3,2,1,0:T(8,128)(2,1)S(1)}, bf16[2,3,128,128]{3,2,1,0:T(8,128)(2,1)S(1)}, s32[10]{0:T(128)S(1)}) custom-call(s32[1,32]{1,0:T(1,128)S(1)} %copy-done.5, bf16[8,3,128,128]{3,2,1,0:T(8,128)(2,1)S(1)} %bitcast.2), custom_call_target="tpu_custom_call" | custom-call | tf_op jit(solution)/shard_map/route/pallas_call | solution.py:63
  4.1 0.0 copy-start.6
  4.1 4.1 %collective-permute-start.7 = (bf16[2,3,128,128]{3,2,1,0:T(8,128)(2,1)S(1)}, bf16[2,3,128,128]{3,2,1,0:T(8,128)(2,1)S(1)}, u32[]{:S(2)}, u32[]{:S(2)}) collective-permute-start(bf16[2,3,128,128]{3,2,1,0:T(8,128)(2,1)S(1)} %get-tuple-element.27), channel_id=1, source_target_pairs={{0,8},{4,12},{8,0},{12,4},{1,9},{5,13},{9,1},{13,5},{2,10},{6,14},... | collective-permute-start | bytes 589832 | tf_op jit(solution)/shard_map/ppermute | solution.py:200
  8.2 1.3 %collective-permute-start.11 = (bf16[2,3,128,128]{3,2,1,0:T(8,128)(2,1)S(1)}, bf16[2,3,128,128]{3,2,1,0:T(8,128)(2,1)S(1)}, u32[]{:S(2)}, u32[]{:S(2)}) collective-permute-start(bf16[2,3,128,128]{3,2,1,0:T(8,128)(2,1)S(1)} %get-tuple-element.32), channel_id=1, source_target_pairs={{0,12},{4,8},{8,4},{12,0},{1,13},{5,9},{9,5},{13,1},{2,14},{6,10},... | collective-permute-start | bytes 589832 | tf_op jit(solution)/shard_map/ppermute | solution.py:200
  9.6 0.2 collective-permute-start.3
  9.8 0.0 copy-done.6
  9.8 0.1 copy.6
  9.9 0.1 reshape.8.ops
  10.0 12.4 %collective-permute-done.7.refs_0_ = bf16[2,3,128,128]{3,2,1,0:T(8,128)(2,1)S(1)} collective-permute-done((bf16[2,3,128,128]{3,2,1,0:T(8,128)(2,1)S(1)}, bf16[2,3,128,128]{3,2,1,0:T(8,128)(2,1)S(1)}, u32[]{:S(2)}, u32[]{:S(2)}) %collective-permute-start.7) | collective-permute-done | bytes 196640 | tf_op jit(solution)/shard_map/ppermute | solution.py:200
  22.4 0.0 copy-done
  22.4 1.0 %copy-done.1 = bf16[2,8,128,128]{3,2,1,0:T(8,128)(2,1)S(1)} copy-done((bf16[2,8,128,128]{3,2,1,0:T(8,128)(2,1)S(1)}, bf16[2,8,128,128]{3,2,1,0:T(8,128)(2,1)}, u32[]{:S(2)}) %copy-start.1) | copy-done | bytes 524312
  23.5 1.9 %apply.4 = (f32[2,3,32,128]{3,2,1,0:T(8,128)S(1)}, bf16[2,3,32,128]{3,2,1,0:T(8,128)(2,1)S(1)}, bf16[2,3,32,128]{3,2,1,0:T(8,128)(2,1)S(1)}, bf16[2,3,32,128]{3,2,1,0:T(8,128)(2,1)S(1)}) custom-call(s32[10]{0:T(128)S(1)} %get-tuple-element.21.order.refs_0_, f32[144]{0:T(256)S(1)} %reshape.8.ops, bf16[2,3,128,128]{3,2,1,0:T(8,128)(2,1)S(1)} %collective-permute-done.7.refs_0_, ...), custom_call_target="tpu_custom_call" | custom-call | flops 100663296 | bytes 458752 | tf_op jit(solution)/shard_map/apply/pallas_call | solution.py:138
  25.3 0.0 copy-start.2
  25.4 0.1 collective-permute-start.10
  25.4 0.0 collective-permute-done.11.refs_0_
  25.4 1.9 %apply.5 = (f32[2,3,32,128]{3,2,1,0:T(8,128)S(1)}, bf16[2,3,32,128]{3,2,1,0:T(8,128)(2,1)S(1)}, bf16[2,3,32,128]{3,2,1,0:T(8,128)(2,1)S(1)}, bf16[2,3,32,128]{3,2,1,0:T(8,128)(2,1)S(1)}) custom-call(s32[10]{0:T(128)S(1)} %get-tuple-element.21.order.refs_0_, f32[144]{0:T(256)S(1)} %reshape.8.ops, ...), custom_call_target="tpu_custom_call" | custom-call | flops 100663296 | bytes 458752 | tf_op jit(solution)/shard_map/apply/pallas_call | solution.py:138
  27.3 2.0 %collective-permute-start.12 = (bf16[2,3,32,128]{3,2,1,0:T(8,128)(2,1)S(1)}, bf16[2,3,32,128]{3,2,1,0:T(8,128)(2,1)S(1)}, u32[]{:S(2)}, u32[]{:S(2)}) collective-permute-start(bf16[2,3,32,128]{3,2,1,0:T(8,128)(2,1)S(1)} %get-tuple-element.34), channel_id=1, source_target_pairs={{0,1},{1,0},{2,3},{3,2},{4,5},{5,4},{6,7},{7,6},{8,9},{9,8},{10,11... | collective-permute-start | bytes 147464 | tf_op jit(solution)/shard_map/ppermute | solution.py:203
  29.3 0.1 collective-permute-start
  29.4 0.3 collective-permute-start.1
  29.8 0.0 collective-permute-done.3.refs_1_
  29.8 1.5 %collective-permute-start.2 = (s32[10]{0:T(128)S(1)}, s32[10]{0:T(128)S(1)}, u32[]{:S(2)}, u32[]{:S(2)}) collective-permute-start(s32[10]{0:T(128)S(1)} %get-tuple-element.21.order.refs_0_), channel_id=1, source_target_pairs={{0,3},{1,2},{2,1},{3,0},{4,7},{5,6},{6,5},{7,4},{8,11},{9,10},{10,... | collective-permute-start | bytes 128 | tf_op jit(solution)/shard_map/ppermute | solution.py:203
  31.2 0.0 copy-done.4
  31.2 0.0 copy-done.2
  31.2 3.2 %apply.3 = (f32[4,3,32,128]{3,2,1,0:T(8,128)S(1)}, bf16[4,3,32,128]{3,2,1,0:T(8,128)(2,1)S(1)}, bf16[4,3,32,128]{3,2,1,0:T(8,128)(2,1)S(1)}, bf16[4,3,32,128]{3,2,1,0:T(8,128)(2,1)S(1)}) custom-call(s32[10]{0:T(128)S(1)} %get-tuple-element.21.order.refs_0_, f32[144]{0:T(256)S(1)} %reshape.8.ops, bf16[8,3,128,128]{3,2,1,0:T(8,128)(2,1)S(1)} %bitcast.3, ...), custom_call_target="tpu_custom_call" | custom-call | flops 201326592 | bytes 917504 | tf_op jit(solution)/shard_map/apply/pallas_call | solution.py:138
  34.4 0.0 collective-permute-done.refs_1_
  34.4 0.4 collective-permute-start.4
  34.9 0.0 collective-permute-done.1.refs_2_
  34.9 0.3 collective-permute-start.13
  35.2 0.0 collective-permute-done.2.refs_3_
  35.2 1.2 %collective-permute-start.14 = (bf16[2,3,32,128]{3,2,1,0:T(8,128)(2,1)S(1)}, bf16[2,3,32,128]{3,2,1,0:T(8,128)(2,1)S(1)}, u32[]{:S(2)}, u32[]{:S(2)}) collective-permute-start(bf16[2,3,32,128]{3,2,1,0:T(8,128)(2,1)S(1)} %get-tuple-element.36), channel_id=1, source_target_pairs={{0,3},{1,2},{2,1},{3,0},{4,7},{5,6},{6,5},{7,4},{8,11},{9,10},{10,... | collective-permute-start | bytes 147464 | tf_op jit(solution)/shard_map/ppermute | solution.py:203
  36.4 0.0 collective-permute-done.10.refs_11_
  36.4 0.6 %collective-permute-start.5 = (bf16[4,3,32,128]{3,2,1,0:T(8,128)(2,1)S(1)}, bf16[4,3,32,128]{3,2,1,0:T(8,128)(2,1)S(1)}, u32[]{:S(2)}, u32[]{:S(2)}) collective-permute-start(bf16[4,3,32,128]{3,2,1,0:T(8,128)(2,1)S(1)} %get-tuple-element.25), channel_id=1, source_target_pairs={{0,2},{1,3},{2,0},{3,1},{4,6},{5,7},{6,4},{7,5},{8,10},{9,11},{10,... | collective-permute-start | bytes 294920 | tf_op jit(solution)/shard_map/ppermute | solution.py:203
  37.0 0.0 collective-permute-done.12.refs_13_
  37.0 1.4 %collective-permute-start.6 = (bf16[4,3,32,128]{3,2,1,0:T(8,128)(2,1)S(1)}, bf16[4,3,32,128]{3,2,1,0:T(8,128)(2,1)S(1)}, u32[]{:S(2)}, u32[]{:S(2)}) collective-permute-start(bf16[4,3,32,128]{3,2,1,0:T(8,128)(2,1)S(1)} %get-tuple-element.26), channel_id=1, source_target_pairs={{0,3},{1,2},{2,1},{3,0},{4,7},{5,6},{6,5},{7,4},{8,11},{9,10},{10,... | collective-permute-start | bytes 294920 | tf_op jit(solution)/shard_map/ppermute | solution.py:203
  38.4 0.9 %collective-permute-done.13.refs_14_ = bf16[2,3,32,128]{3,2,1,0:T(8,128)(2,1)S(1)} collective-permute-done((bf16[2,3,32,128]{3,2,1,0:T(8,128)(2,1)S(1)}, bf16[2,3,32,128]{3,2,1,0:T(8,128)(2,1)S(1)}, u32[]{:S(2)}, u32[]{:S(2)}) %collective-permute-start.13) | collective-permute-done | bytes 49184 | tf_op jit(solution)/shard_map/ppermute | solution.py:203
  39.2 0.0 collective-permute-start.8
  39.3 0.0 collective-permute-done.14.refs_15_
  39.3 1.6 %collective-permute-start.9 = (bf16[2,3,32,128]{3,2,1,0:T(8,128)(2,1)S(1)}, bf16[2,3,32,128]{3,2,1,0:T(8,128)(2,1)S(1)}, u32[]{:S(2)}, u32[]{:S(2)}) collective-permute-start(bf16[2,3,32,128]{3,2,1,0:T(8,128)(2,1)S(1)} %get-tuple-element.30), channel_id=1, source_target_pairs={{0,2},{1,3},{2,0},{3,1},{4,6},{5,7},{6,4},{7,5},{8,10},{9,11},{10,... | collective-permute-start | bytes 147464 | tf_op jit(solution)/shard_map/ppermute | solution.py:203
  40.9 0.0 collective-permute-done.8.refs_9_
  40.9 4.2 %collective-permute-done.9.refs_10_ = bf16[2,3,32,128]{3,2,1,0:T(8,128)(2,1)S(1)} collective-permute-done((bf16[2,3,32,128]{3,2,1,0:T(8,128)(2,1)S(1)}, bf16[2,3,32,128]{3,2,1,0:T(8,128)(2,1)S(1)}, u32[]{:S(2)}, u32[]{:S(2)}) %collective-permute-start.9) | collective-permute-done | bytes 49184 | tf_op jit(solution)/shard_map/ppermute | solution.py:203
  45.0 0.0 collective-permute-done.4.refs_5_
  45.0 0.0 collective-permute-done.5.refs_6_
  45.0 0.0 collective-permute-done.6.refs_7_
  45.1 1.5 %merge.1 = bf16[32,3,8,128]{3,2,1,0:T(8,128)(2,1)} custom-call(s32[10]{0:T(128)S(1)} %get-tuple-element.21.order.refs_0_, s32[10]{0:T(128)S(1)} %collective-permute-done.refs_1_, s32[10]{0:T(128)S(1)} %collective-permute-done.1.refs_2_, s32[10]{0:T(128)S(1)} %collective-permute-done.2.refs_3_, f32[4,3,32,128]{3,2,1,0:T(8,128)S(1)} %get-tuple-element.23.refs_4_, ...), custom_call_target="tpu_custom_call" | custom-call | tf_op jit(solution)/shard_map/merge/pallas_call | solution.py:179
  (3 shorter events, 0.0 us)
Async XLA Ops:
  0.0 22.4 %copy-start = (bf16[2,8,128,128]{3,2,1,0:T(8,128)(2,1)S(1)}, bf16[2,8,128,128]{3,2,1,0:T(8,128)(2,1)}, u32[]{:S(2)}) copy-start(bf16[2,8,128,128]{3,2,1,0:T(8,128)(2,1)} %refs_1_.3) | copy-start | bytes 1572868
  0.0 1.2 %copy-start.3 = (bf16[8,128,3,128]{3,1,2,0:T(8,128)(2,1)S(1)}, bf16[8,128,3,128]{3,1,2,0:T(8,128)(2,1)}, u32[]{:S(2)}) copy-start(bf16[8,128,3,128]{3,1,2,0:T(8,128)(2,1)} %param.5) | copy-start | bytes 2359300
  1.2 0.7 %copy-start.5 = (s32[1,32]{1,0:T(1,128)S(1)}, s32[1,32]{1,0:T(1,128)}, u32[]{:S(2)}) copy-start(s32[1,32]{1,0:T(1,128)} %table.1) | copy-start | bytes 388
  4.1 5.7 %copy-start.6 = (bf16[2,8,3,3]{1,0,3,2:T(2,128)(2,1)S(1)}, bf16[2,8,3,3]{1,0,3,2:T(2,128)(2,1)}, u32[]{:S(2)}) copy-start(bf16[2,8,3,3]{1,0,3,2:T(2,128)(2,1)} %param.8) | copy-start | bytes 868
  4.1 18.3 %collective-permute-start.7 = (bf16[2,3,128,128]{3,2,1,0:T(8,128)(2,1)S(1)}, bf16[2,3,128,128]{3,2,1,0:T(8,128)(2,1)S(1)}, u32[]{:S(2)}, u32[]{:S(2)}) collective-permute-start(bf16[2,3,128,128]{3,2,1,0:T(8,128)(2,1)S(1)} %get-tuple-element.27), channel_id=1, source_target_pairs={{0,8},{4,12},{8,0},{12,4},{1,9},{5,13},{9,1},{13,5},{2,10},{6,14},... | collective-permute-start | bytes 589832 | tf_op jit(solution)/shard_map/ppermute | solution.py:200
  8.2 17.2 %collective-permute-start.11 = (bf16[2,3,128,128]{3,2,1,0:T(8,128)(2,1)S(1)}, bf16[2,3,128,128]{3,2,1,0:T(8,128)(2,1)S(1)}, u32[]{:S(2)}, u32[]{:S(2)}) collective-permute-start(bf16[2,3,128,128]{3,2,1,0:T(8,128)(2,1)S(1)} %get-tuple-element.32), channel_id=1, source_target_pairs={{0,12},{4,8},{8,4},{12,0},{1,13},{5,9},{9,5},{13,1},{2,14},{6,10},... | collective-permute-start | bytes 589832 | tf_op jit(solution)/shard_map/ppermute | solution.py:200
  9.6 20.2 %collective-permute-start.3 = (bf16[2,3,128,128]{3,2,1,0:T(8,128)(2,1)S(1)}, bf16[2,3,128,128]{3,2,1,0:T(8,128)(2,1)S(1)}, u32[]{:S(2)}, u32[]{:S(2)}) collective-permute-start(bf16[2,3,128,128]{3,2,1,0:T(8,128)(2,1)S(1)} %get-tuple-element.22), channel_id=1, source_target_pairs={{0,4},{4,0},{8,12},{12,8},{1,5},{5,1},{9,13},{13,9},{2,6},{6,2},{1... | collective-permute-start | bytes 589832 | tf_op jit(solution)/shard_map/ppermute | solution.py:200
  22.4 1.0 %copy-start.1 = (bf16[2,8,128,128]{3,2,1,0:T(8,128)(2,1)S(1)}, bf16[2,8,128,128]{3,2,1,0:T(8,128)(2,1)}, u32[]{:S(2)}) copy-start(bf16[2,8,128,128]{3,2,1,0:T(8,128)(2,1)} %refs_2_.5) | copy-start | bytes 1572868
  23.5 7.8 %copy-start.4 = (bf16[8,128,3,128]{3,1,2,0:T(8,128)(2,1)S(1)}, bf16[8,128,3,128]{3,1,2,0:T(8,128)(2,1)}, u32[]{:S(2)}) copy-start(bf16[8,128,3,128]{3,1,2,0:T(8,128)(2,1)} %param.5) | copy-start | bytes 2359300
  25.3 5.9 %copy-start.2 = (bf16[2,8,128,128]{3,2,1,0:T(8,128)(2,1)S(1)}, bf16[2,8,128,128]{3,2,1,0:T(8,128)(2,1)}, u32[]{:S(2)}) copy-start(bf16[2,8,128,128]{3,2,1,0:T(8,128)(2,1)} %refs_2_.5) | copy-start | bytes 1572868
  25.4 11.0 %collective-permute-start.10 = (bf16[2,3,32,128]{3,2,1,0:T(8,128)(2,1)S(1)}, bf16[2,3,32,128]{3,2,1,0:T(8,128)(2,1)S(1)}, u32[]{:S(2)}, u32[]{:S(2)}) collective-permute-start(bf16[2,3,32,128]{3,2,1,0:T(8,128)(2,1)S(1)} %get-tuple-element.31), channel_id=1, source_target_pairs={{0,3},{1,2},{2,1},{3,0},{4,7},{5,6},{6,5},{7,4},{8,11},{9,10},{10,... | collective-permute-start | bytes 147464 | tf_op jit(solution)/shard_map/ppermute | solution.py:203
  27.3 9.7 %collective-permute-start.12 = (bf16[2,3,32,128]{3,2,1,0:T(8,128)(2,1)S(1)}, bf16[2,3,32,128]{3,2,1,0:T(8,128)(2,1)S(1)}, u32[]{:S(2)}, u32[]{:S(2)}) collective-permute-start(bf16[2,3,32,128]{3,2,1,0:T(8,128)(2,1)S(1)} %get-tuple-element.34), channel_id=1, source_target_pairs={{0,1},{1,0},{2,3},{3,2},{4,5},{5,4},{6,7},{7,6},{8,9},{9,8},{10,11... | collective-permute-start | bytes 147464 | tf_op jit(solution)/shard_map/ppermute | solution.py:203
  29.3 5.1 %collective-permute-start = (s32[10]{0:T(128)S(1)}, s32[10]{0:T(128)S(1)}, u32[]{:S(2)}, u32[]{:S(2)}) collective-permute-start(s32[10]{0:T(128)S(1)} %get-tuple-element.21.order.refs_0_), channel_id=1, source_target_pairs={{0,1},{1,0},{2,3},{3,2},{4,5},{5,4},{6,7},{7,6},{8,9},{9,8},{10,11... | collective-permute-start | bytes 128 | tf_op jit(solution)/shard_map/ppermute | solution.py:203
  29.4 5.4 %collective-permute-start.1 = (s32[10]{0:T(128)S(1)}, s32[10]{0:T(128)S(1)}, u32[]{:S(2)}, u32[]{:S(2)}) collective-permute-start(s32[10]{0:T(128)S(1)} %get-tuple-element.21.order.refs_0_), channel_id=1, source_target_pairs={{0,2},{1,3},{2,0},{3,1},{4,6},{5,7},{6,4},{7,5},{8,10},{9,11},{10,... | collective-permute-start | bytes 128 | tf_op jit(solution)/shard_map/ppermute | solution.py:203
  29.8 5.4 %collective-permute-start.2 = (s32[10]{0:T(128)S(1)}, s32[10]{0:T(128)S(1)}, u32[]{:S(2)}, u32[]{:S(2)}) collective-permute-start(s32[10]{0:T(128)S(1)} %get-tuple-element.21.order.refs_0_), channel_id=1, source_target_pairs={{0,3},{1,2},{2,1},{3,0},{4,7},{5,6},{6,5},{7,4},{8,11},{9,10},{10,... | collective-permute-start | bytes 128 | tf_op jit(solution)/shard_map/ppermute | solution.py:203
  34.4 10.6 %collective-permute-start.4 = (bf16[4,3,32,128]{3,2,1,0:T(8,128)(2,1)S(1)}, bf16[4,3,32,128]{3,2,1,0:T(8,128)(2,1)S(1)}, u32[]{:S(2)}, u32[]{:S(2)}) collective-permute-start(bf16[4,3,32,128]{3,2,1,0:T(8,128)(2,1)S(1)} %get-tuple-element.24), channel_id=1, source_target_pairs={{0,1},{1,0},{2,3},{3,2},{4,5},{5,4},{6,7},{7,6},{8,9},{9,8},{10,11... | collective-permute-start | bytes 294920 | tf_op jit(solution)/shard_map/ppermute | solution.py:203
  34.9 4.4 %collective-permute-start.13 = (bf16[2,3,32,128]{3,2,1,0:T(8,128)(2,1)S(1)}, bf16[2,3,32,128]{3,2,1,0:T(8,128)(2,1)S(1)}, u32[]{:S(2)}, u32[]{:S(2)}) collective-permute-start(bf16[2,3,32,128]{3,2,1,0:T(8,128)(2,1)S(1)} %get-tuple-element.35), channel_id=1, source_target_pairs={{0,2},{1,3},{2,0},{3,1},{4,6},{5,7},{6,4},{7,5},{8,10},{9,11},{10,... | collective-permute-start | bytes 147464 | tf_op jit(solution)/shard_map/ppermute | solution.py:203
  35.2 4.0 %collective-permute-start.14 = (bf16[2,3,32,128]{3,2,1,0:T(8,128)(2,1)S(1)}, bf16[2,3,32,128]{3,2,1,0:T(8,128)(2,1)S(1)}, u32[]{:S(2)}, u32[]{:S(2)}) collective-permute-start(bf16[2,3,32,128]{3,2,1,0:T(8,128)(2,1)S(1)} %get-tuple-element.36), channel_id=1, source_target_pairs={{0,3},{1,2},{2,1},{3,0},{4,7},{5,6},{6,5},{7,4},{8,11},{9,10},{10,... | collective-permute-start | bytes 147464 | tf_op jit(solution)/shard_map/ppermute | solution.py:203
  36.4 8.7 %collective-permute-start.5 = (bf16[4,3,32,128]{3,2,1,0:T(8,128)(2,1)S(1)}, bf16[4,3,32,128]{3,2,1,0:T(8,128)(2,1)S(1)}, u32[]{:S(2)}, u32[]{:S(2)}) collective-permute-start(bf16[4,3,32,128]{3,2,1,0:T(8,128)(2,1)S(1)} %get-tuple-element.25), channel_id=1, source_target_pairs={{0,2},{1,3},{2,0},{3,1},{4,6},{5,7},{6,4},{7,5},{8,10},{9,11},{10,... | collective-permute-start | bytes 294920 | tf_op jit(solution)/shard_map/ppermute | solution.py:203
  37.0 8.1 %collective-permute-start.6 = (bf16[4,3,32,128]{3,2,1,0:T(8,128)(2,1)S(1)}, bf16[4,3,32,128]{3,2,1,0:T(8,128)(2,1)S(1)}, u32[]{:S(2)}, u32[]{:S(2)}) collective-permute-start(bf16[4,3,32,128]{3,2,1,0:T(8,128)(2,1)S(1)} %get-tuple-element.26), channel_id=1, source_target_pairs={{0,3},{1,2},{2,1},{3,0},{4,7},{5,6},{6,5},{7,4},{8,11},{9,10},{10,... | collective-permute-start | bytes 294920 | tf_op jit(solution)/shard_map/ppermute | solution.py:203
  39.2 1.6 %collective-permute-start.8 = (bf16[2,3,32,128]{3,2,1,0:T(8,128)(2,1)S(1)}, bf16[2,3,32,128]{3,2,1,0:T(8,128)(2,1)S(1)}, u32[]{:S(2)}, u32[]{:S(2)}) collective-permute-start(bf16[2,3,32,128]{3,2,1,0:T(8,128)(2,1)S(1)} %get-tuple-element.29), channel_id=1, source_target_pairs={{0,1},{1,0},{2,3},{3,2},{4,5},{5,4},{6,7},{7,6},{8,9},{9,8},{10,11... | collective-permute-start | bytes 147464 | tf_op jit(solution)/shard_map/ppermute | solution.py:203
  39.3 5.8 %collective-permute-start.9 = (bf16[2,3,32,128]{3,2,1,0:T(8,128)(2,1)S(1)}, bf16[2,3,32,128]{3,2,1,0:T(8,128)(2,1)S(1)}, u32[]{:S(2)}, u32[]{:S(2)}) collective-permute-start(bf16[2,3,32,128]{3,2,1,0:T(8,128)(2,1)S(1)} %get-tuple-element.30), channel_id=1, source_target_pairs={{0,2},{1,3},{2,0},{3,1},{4,6},{5,7},{6,4},{7,5},{8,10},{9,11},{10,... | collective-permute-start | bytes 147464 | tf_op jit(solution)/shard_map/ppermute | solution.py:203

commit v2 on v0

--- a/solution.py
+++ b/solution.py
@@ -1,10 +1,285 @@
+import functools
+
 import jax
 import jax.numpy as jnp
 from jax import lax
+from jax.experimental import pallas as pl
+from jax.experimental.pallas import tpu as pltpu
 from jax.sharding import PartitionSpec as P
 
-
-def shards(psi, left_env, right_env, site_op, source):
+SLOTS = 2
+EARLY = 2
+VMEM_BYTES = 16 * 1024 * 1024
+
+
+def space(kind):
+    return pl.BlockSpec(memory_space=kind)
+
+
+def params():
+    return pltpu.CompilerParams(vmem_limit_bytes=VMEM_BYTES)
+
+
+def split(value, count):
+    if count & (count - 1) == 0:
+        shift = count.bit_length() - 1
+        return jnp.right_shift(value, shift), jnp.bitwise_and(value, count - 1)
+    owner = lax.div(value, jnp.int32(count))
+    return owner, value - owner * count
+
+
+def pick(table, base, count, block):
+    zero = jnp.int32(0)
+    seen, places, rows = zero, [zero, zero], [zero, zero]
+    for t in range(count):
+        owner, row = split(table[0, base + t], count)
+        hit = owner == block
+        for j in range(SLOTS):
+            here = hit & (seen == j)
+            places[j] = jnp.where(here, jnp.int32(t), places[j])
+            rows[j] = jnp.where(here, row, rows[j])
+        seen = seen + hit.astype(jnp.int32)
+    return places, rows
+
+
+def route_kernel(nsec, sdev, source, psi, *refs):
+    outs, order, table, load, sems = refs[: nsec - 1], *refs[nsec - 1 :]
+    me = lax.axis_index("sec")
+    fetch = pltpu.make_async_copy(source, table, load)
+    fetch.start()
+    fetch.wait()
+    copies = []
+    for k in range(1, nsec):
+        other = jnp.bitwise_xor(me, k)
+        rows = pick(table, other * sdev, sdev, me)[1]
+        for j in range(SLOTS):
+            copy = pltpu.make_async_copy(psi.at[rows[j]], outs[k - 1].at[j], sems.at[k - 1, j])
+            copy.start()
+            copies.append(copy)
+    for k in range(nsec):
+        places, rows = pick(table, me * sdev, sdev, jnp.bitwise_xor(me, k))
+        for j in range(SLOTS):
+            order[k * SLOTS + j] = places[j]
+            if k == 0:
+                order[nsec * SLOTS + j] = rows[j]
+    for copy in copies:
+        copy.wait()
+
+
+def route(source, psi, nsec, sdev):
+    block = psi.shape[1:]
+    shapes = [jax.ShapeDtypeStruct((SLOTS,) + block, psi.dtype)] * (nsec - 1)
+    shapes.append(jax.ShapeDtypeStruct((nsec * SLOTS + SLOTS,), jnp.int32))
+    return pl.pallas_call(
+        functools.partial(route_kernel, nsec, sdev),
+        out_shape=shapes,
+        in_specs=[space(pltpu.HBM), space(pltpu.HBM)],
+        out_specs=[space(pl.ANY)] * (nsec - 1) + [space(pltpu.SMEM)],
+        scratch_shapes=[
+            pltpu.SMEM(source.shape, jnp.int32),
+            pltpu.SemaphoreType.DMA,
+            pltpu.SemaphoreType.DMA((nsec - 1, SLOTS)),
+        ],
+        compiler_params=params(),
+        name="route",
+    )(source, psi)
+
+
+def product(lhs, block, rhs, ops, base, wdev, phys):
+    rows = lhs.shape[0] // wdev
+    lefts = []
+    for p in range(phys):
+        done = jnp.dot(lhs, block[p], preferred_element_type=jnp.float32)
+        lefts.append(done.astype(jnp.bfloat16).astype(jnp.float32))
+    outs = []
+    for q in range(phys):
+        across = []
+        for w in range(wdev):
+            total = None
+            for p in range(phys):
+                term = lefts[p][w * rows : (w + 1) * rows] * ops[base[w] + p * phys + q]
+                total = term if total is None else total + term
+            across.append(total.astype(jnp.bfloat16))
+        mixed = jnp.concatenate(across, axis=1)
+        outs.append(jnp.dot(mixed, rhs, preferred_element_type=jnp.float32))
+    return outs
+
+
+def op_base(t, wdev, sdev, phys):
+    return [(w * sdev + t) * (phys * phys) for w in range(wdev)]
+
+
+def early_kernel(nsec, nmpo, order, ops, psi, near_block, left, right, *refs):
+    far_keep, far_give, near_keep, near_give, lfar, lnear, rstage, local, sems = refs
+    wdev, sdev, blk = left.shape[:3]
+    phys = local.shape[1]
+    part = blk // nmpo
+    me = lax.axis_index("mpo")
+    copies = []
+    for j in range(SLOTS):
+        copy = pltpu.make_async_copy(psi.at[order[nsec * SLOTS + j]], local.at[j], sems.at[j])
+        copy.start()
+        copies.append(copy)
+
+    def rows(w, t, m):
+        start = pl.multiple_of(jnp.bitwise_xor(me, m) * part, part)
+        return left[w, t, pl.ds(start, part), :]
+
+    for s in range((nsec - EARLY) * SLOTS):
+        t = order[EARLY * SLOTS + s]
+        lfar[s] = jnp.concatenate([rows(w, t, m) for w in range(wdev) for m in (2, 3)], axis=0)
+        lnear[s] = jnp.concatenate([rows(w, t, m) for w in range(wdev) for m in (0, 1)], axis=0)
+        rstage[s] = right[:, t].reshape(wdev * blk, blk)
+    for copy in copies:
+        copy.wait()
+    for k in (1, 0):
+        for j in range(SLOTS):
+            s = k * SLOTS + j
+            t = order[s]
+            lhs = jnp.concatenate(
+                [rows(w, t, m) for w in range(wdev) for m in (2, 3, 0, 1)], axis=0
+            )
+            rhs = right[:, t].reshape(wdev * blk, blk)
+            source = near_block if k == 1 else local
+            block = [source[j, p] for p in range(phys)]
+            outs = product(lhs, block, rhs, ops, op_base(t, wdev, sdev, phys), wdev, phys)
+            for q in range(phys):
+                far_keep[s, q] = outs[q][:part]
+                far_give[s, q] = outs[q][part : 2 * part].astype(jnp.bfloat16)
+                near_keep[s, q] = outs[q][2 * part : 3 * part]
+                near_give[s, q] = outs[q][3 * part :].astype(jnp.bfloat16)
+
+
+def early(order, ops, psi, near_block, left, right, nsec, nmpo):
+    wdev, sdev, blk = left.shape[:3]
+    phys = psi.shape[1]
+    part = blk // nmpo
+    n, late_n = EARLY * SLOTS, (nsec - EARLY) * SLOTS
+    keep = jax.ShapeDtypeStruct((n, phys, part, blk), jnp.float32)
+    give = jax.ShapeDtypeStruct((n, phys, part, blk), jnp.bfloat16)
+    half = jax.ShapeDtypeStruct((late_n, wdev * 2 * part, blk), jnp.bfloat16)
+    whole = jax.ShapeDtypeStruct((late_n, wdev * blk, blk), jnp.bfloat16)
+    return pl.pallas_call(
+        functools.partial(early_kernel, nsec, nmpo),
+        out_shape=[keep, give, keep, give, half, half, whole],
+        in_specs=[space(pltpu.SMEM)] * 2 + [space(pltpu.HBM)] + [space(pltpu.VMEM)] * 3,
+        out_specs=[space(pltpu.VMEM)] * 7,
+        scratch_shapes=[
+            pltpu.VMEM((SLOTS, phys, blk, blk), jnp.bfloat16),
+            pltpu.SemaphoreType.DMA((SLOTS,)),
+        ],
+        compiler_params=params(),
+        cost_estimate=pl.CostEstimate(
+            flops=n * wdev * phys * blk**3 * 4,
+            bytes_accessed=8 * 1024 * 1024,
+            transcendentals=0,
+        ),
+        name="early",
+    )(order, ops, psi, near_block, left, right)
+
+
+def late_kernel(nsec, wdev, sdev, order, ops, *refs):
+    nlate = nsec - EARLY
+    blocks, (lside, rstage, early_keep, early_give, keep, give) = refs[:nlate], refs[nlate:]
+    phys, part = keep.shape[1], keep.shape[2]
+    for s in range(EARLY * SLOTS):
+        t = order[s]
+        keep[t] = early_keep[s]
+        give[t] = early_give[s]
+    for s in range(nlate * SLOTS):
+        t = order[EARLY * SLOTS + s]
+        block = [blocks[s // SLOTS][s % SLOTS, p] for p in range(phys)]
+        base = op_base(t, wdev, sdev, phys)
+        outs = product(lside[s], block, rstage[s], ops, base, wdev, phys)
+        for q in range(phys):
+            keep[t, q] = outs[q][:part]
+            give[t, q] = outs[q][part:].astype(jnp.bfloat16)
+
+
+def late(order, ops, blocks, lside, rstage, early_keep, early_give, nsec, wdev, sdev):
+    phys, part, blk = early_keep.shape[1:]
+    n = len(blocks) * SLOTS
+    return pl.pallas_call(
+        functools.partial(late_kernel, nsec, wdev, sdev),
+        out_shape=[
+            jax.ShapeDtypeStruct((sdev, phys, part, blk), jnp.float32),
+            jax.ShapeDtypeStruct((sdev, phys, part, blk), jnp.bfloat16),
+        ],
+        in_specs=[space(pltpu.SMEM)] * 2 + [space(pltpu.VMEM)] * (len(blocks) + 4),
+        out_specs=[space(pltpu.VMEM)] * 2,
+        compiler_params=params(),
+        cost_estimate=pl.CostEstimate(
+            flops=n * wdev * phys * blk**3 * 2,
+            bytes_accessed=4 * 1024 * 1024,
+            transcendentals=0,
+        ),
+        name="late",
+    )(order, ops, *blocks, lside, rstage, early_keep, early_give)
+
+
+def pair_kernel(keep, got, out):
+    out[...] = (keep[...] + got[...].astype(jnp.float32)).astype(out.dtype)
+
+
+def pair(keep, got):
+    return pl.pallas_call(
+        pair_kernel,
+        out_shape=jax.ShapeDtypeStruct(got.shape, got.dtype),
+        in_specs=[space(pltpu.VMEM)] * 2,
+        out_specs=space(pltpu.VMEM),
+        compiler_params=params(),
+        name="pair",
+    )(keep, got)
+
+
+def finish_kernel(keep, near, far, out):
+    for q in range(out.shape[1]):
+        total = keep[:, q] + near[:, q].astype(jnp.float32) + far[:, q].astype(jnp.float32)
+        out[:, q] = jnp.swapaxes(total, 0, 1).astype(out.dtype)
+
+
+def finish(keep, near, far):
+    sdev, phys, part, blk = keep.shape
+    return pl.pallas_call(
+        finish_kernel,
+        out_shape=jax.ShapeDtypeStruct((part, phys, sdev, blk), jnp.bfloat16),
+        in_specs=[space(pltpu.VMEM)] * 3,
+        out_specs=space(pltpu.VMEM),
+        compiler_params=params(),
+        name="finish",
+    )(keep, near, far)
+
+
+def fast_shards(psi, left_env, right_env, site_op, source):
+    nsec = lax.axis_size("sec")
+    nmpo = lax.axis_size("mpo")
+    sdev = psi.shape[0]
+    wdev = left_env.shape[0]
+    blocks = jnp.transpose(psi, (0, 2, 1, 3))
+    ops = site_op.astype(jnp.float32).reshape(-1)
+    routed = route(source, blocks, nsec, sdev)
+    outgoing, order = routed[:-1], routed[-1]
+    arrived = []
+    for k in range(1, nsec):
+        arrived.append(lax.ppermute(outgoing[k - 1], "sec", [(i, i ^ k) for i in range(nsec)]))
+
+    def across(value, m):
+        return lax.ppermute(value, "mpo", [(i, i ^ m) for i in range(nmpo)])
+
+    far_keep, far_give, near_keep, near_give, lfar, lnear, rstage = early(
+        order, ops, blocks, arrived[0], left_env, right_env, nsec, nmpo
+    )
+    rest = arrived[1:]
+    keep_far, give_far = late(order, ops, rest, lfar, rstage, far_keep, far_give, nsec, wdev, sdev)
+    over = across(pair(keep_far, across(give_far, 1)), 2)
+    keep_near, give_near = late(
+        order, ops, rest, lnear, rstage, near_keep, near_give, nsec, wdev, sdev
+    )
+    out = finish(keep_near, across(give_near, 1), over)
+    return jnp.transpose(out, (0, 2, 1, 3))
+
+
+def any_shards(psi, left_env, right_env, site_op, source):
     me_sec = lax.axis_index("sec")
     nsec = lax.axis_size("sec")
     sdev = psi.shape[0]
@@ -41,6 +316,14 @@
     return summed.astype(jnp.bfloat16)
 
 
+def shards(psi, left_env, right_env, site_op, source):
+    nsec = lax.axis_size("sec")
+    nmpo = lax.axis_size("mpo")
+    exact = psi.shape[0] == SLOTS * nsec and nsec == 4 and nmpo == 4
+    body = fast_shards if exact else any_shards
+    return body(psi, left_env, right_env, site_op, source)
+
+
 def solution(mesh):
     placed = (
         P(("grp", "sec"), None, None, None),

time: 83.4 us -> 36.2 us (0.43)
  the two profiles are of different devices: /device:TPU:0 before, /device:TPU:10 now
where the time goes in v2:
time: 36.2 us; the launch traced here: 35.9 us
  waiting for transfers between devices  18.9 us (52%)
  Pallas kernels  8.09 us (22%)
  starting transfers between devices  4.78 us (13%)
  local copies, waits for them, and re-layouts  4.13 us (11%)
    ppermute x3, waiting for transfers between devices, fast_shards(): lax.ppermute(outgoing[k - 1], 'sec', [(i, i ^ k) for i in range(nsec)])  12.6 us
    ppermute x3, waiting for transfers between devices, across(): return lax.ppermute(value, 'mpo', [(i, i ^ m) for i in range(nmpo)])  6.3 us
    unnamed x12, local copies, waits for them, and re-layouts  3.88 us
    ppermute x3, starting transfers between devices, fast_shards(): lax.ppermute(outgoing[k - 1], 'sec', [(i, i ^ k) for i in range(nsec)])  3.55 us
    pallas_call x2, Pallas kernels, late(): pl.pallas_call(functools.partial(late_kernel, nsec, wdev, sdev), out_shap...  2.99 us
    pallas_call x1, Pallas kernels, route(): pl.pallas_call(functools.partial(route_kernel, nsec, sdev), out_shape=sha...  2.16 us
    pallas_call x1, Pallas kernels, early(): pl.pallas_call(functools.partial(early_kernel, nsec, nmpo), out_shape=[ke...  2.09 us
    ppermute x3, starting transfers between devices, across(): return lax.ppermute(value, 'mpo', [(i, i ^ m) for i in range(nmpo)])  1.22 us
  transfers between devices with their start and end apart: 6, of which 5 were waited for; matrix products, arithmetic and copies ran while one was open for 1% of the time, Pallas kernels for 10%

profile of v2, /device:TPU:10, one launch (start us, length us, event | category | flops | bytes accessed | tf_op | source)
XLA Modules:
  0.0 35.9 jit_solution(3303068721714592800)
XLA Ops:
  0.0 0.0 copy-start.4
  0.0 0.7 %copy-done.4 = s32[1,32]{1,0:T(1,128)S(1)} copy-done((s32[1,32]{1,0:T(1,128)S(1)}, s32[1,32]{1,0:T(1,128)}, u32[]{:S(2)}) %copy-start.4) | copy-done | bytes 152
  0.7 0.0 copy-start
  0.7 1.1 %copy-done = bf16[8,128,3,128]{3,1,2,0:T(8,128)(2,1)S(1)} copy-done((bf16[8,128,3,128]{3,1,2,0:T(8,128)(2,1)S(1)}, bf16[8,128,3,128]{3,1,2,0:T(8,128)(2,1)}, u32[]{:S(2)}) %copy-start) | copy-done | bytes 786456
  1.8 0.0 copy-start.1
  1.8 2.2 %route.1 = (bf16[2,3,128,128]{3,2,1,0:T(8,128)(2,1)S(1)}, bf16[2,3,128,128]{3,2,1,0:T(8,128)(2,1)S(1)}, bf16[2,3,128,128]{3,2,1,0:T(8,128)(2,1)S(1)}, s32[10]{0:T(128)S(1)}) custom-call(s32[1,32]{1,0:T(1,128)S(1)} %copy-done.4, bf16[8,3,128,128]{3,2,1,0:T(8,128)(2,1)S(1)} %bitcast.2), custom_call_target="tpu_custom_call" | custom-call | tf_op jit(solution)/shard_map/route/pallas_call | solution.py:73
  4.0 0.0 copy-start.5
  4.0 0.5 %collective-permute-start.2 = (bf16[2,3,128,128]{3,2,1,0:T(8,128)(2,1)S(1)}, bf16[2,3,128,128]{3,2,1,0:T(8,128)(2,1)S(1)}, u32[]{:S(2)}, u32[]{:S(2)}) collective-permute-start(bf16[2,3,128,128]{3,2,1,0:T(8,128)(2,1)S(1)} %get-tuple-element.23), channel_id=1, source_target_pairs={{0,4},{4,0},{8,12},{12,8},{1,5},{5,1},{9,13},{13,9},{2,6},{6,2},{1... | collective-permute-start | bytes 589832 | tf_op jit(solution)/shard_map/ppermute | solution.py:264
  4.5 2.6 %collective-permute-start = (bf16[2,3,128,128]{3,2,1,0:T(8,128)(2,1)S(1)}, bf16[2,3,128,128]{3,2,1,0:T(8,128)(2,1)S(1)}, u32[]{:S(2)}, u32[]{:S(2)}) collective-permute-start(bf16[2,3,128,128]{3,2,1,0:T(8,128)(2,1)S(1)} %get-tuple-element.21), channel_id=1, source_target_pairs={{0,8},{4,12},{8,0},{12,4},{1,9},{5,13},{9,1},{13,5},{2,10},{6,14},... | collective-permute-start | bytes 589832 | tf_op jit(solution)/shard_map/ppermute | solution.py:264
  7.1 0.5 %collective-permute-start.1 = (bf16[2,3,128,128]{3,2,1,0:T(8,128)(2,1)S(1)}, bf16[2,3,128,128]{3,2,1,0:T(8,128)(2,1)S(1)}, u32[]{:S(2)}, u32[]{:S(2)}) collective-permute-start(bf16[2,3,128,128]{3,2,1,0:T(8,128)(2,1)S(1)} %get-tuple-element.22), channel_id=1, source_target_pairs={{0,12},{4,8},{8,4},{12,0},{1,13},{5,9},{9,5},{13,1},{2,14},{6,10},... | collective-permute-start | bytes 589832 | tf_op jit(solution)/shard_map/ppermute | solution.py:264
  7.5 0.0 copy-done.5
  7.5 0.1 copy.6
  7.7 0.1 reshape.8.ops
  7.8 4.3 %collective-permute-done.2.near_block = bf16[2,3,128,128]{3,2,1,0:T(8,128)(2,1)S(1)} collective-permute-done((bf16[2,3,128,128]{3,2,1,0:T(8,128)(2,1)S(1)}, bf16[2,3,128,128]{3,2,1,0:T(8,128)(2,1)S(1)}, u32[]{:S(2)}, u32[]{:S(2)}) %collective-permute-start.2) | collective-permute-done | bytes 196640 | tf_op jit(solution)/shard_map/ppermute | solution.py:264
  12.1 0.0 copy-done.1
  12.1 0.0 copy-start.2
  12.1 1.0 %copy-done.2 = bf16[2,8,128,128]{3,2,1,0:T(8,128)(2,1)S(1)} copy-done((bf16[2,8,128,128]{3,2,1,0:T(8,128)(2,1)S(1)}, bf16[2,8,128,128]{3,2,1,0:T(8,128)(2,1)}, u32[]{:S(2)}) %copy-start.2) | copy-done | bytes 524312
  13.2 0.0 copy-start.3
  13.2 1.0 %copy-done.3 = bf16[2,8,128,128]{3,2,1,0:T(8,128)(2,1)S(1)} copy-done((bf16[2,8,128,128]{3,2,1,0:T(8,128)(2,1)S(1)}, bf16[2,8,128,128]{3,2,1,0:T(8,128)(2,1)}, u32[]{:S(2)}) %copy-start.3) | copy-done | bytes 524312
  14.2 2.1 %early.1 = (f32[4,3,32,128]{3,2,1,0:T(8,128)S(1)}, bf16[4,3,32,128]{3,2,1,0:T(8,128)(2,1)S(1)}, f32[4,3,32,128]{3,2,1,0:T(8,128)S(1)}, bf16[4,3,32,128]{3,2,1,0:...) custom-call(s32[10]{0:T(128)S(1)} %get-tuple-element.20.order, ...), custom_call_target="tpu_custom_call" | custom-call | flops 201326592 | bytes 8388608 | tf_op jit(solution)/shard_map/early/pallas_call | solution.py:162
  16.3 4.6 %collective-permute-done.refs_0_ = bf16[2,3,128,128]{3,2,1,0:T(8,128)(2,1)S(1)} collective-permute-done((bf16[2,3,128,128]{3,2,1,0:T(8,128)(2,1)S(1)}, bf16[2,3,128,128]{3,2,1,0:T(8,128)(2,1)S(1)}, u32[]{:S(2)}, u32[]{:S(2)}) %collective-permute-start) | collective-permute-done | bytes 196640 | tf_op jit(solution)/shard_map/ppermute | solution.py:264
  20.8 3.7 %collective-permute-done.1.refs_1_ = bf16[2,3,128,128]{3,2,1,0:T(8,128)(2,1)S(1)} collective-permute-done((bf16[2,3,128,128]{3,2,1,0:T(8,128)(2,1)S(1)}, bf16[2,3,128,128]{3,2,1,0:T(8,128)(2,1)S(1)}, u32[]{:S(2)}, u32[]{:S(2)}) %collective-permute-start.1) | collective-permute-done | bytes 196640 | tf_op jit(solution)/shard_map/ppermute | solution.py:264
  24.6 1.5 %late.3 = (f32[8,3,32,128]{3,2,1,0:T(8,128)S(1)}, bf16[8,3,32,128]{3,2,1,0:T(8,128)(2,1)S(1)}) custom-call(s32[10]{0:T(128)S(1)} %get-tuple-element.20.order, f32[144]{0:T(256)S(1)} %reshape.8.ops, bf16[2,3,128,128]{3,2,1,0:T(8,128)(2,1)S(1)} %collective-permute-done.refs_0_, bf16[2,3,128,128]{3,2,1,0:T(8,128)(2,1)S(1)} %collective-permute-done.1.refs_1_, ...), custom_call_target="tpu_custom_call" | custom-call | flops 100663296 | bytes 4194304 | tf_op jit(solution)/shard_map/late/pallas_call | solution.py:202
  26.1 0.1 collective-permute-start.4
  26.1 1.5 %late.2 = (f32[8,3,32,128]{3,2,1,0:T(8,128)S(1)}, bf16[8,3,32,128]{3,2,1,0:T(8,128)(2,1)S(1)}) custom-call(s32[10]{0:T(128)S(1)} %get-tuple-element.20.order, f32[144]{0:T(256)S(1)} %reshape.8.ops, bf16[2,3,128,128]{3,2,1,0:T(8,128)(2,1)S(1)} %collective-permute-done.refs_0_, bf16[2,3,128,128]{3,2,1,0:T(8,128)(2,1)S(1)} %collective-permute-done.1.refs_1_, ...), custom_call_target="tpu_custom_call" | custom-call | flops 100663296 | bytes 4194304 | tf_op jit(solution)/shard_map/late/pallas_call | solution.py:202
  27.6 0.6 %collective-permute-start.3 = (bf16[8,3,32,128]{3,2,1,0:T(8,128)(2,1)S(1)}, bf16[8,3,32,128]{3,2,1,0:T(8,128)(2,1)S(1)}, u32[]{:S(2)}, u32[]{:S(2)}) collective-permute-start(bf16[8,3,32,128]{3,2,1,0:T(8,128)(2,1)S(1)} %get-tuple-element.29), channel_id=1, source_target_pairs={{0,1},{1,0},{2,3},{3,2},{4,5},{5,4},{6,7},{7,6},{8,9},{9,8},{10,11... | collective-permute-start | bytes 589832 | tf_op jit(solution)/shard_map/ppermute | solution.py:267
  28.2 0.0 collective-permute-done.4.got
  28.2 0.6 %collective-permute-start.5 = (bf16[8,3,32,128]{3,2,1,0:T(8,128)(2,1)S(1)}, bf16[8,3,32,128]{3,2,1,0:T(8,128)(2,1)S(1)}, u32[]{:S(2)}, u32[]{:S(2)}) collective-permute-start(bf16[8,3,32,128]{3,2,1,0:T(8,128)(2,1)S(1)} %pair.1), channel_id=1, source_target_pairs={{0,2},{1,3},{2,0},{3,1},{4,6},{5,7},{6,4},{7,5},{8,10},{9,11},{10,... | collective-permute-start | bytes 589832 | tf_op jit(solution)/shard_map/ppermute | solution.py:267
  28.8 0.4 %collective-permute-done.3.near = bf16[8,3,32,128]{3,2,1,0:T(8,128)(2,1)S(1)} collective-permute-done((bf16[8,3,32,128]{3,2,1,0:T(8,128)(2,1)S(1)}, bf16[8,3,32,128]{3,2,1,0:T(8,128)(2,1)S(1)}, u32[]{:S(2)}, u32[]{:S(2)}) %collective-permute-start.3) | collective-permute-done | bytes 196640 | tf_op jit(solution)/shard_map/ppermute | solution.py:267
  29.3 5.9 %collective-permute-done.5.far = bf16[8,3,32,128]{3,2,1,0:T(8,128)(2,1)S(1)} collective-permute-done((bf16[8,3,32,128]{3,2,1,0:T(8,128)(2,1)S(1)}, bf16[8,3,32,128]{3,2,1,0:T(8,128)(2,1)S(1)}, u32[]{:S(2)}, u32[]{:S(2)}) %collective-permute-start.5) | collective-permute-done | bytes 196640 | tf_op jit(solution)/shard_map/ppermute | solution.py:267
  35.1 0.8 %finish.1 = bf16[32,3,8,128]{3,2,1,0:T(8,128)(2,1)} custom-call(f32[8,3,32,128]{3,2,1,0:T(8,128)S(1)} %get-tuple-element.28.keep, bf16[8,3,32,128]{3,2,1,0:T(8,128)(2,1)S(1)} %collective-permute-done.3.near, bf16[8,3,32,128]{3,2,1,0:T(8,128)(2,1)S(1)} %collective-permute-done.5.far), custom_call_target="tpu_custom_call" | custom-call | tf_op jit(solution)/shard_map/finish/pallas_call | solution.py:243
  (1 shorter events, 0.0 us)
Async XLA Ops:
  0.0 0.7 %copy-start.4 = (s32[1,32]{1,0:T(1,128)S(1)}, s32[1,32]{1,0:T(1,128)}, u32[]{:S(2)}) copy-start(s32[1,32]{1,0:T(1,128)} %source.1) | copy-start | bytes 388
  0.7 1.1 %copy-start = (bf16[8,128,3,128]{3,1,2,0:T(8,128)(2,1)S(1)}, bf16[8,128,3,128]{3,1,2,0:T(8,128)(2,1)}, u32[]{:S(2)}) copy-start(bf16[8,128,3,128]{3,1,2,0:T(8,128)(2,1)} %param.5) | copy-start | bytes 2359300
  1.8 10.3 %copy-start.1 = (bf16[8,128,3,128]{3,1,2,0:T(8,128)(2,1)S(1)}, bf16[8,128,3,128]{3,1,2,0:T(8,128)(2,1)}, u32[]{:S(2)}) copy-start(bf16[8,128,3,128]{3,1,2,0:T(8,128)(2,1)} %param.5) | copy-start | bytes 2359300
  4.0 3.6 %copy-start.5 = (bf16[2,8,3,3]{1,0,3,2:T(2,128)(2,1)S(1)}, bf16[2,8,3,3]{1,0,3,2:T(2,128)(2,1)}, u32[]{:S(2)}) copy-start(bf16[2,8,3,3]{1,0,3,2:T(2,128)(2,1)} %param.8) | copy-start | bytes 868
  4.0 8.1 %collective-permute-start.2 = (bf16[2,3,128,128]{3,2,1,0:T(8,128)(2,1)S(1)}, bf16[2,3,128,128]{3,2,1,0:T(8,128)(2,1)S(1)}, u32[]{:S(2)}, u32[]{:S(2)}) collective-permute-start(bf16[2,3,128,128]{3,2,1,0:T(8,128)(2,1)S(1)} %get-tuple-element.23), channel_id=1, source_target_pairs={{0,4},{4,0},{8,12},{12,8},{1,5},{5,1},{9,13},{13,9},{2,6},{6,2},{1... | collective-permute-start | bytes 589832 | tf_op jit(solution)/shard_map/ppermute | solution.py:264
  4.5 16.4 %collective-permute-start = (bf16[2,3,128,128]{3,2,1,0:T(8,128)(2,1)S(1)}, bf16[2,3,128,128]{3,2,1,0:T(8,128)(2,1)S(1)}, u32[]{:S(2)}, u32[]{:S(2)}) collective-permute-start(bf16[2,3,128,128]{3,2,1,0:T(8,128)(2,1)S(1)} %get-tuple-element.21), channel_id=1, source_target_pairs={{0,8},{4,12},{8,0},{12,4},{1,9},{5,13},{9,1},{13,5},{2,10},{6,14},... | collective-permute-start | bytes 589832 | tf_op jit(solution)/shard_map/ppermute | solution.py:264
  7.1 17.5 %collective-permute-start.1 = (bf16[2,3,128,128]{3,2,1,0:T(8,128)(2,1)S(1)}, bf16[2,3,128,128]{3,2,1,0:T(8,128)(2,1)S(1)}, u32[]{:S(2)}, u32[]{:S(2)}) collective-permute-start(bf16[2,3,128,128]{3,2,1,0:T(8,128)(2,1)S(1)} %get-tuple-element.22), channel_id=1, source_target_pairs={{0,12},{4,8},{8,4},{12,0},{1,13},{5,9},{9,5},{13,1},{2,14},{6,10},... | collective-permute-start | bytes 589832 | tf_op jit(solution)/shard_map/ppermute | solution.py:264
  12.1 1.0 %copy-start.2 = (bf16[2,8,128,128]{3,2,1,0:T(8,128)(2,1)S(1)}, bf16[2,8,128,128]{3,2,1,0:T(8,128)(2,1)}, u32[]{:S(2)}) copy-start(bf16[2,8,128,128]{3,2,1,0:T(8,128)(2,1)} %left.1) | copy-start | bytes 1572868
  13.2 1.0 %copy-start.3 = (bf16[2,8,128,128]{3,2,1,0:T(8,128)(2,1)S(1)}, bf16[2,8,128,128]{3,2,1,0:T(8,128)(2,1)}, u32[]{:S(2)}) copy-start(bf16[2,8,128,128]{3,2,1,0:T(8,128)(2,1)} %right.1) | copy-start | bytes 1572868
  26.1 2.1 %collective-permute-start.4 = (bf16[8,3,32,128]{3,2,1,0:T(8,128)(2,1)S(1)}, bf16[8,3,32,128]{3,2,1,0:T(8,128)(2,1)S(1)}, u32[]{:S(2)}, u32[]{:S(2)}) collective-permute-start(bf16[8,3,32,128]{3,2,1,0:T(8,128)(2,1)S(1)} %get-tuple-element.34), channel_id=1, source_target_pairs={{0,1},{1,0},{2,3},{3,2},{4,5},{5,4},{6,7},{7,6},{8,9},{9,8},{10,11... | collective-permute-start | bytes 589832 | tf_op jit(solution)/shard_map/ppermute | solution.py:267
  27.6 1.6 %collective-permute-start.3 = (bf16[8,3,32,128]{3,2,1,0:T(8,128)(2,1)S(1)}, bf16[8,3,32,128]{3,2,1,0:T(8,128)(2,1)S(1)}, u32[]{:S(2)}, u32[]{:S(2)}) collective-permute-start(bf16[8,3,32,128]{3,2,1,0:T(8,128)(2,1)S(1)} %get-tuple-element.29), channel_id=1, source_target_pairs={{0,1},{1,0},{2,3},{3,2},{4,5},{5,4},{6,7},{7,6},{8,9},{9,8},{10,11... | collective-permute-start | bytes 589832 | tf_op jit(solution)/shard_map/ppermute | solution.py:267
  28.2 6.9 %collective-permute-start.5 = (bf16[8,3,32,128]{3,2,1,0:T(8,128)(2,1)S(1)}, bf16[8,3,32,128]{3,2,1,0:T(8,128)(2,1)S(1)}, u32[]{:S(2)}, u32[]{:S(2)}) collective-permute-start(bf16[8,3,32,128]{3,2,1,0:T(8,128)(2,1)S(1)} %pair.1), channel_id=1, source_target_pairs={{0,2},{1,3},{2,0},{3,1},{4,6},{5,7},{6,4},{7,5},{8,10},{9,11},{10,... | collective-permute-start | bytes 589832 | tf_op jit(solution)/shard_map/ppermute | solution.py:267

commit v3 on v2

--- a/solution.py
+++ b/solution.py
@@ -42,55 +42,72 @@
     return places, rows
 
 
-def route_kernel(nsec, sdev, source, psi, *refs):
-    outs, order, table, load, sems = refs[: nsec - 1], *refs[nsec - 1 :]
+def route_kernel(classes, sdev, source, psi, *refs):
+    outs, (table, load, sems) = refs[: len(classes)], refs[len(classes) :]
     me = lax.axis_index("sec")
     fetch = pltpu.make_async_copy(source, table, load)
     fetch.start()
     fetch.wait()
     copies = []
-    for k in range(1, nsec):
+    for i, k in enumerate(classes):
         other = jnp.bitwise_xor(me, k)
         rows = pick(table, other * sdev, sdev, me)[1]
         for j in range(SLOTS):
-            copy = pltpu.make_async_copy(psi.at[rows[j]], outs[k - 1].at[j], sems.at[k - 1, j])
+            copy = pltpu.make_async_copy(psi.at[rows[j]], outs[i].at[j], sems.at[i, j])
             copy.start()
             copies.append(copy)
+    for copy in copies:
+        copy.wait()
+
+
+def route(classes, source, psi):
+    block = psi.shape[1:]
+    return pl.pallas_call(
+        functools.partial(route_kernel, classes, psi.shape[0]),
+        out_shape=[jax.ShapeDtypeStruct((SLOTS,) + block, psi.dtype)] * len(classes),
+        in_specs=[space(pl.ANY)] * 2,
+        out_specs=[space(pl.ANY)] * len(classes),
+        scratch_shapes=[
+            pltpu.SMEM(source.shape, jnp.int32),
+            pltpu.SemaphoreType.DMA,
+            pltpu.SemaphoreType.DMA((len(classes), SLOTS)),
+        ],
+        compiler_params=params(),
+        name="route",
+    )(source, psi)
+
+
+def order_kernel(nsec, sdev, source, after, order, table, load):
+    me = lax.axis_index("sec")
+    fetch = pltpu.make_async_copy(source, table, load)
+    fetch.start()
+    fetch.wait()
     for k in range(nsec):
         places, rows = pick(table, me * sdev, sdev, jnp.bitwise_xor(me, k))
         for j in range(SLOTS):
             order[k * SLOTS + j] = places[j]
             if k == 0:
                 order[nsec * SLOTS + j] = rows[j]
-    for copy in copies:
-        copy.wait()
-
-
-def route(source, psi, nsec, sdev):
-    block = psi.shape[1:]
-    shapes = [jax.ShapeDtypeStruct((SLOTS,) + block, psi.dtype)] * (nsec - 1)
-    shapes.append(jax.ShapeDtypeStruct((nsec * SLOTS + SLOTS,), jnp.int32))
-    return pl.pallas_call(
-        functools.partial(route_kernel, nsec, sdev),
-        out_shape=shapes,
-        in_specs=[space(pltpu.HBM), space(pltpu.HBM)],
-        out_specs=[space(pl.ANY)] * (nsec - 1) + [space(pltpu.SMEM)],
-        scratch_shapes=[
-            pltpu.SMEM(source.shape, jnp.int32),
-            pltpu.SemaphoreType.DMA,
-            pltpu.SemaphoreType.DMA((nsec - 1, SLOTS)),
-        ],
-        compiler_params=params(),
-        name="route",
-    )(source, psi)
+
+
+def receive_order(source, after, nsec, sdev):
+    return pl.pallas_call(
+        functools.partial(order_kernel, nsec, sdev),
+        out_shape=jax.ShapeDtypeStruct((nsec * SLOTS + SLOTS,), jnp.int32),
+        in_specs=[space(pl.ANY)] * 2,
+        out_specs=space(pltpu.SMEM),
+        scratch_shapes=[pltpu.SMEM(source.shape, jnp.int32), pltpu.SemaphoreType.DMA],
+        compiler_params=params(),
+        name="order",
+    )(source, after)
 
 
 def product(lhs, block, rhs, ops, base, wdev, phys):
     rows = lhs.shape[0] // wdev
-    lefts = []
-    for p in range(phys):
-        done = jnp.dot(lhs, block[p], preferred_element_type=jnp.float32)
-        lefts.append(done.astype(jnp.bfloat16).astype(jnp.float32))
+    blk = block[0].shape[1]
+    wide = jnp.dot(lhs, jnp.concatenate(block, axis=1), preferred_element_type=jnp.float32)
+    wide = wide.astype(jnp.bfloat16).astype(jnp.float32)
+    lefts = [wide[:, p * blk : (p + 1) * blk] for p in range(phys)]
     outs = []
     for q in range(phys):
         across = []
@@ -109,8 +126,11 @@
     return [(w * sdev + t) * (phys * phys) for w in range(wdev)]
 
 
+QUARTERS = (2, 0, 3, 1)
+
+
 def early_kernel(nsec, nmpo, order, ops, psi, near_block, left, right, *refs):
-    far_keep, far_give, near_keep, near_give, lfar, lnear, rstage, local, sems = refs
+    keep, far_give, near_give, lstage, rstage, local, sems = refs
     wdev, sdev, blk = left.shape[:3]
     phys = local.shape[1]
     part = blk // nmpo
@@ -121,14 +141,17 @@
         copy.start()
         copies.append(copy)
 
-    def rows(w, t, m):
-        start = pl.multiple_of(jnp.bitwise_xor(me, m) * part, part)
-        return left[w, t, pl.ds(start, part), :]
+    def side(t):
+        rows = []
+        for w in range(wdev):
+            for m in QUARTERS:
+                start = pl.multiple_of(jnp.bitwise_xor(me, m) * part, part)
+                rows.append(left[w, t, pl.ds(start, part), :])
+        return jnp.concatenate(rows, axis=0)
 
     for s in range((nsec - EARLY) * SLOTS):
         t = order[EARLY * SLOTS + s]
-        lfar[s] = jnp.concatenate([rows(w, t, m) for w in range(wdev) for m in (2, 3)], axis=0)
-        lnear[s] = jnp.concatenate([rows(w, t, m) for w in range(wdev) for m in (0, 1)], axis=0)
+        lstage[s] = side(t)
         rstage[s] = right[:, t].reshape(wdev * blk, blk)
     for copy in copies:
         copy.wait()
@@ -136,17 +159,14 @@
         for j in range(SLOTS):
             s = k * SLOTS + j
             t = order[s]
-            lhs = jnp.concatenate(
-                [rows(w, t, m) for w in range(wdev) for m in (2, 3, 0, 1)], axis=0
-            )
             rhs = right[:, t].reshape(wdev * blk, blk)
             source = near_block if k == 1 else local
             block = [source[j, p] for p in range(phys)]
-            outs = product(lhs, block, rhs, ops, op_base(t, wdev, sdev, phys), wdev, phys)
+            outs = product(side(t), block, rhs, ops, op_base(t, wdev, sdev, phys), wdev, phys)
             for q in range(phys):
-                far_keep[s, q] = outs[q][:part]
-                far_give[s, q] = outs[q][part : 2 * part].astype(jnp.bfloat16)
-                near_keep[s, q] = outs[q][2 * part : 3 * part]
+                keep[0, s, q] = outs[q][:part]
+                keep[1, s, q] = outs[q][part : 2 * part]
+                far_give[s, q] = outs[q][2 * part : 3 * part].astype(jnp.bfloat16)
                 near_give[s, q] = outs[q][3 * part :].astype(jnp.bfloat16)
 
 
@@ -155,15 +175,14 @@
     phys = psi.shape[1]
     part = blk // nmpo
     n, late_n = EARLY * SLOTS, (nsec - EARLY) * SLOTS
-    keep = jax.ShapeDtypeStruct((n, phys, part, blk), jnp.float32)
+    keep = jax.ShapeDtypeStruct((2, n, phys, part, blk), jnp.float32)
     give = jax.ShapeDtypeStruct((n, phys, part, blk), jnp.bfloat16)
-    half = jax.ShapeDtypeStruct((late_n, wdev * 2 * part, blk), jnp.bfloat16)
     whole = jax.ShapeDtypeStruct((late_n, wdev * blk, blk), jnp.bfloat16)
     return pl.pallas_call(
         functools.partial(early_kernel, nsec, nmpo),
-        out_shape=[keep, give, keep, give, half, half, whole],
-        in_specs=[space(pltpu.SMEM)] * 2 + [space(pltpu.HBM)] + [space(pltpu.VMEM)] * 3,
-        out_specs=[space(pltpu.VMEM)] * 7,
+        out_shape=[keep, give, give, whole, whole],
+        in_specs=[space(pltpu.SMEM)] * 2 + [space(pl.ANY)] + [space(pltpu.VMEM)] * 3,
+        out_specs=[space(pltpu.VMEM)] * 5,
         scratch_shapes=[
             pltpu.VMEM((SLOTS, phys, blk, blk), jnp.bfloat16),
             pltpu.SemaphoreType.DMA((SLOTS,)),
@@ -180,45 +199,48 @@
 
 def late_kernel(nsec, wdev, sdev, order, ops, *refs):
     nlate = nsec - EARLY
-    blocks, (lside, rstage, early_keep, early_give, keep, give) = refs[:nlate], refs[nlate:]
-    phys, part = keep.shape[1], keep.shape[2]
+    blocks, refs = refs[:nlate], refs[nlate:]
+    lstage, rstage, early_keep, early_far, early_near, keep, far_give, near_give = refs
+    phys, part = far_give.shape[1], far_give.shape[2]
     for s in range(EARLY * SLOTS):
         t = order[s]
-        keep[t] = early_keep[s]
-        give[t] = early_give[s]
+        for side in range(2):
+            keep[side, t] = early_keep[side, s]
+        far_give[t] = early_far[s]
+        near_give[t] = early_near[s]
     for s in range(nlate * SLOTS):
         t = order[EARLY * SLOTS + s]
         block = [blocks[s // SLOTS][s % SLOTS, p] for p in range(phys)]
         base = op_base(t, wdev, sdev, phys)
-        outs = product(lside[s], block, rstage[s], ops, base, wdev, phys)
+        outs = product(lstage[s], block, rstage[s], ops, base, wdev, phys)
         for q in range(phys):
-            keep[t, q] = outs[q][:part]
-            give[t, q] = outs[q][part:].astype(jnp.bfloat16)
-
-
-def late(order, ops, blocks, lside, rstage, early_keep, early_give, nsec, wdev, sdev):
-    phys, part, blk = early_keep.shape[1:]
+            keep[0, t, q] = outs[q][:part]
+            keep[1, t, q] = outs[q][part : 2 * part]
+            far_give[t, q] = outs[q][2 * part : 3 * part].astype(jnp.bfloat16)
+            near_give[t, q] = outs[q][3 * part :].astype(jnp.bfloat16)
+
+
+def late(order, ops, blocks, staged, nsec, wdev, sdev):
+    phys, part, blk = staged[0].shape[2:]
     n = len(blocks) * SLOTS
+    give = jax.ShapeDtypeStruct((sdev, phys, part, blk), jnp.bfloat16)
     return pl.pallas_call(
         functools.partial(late_kernel, nsec, wdev, sdev),
-        out_shape=[
-            jax.ShapeDtypeStruct((sdev, phys, part, blk), jnp.float32),
-            jax.ShapeDtypeStruct((sdev, phys, part, blk), jnp.bfloat16),
-        ],
-        in_specs=[space(pltpu.SMEM)] * 2 + [space(pltpu.VMEM)] * (len(blocks) + 4),
-        out_specs=[space(pltpu.VMEM)] * 2,
+        out_shape=[jax.ShapeDtypeStruct((2, sdev, phys, part, blk), jnp.float32), give, give],
+        in_specs=[space(pltpu.SMEM)] * 2 + [space(pltpu.VMEM)] * (len(blocks) + 5),
+        out_specs=[space(pltpu.VMEM)] * 3,
         compiler_params=params(),
         cost_estimate=pl.CostEstimate(
-            flops=n * wdev * phys * blk**3 * 2,
-            bytes_accessed=4 * 1024 * 1024,
+            flops=n * wdev * phys * blk**3 * 4,
+            bytes_accessed=8 * 1024 * 1024,
             transcendentals=0,
         ),
         name="late",
-    )(order, ops, *blocks, lside, rstage, early_keep, early_give)
+    )(order, ops, *blocks, *staged[3:], *staged[:3])
 
 
 def pair_kernel(keep, got, out):
-    out[...] = (keep[...] + got[...].astype(jnp.float32)).astype(out.dtype)
+    out[...] = (keep[0] + got[...].astype(jnp.float32)).astype(out.dtype)
 
 
 def pair(keep, got):
@@ -234,12 +256,12 @@
 
 def finish_kernel(keep, near, far, out):
     for q in range(out.shape[1]):
-        total = keep[:, q] + near[:, q].astype(jnp.float32) + far[:, q].astype(jnp.float32)
+        total = keep[1, :, q] + near[:, q].astype(jnp.float32) + far[:, q].astype(jnp.float32)
         out[:, q] = jnp.swapaxes(total, 0, 1).astype(out.dtype)
 
 
 def finish(keep, near, far):
-    sdev, phys, part, blk = keep.shape
+    sdev, phys, part, blk = far.shape
     return pl.pallas_call(
         finish_kernel,
         out_shape=jax.ShapeDtypeStruct((part, phys, sdev, blk), jnp.bfloat16),
@@ -257,8 +279,11 @@
     wdev = left_env.shape[0]
     blocks = jnp.transpose(psi, (0, 2, 1, 3))
     ops = site_op.astype(jnp.float32).reshape(-1)
-    routed = route(source, blocks, nsec, sdev)
-    outgoing, order = routed[:-1], routed[-1]
+    table = pltpu.with_memory_space_constraint(source, pltpu.HBM)
+    outgoing = route(
+        tuple(range(1, nsec)), table, pltpu.with_memory_space_constraint(blocks, pltpu.HBM)
+    )
+    order = receive_order(table, outgoing[0], nsec, sdev)
     arrived = []
     for k in range(1, nsec):
         arrived.append(lax.ppermute(outgoing[k - 1], "sec", [(i, i ^ k) for i in range(nsec)]))
@@ -266,16 +291,10 @@
     def across(value, m):
         return lax.ppermute(value, "mpo", [(i, i ^ m) for i in range(nmpo)])
 
-    far_keep, far_give, near_keep, near_give, lfar, lnear, rstage = early(
-        order, ops, blocks, arrived[0], left_env, right_env, nsec, nmpo
-    )
-    rest = arrived[1:]
-    keep_far, give_far = late(order, ops, rest, lfar, rstage, far_keep, far_give, nsec, wdev, sdev)
-    over = across(pair(keep_far, across(give_far, 1)), 2)
-    keep_near, give_near = late(
-        order, ops, rest, lnear, rstage, near_keep, near_give, nsec, wdev, sdev
-    )
-    out = finish(keep_near, across(give_near, 1), over)
+    staged = early(order, ops, blocks, arrived[0], left_env, right_env, nsec, nmpo)
+    keep, far_give, near_give = late(order, ops, arrived[1:], staged, nsec, wdev, sdev)
+    over = across(pair(keep, across(far_give, 1)), 2)
+    out = finish(keep, across(near_give, 1), over)
     return jnp.transpose(out, (0, 2, 1, 3))
 
 

time: 36.2 us -> 34 us (0.939)
  local copies, waits for them, and re-layouts: 4.13 us -> 2.34 us
    unnamed x12 -> x8, local copies, waits for them, and re-layouts: 3.88 us -> 2.09 us
    ppermute x3, waiting for transfers between devices: 12.6 us -> 11.3 us  [fast_shards(): lax.ppermute(outgoing[k - 1], 'sec', [(i, i ^ k) for i in range(nsec)])]
    pallas_call x2 -> x1, Pallas kernels: 2.99 us -> 1.68 us  [late(): pl.pallas_call(functools.partial(late_kernel, nsec, wdev, sdev), out_shap...]
    pallas_call x1 -> x2, Pallas kernels: 2.16 us -> 3.39 us  [the longest x1 2.03 us: route(): pl.pallas_call(functools.partial(route_kernel, classes, psi.shape[0]), ou...]
    ppermute x3, waiting for transfers between devices: 6.3 us -> 7.34 us  [across(): return lax.ppermute(value, 'mpo', [(i, i ^ m) for i in range(nmpo)])]
where the time goes in v3:
time: 34 us; the launch traced here: 33.7 us
  waiting for transfers between devices  18.6 us (55%)
  Pallas kernels  7.98 us (23%)
  starting transfers between devices  4.72 us (14%)
  local copies, waits for them, and re-layouts  2.34 us (7%)
    ppermute x3, waiting for transfers between devices, fast_shards(): lax.ppermute(outgoing[k - 1], 'sec', [(i, i ^ k) for i in range(nsec)])  11.3 us
    ppermute x3, waiting for transfers between devices, across(): return lax.ppermute(value, 'mpo', [(i, i ^ m) for i in range(nmpo)])  7.34 us
    ppermute x3, starting transfers between devices, fast_shards(): lax.ppermute(outgoing[k - 1], 'sec', [(i, i ^ k) for i in range(nsec)])  3.55 us
    unnamed x8, local copies, waits for them, and re-layouts  2.09 us
    pallas_call x1, Pallas kernels, early(): pl.pallas_call(functools.partial(early_kernel, nsec, nmpo), out_shape=[ke...  2.04 us
    pallas_call x1, Pallas kernels, route(): pl.pallas_call(functools.partial(route_kernel, classes, psi.shape[0]), ou...  2.03 us
    pallas_call x1, Pallas kernels, late(): pl.pallas_call(functools.partial(late_kernel, nsec, wdev, sdev), out_shap...  1.68 us
    pallas_call x1, Pallas kernels, receive_order(): pl.pallas_call(functools.partial(order_kernel, nsec, sdev), out_shape=jax...  1.37 us
  transfers between devices with their start and end apart: 6, of which 5 were waited for; matrix products, arithmetic and copies ran while one was open for 1% of the time, Pallas kernels for 10%

profile of v3, /device:TPU:10, one launch (start us, length us, event | category | flops | bytes accessed | tf_op | source)
XLA Modules:
  0.0 33.7 jit_solution(1400675370546430155)
XLA Ops:
  0.0 0.0 copy-start
  0.0 2.0 %route.1 = (bf16[2,3,128,128]{3,2,1,0:T(8,128)(2,1)S(1)}, bf16[2,3,128,128]{3,2,1,0:T(8,128)(2,1)S(1)}, bf16[2,3,128,128]{3,2,1,0:T(8,128)(2,1)S(1)}) custom-call(s32[1,32]{1,0:T(1,128)} %source.3, bf16[8,3,128,128]{3,2,1,0:T(8,128)(2,1)} %bitcast.2), custom_call_target="tpu_custom_call" | custom-call | tf_op jit(solution)/shard_map/route/pallas_call | solution.py:65
  2.0 0.5 %collective-permute-start.2 = (bf16[2,3,128,128]{3,2,1,0:T(8,128)(2,1)S(1)}, bf16[2,3,128,128]{3,2,1,0:T(8,128)(2,1)S(1)}, u32[]{:S(2)}, u32[]{:S(2)}) collective-permute-start(bf16[2,3,128,128]{3,2,1,0:T(8,128)(2,1)S(1)} %get-tuple-element.16.after), channel_id=1, source_target_pairs={{0,4},{4,0},{8,12},{12,8},{1,5},{5,1},{9,13},{13,9},{2,6},{6,2},{1... | collective-permute-start | bytes 589832 | tf_op jit(solution)/shard_map/ppermute | solution.py:289
  2.6 2.6 %collective-permute-start = (bf16[2,3,128,128]{3,2,1,0:T(8,128)(2,1)S(1)}, bf16[2,3,128,128]{3,2,1,0:T(8,128)(2,1)S(1)}, u32[]{:S(2)}, u32[]{:S(2)}) collective-permute-start(bf16[2,3,128,128]{3,2,1,0:T(8,128)(2,1)S(1)} %get-tuple-element.17), channel_id=1, source_target_pairs={{0,8},{4,12},{8,0},{12,4},{1,9},{5,13},{9,1},{13,5},{2,10},{6,14},... | collective-permute-start | bytes 589832 | tf_op jit(solution)/shard_map/ppermute | solution.py:289
  5.1 0.0 copy-start.3
  5.1 0.5 %collective-permute-start.1 = (bf16[2,3,128,128]{3,2,1,0:T(8,128)(2,1)S(1)}, bf16[2,3,128,128]{3,2,1,0:T(8,128)(2,1)S(1)}, u32[]{:S(2)}, u32[]{:S(2)}) collective-permute-start(bf16[2,3,128,128]{3,2,1,0:T(8,128)(2,1)S(1)} %get-tuple-element.18), channel_id=1, source_target_pairs={{0,12},{4,8},{8,4},{12,0},{1,13},{5,9},{9,5},{13,1},{2,14},{6,10},... | collective-permute-start | bytes 589832 | tf_op jit(solution)/shard_map/ppermute | solution.py:289
  5.6 1.4 %order.1 = s32[10]{0:T(128)S(1)} custom-call(s32[1,32]{1,0:T(1,128)} %source.3, bf16[2,3,128,128]{3,2,1,0:T(8,128)(2,1)S(1)} %get-tuple-element.16.after), custom_call_target="tpu_custom_call" | custom-call | tf_op jit(solution)/shard_map/order/pallas_call | solution.py:94
  7.0 0.0 copy-done.3
  7.0 0.1 copy.6
  7.1 0.1 reshape.8.ops
  7.2 2.9 %collective-permute-done.2.near_block = bf16[2,3,128,128]{3,2,1,0:T(8,128)(2,1)S(1)} collective-permute-done((bf16[2,3,128,128]{3,2,1,0:T(8,128)(2,1)S(1)}, bf16[2,3,128,128]{3,2,1,0:T(8,128)(2,1)S(1)}, u32[]{:S(2)}, u32[]{:S(2)}) %collective-permute-start.2) | collective-permute-done | bytes 196640 | tf_op jit(solution)/shard_map/ppermute | solution.py:289
  10.2 0.0 copy-done
  10.2 0.0 copy-start.1
  10.2 1.0 %copy-done.1 = bf16[2,8,128,128]{3,2,1,0:T(8,128)(2,1)S(1)} copy-done((bf16[2,8,128,128]{3,2,1,0:T(8,128)(2,1)S(1)}, bf16[2,8,128,128]{3,2,1,0:T(8,128)(2,1)}, u32[]{:S(2)}) %copy-start.1) | copy-done | bytes 524312
  11.2 0.0 copy-start.2
  11.2 1.0 %copy-done.2 = bf16[2,8,128,128]{3,2,1,0:T(8,128)(2,1)S(1)} copy-done((bf16[2,8,128,128]{3,2,1,0:T(8,128)(2,1)S(1)}, bf16[2,8,128,128]{3,2,1,0:T(8,128)(2,1)}, u32[]{:S(2)}) %copy-start.2) | copy-done | bytes 524312
  12.3 2.0 %early.1 = (f32[2,4,3,32,128]{4,3,2,1,0:T(8,128)S(1)}, bf16[4,3,32,128]{3,2,1,0:T(8,128)(2,1)S(1)}, bf16[4,3,32,128]{3,2,1,0:T(8,128)(2,1)S(1)}, bf16[4,256,128]...) custom-call(s32[10]{0:T(128)S(1)} %order.1, f32[144]{0:T(256)S(1)} %reshape.8.ops, bf16[8,3,128,128]{3,2,1,0:T(8,128)(2,1)S(1)} %bitcast.3, ...), custom_call_target="tpu_custom_call" | custom-call | flops 201326592 | bytes 8388608 | tf_op jit(solution)/shard_map/early/pallas_call | solution.py:181
  14.3 4.6 %collective-permute-done.refs_0_ = bf16[2,3,128,128]{3,2,1,0:T(8,128)(2,1)S(1)} collective-permute-done((bf16[2,3,128,128]{3,2,1,0:T(8,128)(2,1)S(1)}, bf16[2,3,128,128]{3,2,1,0:T(8,128)(2,1)S(1)}, u32[]{:S(2)}, u32[]{:S(2)}) %collective-permute-start) | collective-permute-done | bytes 196640 | tf_op jit(solution)/shard_map/ppermute | solution.py:289
  18.9 3.7 %collective-permute-done.1.refs_1_ = bf16[2,3,128,128]{3,2,1,0:T(8,128)(2,1)S(1)} collective-permute-done((bf16[2,3,128,128]{3,2,1,0:T(8,128)(2,1)S(1)}, bf16[2,3,128,128]{3,2,1,0:T(8,128)(2,1)S(1)}, u32[]{:S(2)}, u32[]{:S(2)}) %collective-permute-start.1) | collective-permute-done | bytes 196640 | tf_op jit(solution)/shard_map/ppermute | solution.py:289
  22.6 1.7 %late.1 = (f32[2,8,3,32,128]{4,3,2,1,0:T(8,128)S(1)}, bf16[8,3,32,128]{3,2,1,0:T(8,128)(2,1)S(1)}, bf16[8,3,32,128]{3,2,1,0:T(8,128)(2,1)S(1)}) custom-call(s32[10]{0:T(128)S(1)} %order.1, f32[144]{0:T(256)S(1)} %reshape.8.ops, bf16[2,3,128,128]{3,2,1,0:T(8,128)(2,1)S(1)} %collective-permute-done.refs_0_, ...), custom_call_target="tpu_custom_call" | custom-call | flops 201326592 | bytes 8388608 | tf_op jit(solution)/shard_map/late/pallas_call | solution.py:227
  24.3 0.1 collective-permute-start.4
  24.4 0.5 %collective-permute-start.3 = (bf16[8,3,32,128]{3,2,1,0:T(8,128)(2,1)S(1)}, bf16[8,3,32,128]{3,2,1,0:T(8,128)(2,1)S(1)}, u32[]{:S(2)}, u32[]{:S(2)}) collective-permute-start(bf16[8,3,32,128]{3,2,1,0:T(8,128)(2,1)S(1)} %get-tuple-element.25), channel_id=1, source_target_pairs={{0,1},{1,0},{2,3},{3,2},{4,5},{5,4},{6,7},{7,6},{8,9},{9,8},{10,11... | collective-permute-start | bytes 589832 | tf_op jit(solution)/shard_map/ppermute | solution.py:292
  24.9 0.9 %collective-permute-done.4.got = bf16[8,3,32,128]{3,2,1,0:T(8,128)(2,1)S(1)} collective-permute-done((bf16[8,3,32,128]{3,2,1,0:T(8,128)(2,1)S(1)}, bf16[8,3,32,128]{3,2,1,0:T(8,128)(2,1)S(1)}, u32[]{:S(2)}, u32[]{:S(2)}) %collective-permute-start.4) | collective-permute-done | bytes 196640 | tf_op jit(solution)/shard_map/ppermute | solution.py:292
  25.9 0.6 %collective-permute-start.5 = (bf16[8,3,32,128]{3,2,1,0:T(8,128)(2,1)S(1)}, bf16[8,3,32,128]{3,2,1,0:T(8,128)(2,1)S(1)}, u32[]{:S(2)}, u32[]{:S(2)}) collective-permute-start(bf16[8,3,32,128]{3,2,1,0:T(8,128)(2,1)S(1)} %pair.1), channel_id=1, source_target_pairs={{0,2},{1,3},{2,0},{3,1},{4,6},{5,7},{6,4},{7,5},{8,10},{9,11},{10,... | collective-permute-start | bytes 589832 | tf_op jit(solution)/shard_map/ppermute | solution.py:292
  26.5 0.0 collective-permute-done.3.near
  26.5 6.4 %collective-permute-done.5.far = bf16[8,3,32,128]{3,2,1,0:T(8,128)(2,1)S(1)} collective-permute-done((bf16[8,3,32,128]{3,2,1,0:T(8,128)(2,1)S(1)}, bf16[8,3,32,128]{3,2,1,0:T(8,128)(2,1)S(1)}, u32[]{:S(2)}, u32[]{:S(2)}) %collective-permute-start.5) | collective-permute-done | bytes 196640 | tf_op jit(solution)/shard_map/ppermute | solution.py:292
  32.9 0.8 %finish.1 = bf16[32,3,8,128]{3,2,1,0:T(8,128)(2,1)} custom-call(f32[2,8,3,32,128]{4,3,2,1,0:T(8,128)S(1)} %get-tuple-element.24.keep, bf16[8,3,32,128]{3,2,1,0:T(8,128)(2,1)S(1)} %collective-permute-done.3.near, bf16[8,3,32,128]{3,2,1,0:T(8,128)(2,1)S(1)} %collective-permute-done.5.far), custom_call_target="tpu_custom_call" | custom-call | tf_op jit(solution)/shard_map/finish/pallas_call | solution.py:265
  (1 shorter events, 0.0 us)
Async XLA Ops:
  0.0 10.2 %copy-start = (bf16[8,128,3,128]{3,1,2,0:T(8,128)(2,1)S(1)}, bf16[8,128,3,128]{3,1,2,0:T(8,128)(2,1)}, u32[]{:S(2)}) copy-start(bf16[8,128,3,128]{3,1,2,0:T(8,128)(2,1)} %param.5) | copy-start | bytes 2359300
  2.0 8.1 %collective-permute-start.2 = (bf16[2,3,128,128]{3,2,1,0:T(8,128)(2,1)S(1)}, bf16[2,3,128,128]{3,2,1,0:T(8,128)(2,1)S(1)}, u32[]{:S(2)}, u32[]{:S(2)}) collective-permute-start(bf16[2,3,128,128]{3,2,1,0:T(8,128)(2,1)S(1)} %get-tuple-element.16.after), channel_id=1, source_target_pairs={{0,4},{4,0},{8,12},{12,8},{1,5},{5,1},{9,13},{13,9},{2,6},{6,2},{1... | collective-permute-start | bytes 589832 | tf_op jit(solution)/shard_map/ppermute | solution.py:289
  2.6 16.4 %collective-permute-start = (bf16[2,3,128,128]{3,2,1,0:T(8,128)(2,1)S(1)}, bf16[2,3,128,128]{3,2,1,0:T(8,128)(2,1)S(1)}, u32[]{:S(2)}, u32[]{:S(2)}) collective-permute-start(bf16[2,3,128,128]{3,2,1,0:T(8,128)(2,1)S(1)} %get-tuple-element.17), channel_id=1, source_target_pairs={{0,8},{4,12},{8,0},{12,4},{1,9},{5,13},{9,1},{13,5},{2,10},{6,14},... | collective-permute-start | bytes 589832 | tf_op jit(solution)/shard_map/ppermute | solution.py:289
  5.1 1.8 %copy-start.3 = (bf16[2,8,3,3]{1,0,3,2:T(2,128)(2,1)S(1)}, bf16[2,8,3,3]{1,0,3,2:T(2,128)(2,1)}, u32[]{:S(2)}) copy-start(bf16[2,8,3,3]{1,0,3,2:T(2,128)(2,1)} %param.8) | copy-start | bytes 868
  5.1 17.5 %collective-permute-start.1 = (bf16[2,3,128,128]{3,2,1,0:T(8,128)(2,1)S(1)}, bf16[2,3,128,128]{3,2,1,0:T(8,128)(2,1)S(1)}, u32[]{:S(2)}, u32[]{:S(2)}) collective-permute-start(bf16[2,3,128,128]{3,2,1,0:T(8,128)(2,1)S(1)} %get-tuple-element.18), channel_id=1, source_target_pairs={{0,12},{4,8},{8,4},{12,0},{1,13},{5,9},{9,5},{13,1},{2,14},{6,10},... | collective-permute-start | bytes 589832 | tf_op jit(solution)/shard_map/ppermute | solution.py:289
  10.2 1.0 %copy-start.1 = (bf16[2,8,128,128]{3,2,1,0:T(8,128)(2,1)S(1)}, bf16[2,8,128,128]{3,2,1,0:T(8,128)(2,1)}, u32[]{:S(2)}) copy-start(bf16[2,8,128,128]{3,2,1,0:T(8,128)(2,1)} %left.1) | copy-start | bytes 1572868
  11.2 1.0 %copy-start.2 = (bf16[2,8,128,128]{3,2,1,0:T(8,128)(2,1)S(1)}, bf16[2,8,128,128]{3,2,1,0:T(8,128)(2,1)}, u32[]{:S(2)}) copy-start(bf16[2,8,128,128]{3,2,1,0:T(8,128)(2,1)} %right.1) | copy-start | bytes 1572868
  24.3 1.5 %collective-permute-start.4 = (bf16[8,3,32,128]{3,2,1,0:T(8,128)(2,1)S(1)}, bf16[8,3,32,128]{3,2,1,0:T(8,128)(2,1)S(1)}, u32[]{:S(2)}, u32[]{:S(2)}) collective-permute-start(bf16[8,3,32,128]{3,2,1,0:T(8,128)(2,1)S(1)} %get-tuple-element.26), channel_id=1, source_target_pairs={{0,1},{1,0},{2,3},{3,2},{4,5},{5,4},{6,7},{7,6},{8,9},{9,8},{10,11... | collective-permute-start | bytes 589832 | tf_op jit(solution)/shard_map/ppermute | solution.py:292
  24.4 2.1 %collective-permute-start.3 = (bf16[8,3,32,128]{3,2,1,0:T(8,128)(2,1)S(1)}, bf16[8,3,32,128]{3,2,1,0:T(8,128)(2,1)S(1)}, u32[]{:S(2)}, u32[]{:S(2)}) collective-permute-start(bf16[8,3,32,128]{3,2,1,0:T(8,128)(2,1)S(1)} %get-tuple-element.25), channel_id=1, source_target_pairs={{0,1},{1,0},{2,3},{3,2},{4,5},{5,4},{6,7},{7,6},{8,9},{9,8},{10,11... | collective-permute-start | bytes 589832 | tf_op jit(solution)/shard_map/ppermute | solution.py:292
  25.9 7.0 %collective-permute-start.5 = (bf16[8,3,32,128]{3,2,1,0:T(8,128)(2,1)S(1)}, bf16[8,3,32,128]{3,2,1,0:T(8,128)(2,1)S(1)}, u32[]{:S(2)}, u32[]{:S(2)}) collective-permute-start(bf16[8,3,32,128]{3,2,1,0:T(8,128)(2,1)S(1)} %pair.1), channel_id=1, source_target_pairs={{0,2},{1,3},{2,0},{3,1},{4,6},{5,7},{6,4},{7,5},{8,10},{9,11},{10,... | collective-permute-start | bytes 589832 | tf_op jit(solution)/shard_map/ppermute | solution.py:292

commit v4 on v3

--- a/solution.py
+++ b/solution.py
@@ -8,7 +8,8 @@
 from jax.sharding import PartitionSpec as P
 
 SLOTS = 2
-EARLY = 2
+EARLY = (0,)
+LATE = (2, 1, 3)
 VMEM_BYTES = 16 * 1024 * 1024
 
 
@@ -42,35 +43,38 @@
     return places, rows
 
 
-def route_kernel(classes, sdev, source, psi, *refs):
-    outs, (table, load, sems) = refs[: len(classes)], refs[len(classes) :]
+def route_kernel(nsec, source, psi, *refs):
+    outs, (table, held, load, sems) = refs[:nsec], refs[nsec:]
+    sdev = psi.shape[0]
     me = lax.axis_index("sec")
     fetch = pltpu.make_async_copy(source, table, load)
     fetch.start()
+    copies = []
+    for row in range(sdev):
+        copy = pltpu.make_async_copy(psi.at[row], held.at[row], sems.at[row])
+        copy.start()
+        copies.append(copy)
     fetch.wait()
-    copies = []
-    for i, k in enumerate(classes):
-        other = jnp.bitwise_xor(me, k)
-        rows = pick(table, other * sdev, sdev, me)[1]
-        for j in range(SLOTS):
-            copy = pltpu.make_async_copy(psi.at[rows[j]], outs[i].at[j], sems.at[i, j])
-            copy.start()
-            copies.append(copy)
+    rows = [pick(table, jnp.bitwise_xor(me, k) * sdev, sdev, me)[1] for k in range(nsec)]
     for copy in copies:
         copy.wait()
-
-
-def route(classes, source, psi):
+    for k in range(nsec):
+        for j in range(SLOTS):
+            outs[k][j] = held[rows[k][j]]
+
+
+def route(source, psi, nsec):
     block = psi.shape[1:]
     return pl.pallas_call(
-        functools.partial(route_kernel, classes, psi.shape[0]),
-        out_shape=[jax.ShapeDtypeStruct((SLOTS,) + block, psi.dtype)] * len(classes),
+        functools.partial(route_kernel, nsec),
+        out_shape=[jax.ShapeDtypeStruct((SLOTS,) + block, psi.dtype)] * nsec,
         in_specs=[space(pl.ANY)] * 2,
-        out_specs=[space(pl.ANY)] * len(classes),
+        out_specs=[space(pltpu.VMEM)] * nsec,
         scratch_shapes=[
             pltpu.SMEM(source.shape, jnp.int32),
+            pltpu.VMEM(psi.shape, psi.dtype),
             pltpu.SemaphoreType.DMA,
-            pltpu.SemaphoreType.DMA((len(classes), SLOTS)),
+            pltpu.SemaphoreType.DMA((psi.shape[0],)),
         ],
         compiler_params=params(),
         name="route",
@@ -83,17 +87,15 @@
     fetch.start()
     fetch.wait()
     for k in range(nsec):
-        places, rows = pick(table, me * sdev, sdev, jnp.bitwise_xor(me, k))
+        places = pick(table, me * sdev, sdev, jnp.bitwise_xor(me, k))[0]
         for j in range(SLOTS):
             order[k * SLOTS + j] = places[j]
-            if k == 0:
-                order[nsec * SLOTS + j] = rows[j]
 
 
 def receive_order(source, after, nsec, sdev):
     return pl.pallas_call(
         functools.partial(order_kernel, nsec, sdev),
-        out_shape=jax.ShapeDtypeStruct((nsec * SLOTS + SLOTS,), jnp.int32),
+        out_shape=jax.ShapeDtypeStruct((nsec * SLOTS,), jnp.int32),
         in_specs=[space(pl.ANY)] * 2,
         out_specs=space(pltpu.SMEM),
         scratch_shapes=[pltpu.SMEM(source.shape, jnp.int32), pltpu.SemaphoreType.DMA],
@@ -102,19 +104,22 @@
     )(source, after)
 
 
-def product(lhs, block, rhs, ops, base, wdev, phys):
-    rows = lhs.shape[0] // wdev
-    blk = block[0].shape[1]
+def left_rows(lhs, block):
     wide = jnp.dot(lhs, jnp.concatenate(block, axis=1), preferred_element_type=jnp.float32)
-    wide = wide.astype(jnp.bfloat16).astype(jnp.float32)
-    lefts = [wide[:, p * blk : (p + 1) * blk] for p in range(phys)]
+    return wide.astype(jnp.bfloat16)
+
+
+def right_rows(wide, rhs, ops, base, wdev, phys):
+    rows = wide.shape[0] // wdev
+    blk = rhs.shape[1]
     outs = []
     for q in range(phys):
         across = []
         for w in range(wdev):
             total = None
             for p in range(phys):
-                term = lefts[p][w * rows : (w + 1) * rows] * ops[base[w] + p * phys + q]
+                part = wide[w * rows : (w + 1) * rows, p * blk : (p + 1) * blk]
+                term = part.astype(jnp.float32) * ops[base[w] + p * phys + q]
                 total = term if total is None else total + term
             across.append(total.astype(jnp.bfloat16))
         mixed = jnp.concatenate(across, axis=1)
@@ -122,6 +127,10 @@
     return outs
 
 
+def product(lhs, block, rhs, ops, base, wdev, phys):
+    return right_rows(left_rows(lhs, block), rhs, ops, base, wdev, phys)
+
+
 def op_base(t, wdev, sdev, phys):
     return [(w * sdev + t) * (phys * phys) for w in range(wdev)]
 
@@ -129,17 +138,13 @@
 QUARTERS = (2, 0, 3, 1)
 
 
-def early_kernel(nsec, nmpo, order, ops, psi, near_block, left, right, *refs):
-    keep, far_give, near_give, lstage, rstage, local, sems = refs
+def early_kernel(nsec, nmpo, order, ops, *refs):
+    blocks, refs = refs[: len(EARLY)], refs[len(EARLY) :]
+    left, right, keep, far_give, near_give, lstage, rstage = refs
     wdev, sdev, blk = left.shape[:3]
-    phys = local.shape[1]
+    phys = blocks[0].shape[1]
     part = blk // nmpo
     me = lax.axis_index("mpo")
-    copies = []
-    for j in range(SLOTS):
-        copy = pltpu.make_async_copy(psi.at[order[nsec * SLOTS + j]], local.at[j], sems.at[j])
-        copy.start()
-        copies.append(copy)
 
     def side(t):
         rows = []
@@ -149,19 +154,16 @@
                 rows.append(left[w, t, pl.ds(start, part), :])
         return jnp.concatenate(rows, axis=0)
 
-    for s in range((nsec - EARLY) * SLOTS):
-        t = order[EARLY * SLOTS + s]
+    for s in range(len(LATE) * SLOTS):
+        t = order[LATE[s // SLOTS] * SLOTS + s % SLOTS]
         lstage[s] = side(t)
         rstage[s] = right[:, t].reshape(wdev * blk, blk)
-    for copy in copies:
-        copy.wait()
-    for k in (1, 0):
+    for i, k in enumerate(EARLY):
         for j in range(SLOTS):
-            s = k * SLOTS + j
-            t = order[s]
+            s = i * SLOTS + j
+            t = order[k * SLOTS + j]
             rhs = right[:, t].reshape(wdev * blk, blk)
-            source = near_block if k == 1 else local
-            block = [source[j, p] for p in range(phys)]
+            block = [blocks[i][j, p] for p in range(phys)]
             outs = product(side(t), block, rhs, ops, op_base(t, wdev, sdev, phys), wdev, phys)
             for q in range(phys):
                 keep[0, s, q] = outs[q][:part]
@@ -170,23 +172,19 @@
                 near_give[s, q] = outs[q][3 * part :].astype(jnp.bfloat16)
 
 
-def early(order, ops, psi, near_block, left, right, nsec, nmpo):
+def early(order, ops, blocks, left, right, nsec, nmpo):
     wdev, sdev, blk = left.shape[:3]
-    phys = psi.shape[1]
+    phys = blocks[0].shape[1]
     part = blk // nmpo
-    n, late_n = EARLY * SLOTS, (nsec - EARLY) * SLOTS
+    n, late_n = len(EARLY) * SLOTS, len(LATE) * SLOTS
     keep = jax.ShapeDtypeStruct((2, n, phys, part, blk), jnp.float32)
     give = jax.ShapeDtypeStruct((n, phys, part, blk), jnp.bfloat16)
     whole = jax.ShapeDtypeStruct((late_n, wdev * blk, blk), jnp.bfloat16)
     return pl.pallas_call(
         functools.partial(early_kernel, nsec, nmpo),
         out_shape=[keep, give, give, whole, whole],
-        in_specs=[space(pltpu.SMEM)] * 2 + [space(pl.ANY)] + [space(pltpu.VMEM)] * 3,
+        in_specs=[space(pltpu.SMEM)] * 2 + [space(pltpu.VMEM)] * (len(EARLY) + 2),
         out_specs=[space(pltpu.VMEM)] * 5,
-        scratch_shapes=[
-            pltpu.VMEM((SLOTS, phys, blk, blk), jnp.bfloat16),
-            pltpu.SemaphoreType.DMA((SLOTS,)),
-        ],
         compiler_params=params(),
         cost_estimate=pl.CostEstimate(
             flops=n * wdev * phys * blk**3 * 4,
@@ -194,30 +192,42 @@
             transcendentals=0,
         ),
         name="early",
-    )(order, ops, psi, near_block, left, right)
-
-
-def late_kernel(nsec, wdev, sdev, order, ops, *refs):
-    nlate = nsec - EARLY
+    )(order, ops, *blocks, left, right)
+
+
+def late_kernel(nsec, wdev, sdev, order_in, ops_in, *refs):
+    nlate = len(LATE)
     blocks, refs = refs[:nlate], refs[nlate:]
-    lstage, rstage, early_keep, early_far, early_near, keep, far_give, near_give = refs
+    lstage, rstage, early_keep, early_far, early_near, keep, far_give, near_give = refs[:8]
+    order, ops, sems = refs[8:]
     phys, part = far_give.shape[1], far_give.shape[2]
-    for s in range(EARLY * SLOTS):
-        t = order[s]
-        for side in range(2):
-            keep[side, t] = early_keep[side, s]
-        far_give[t] = early_far[s]
-        near_give[t] = early_near[s]
+    loads = [
+        pltpu.make_async_copy(order_in, order, sems.at[0]),
+        pltpu.make_async_copy(ops_in, ops, sems.at[1]),
+    ]
+    for load in loads:
+        load.start()
+    wides = []
     for s in range(nlate * SLOTS):
-        t = order[EARLY * SLOTS + s]
         block = [blocks[s // SLOTS][s % SLOTS, p] for p in range(phys)]
+        wides.append(left_rows(lstage[s], block))
+    for load in loads:
+        load.wait()
+    for s in range(nlate * SLOTS):
+        t = order[LATE[s // SLOTS] * SLOTS + s % SLOTS]
         base = op_base(t, wdev, sdev, phys)
-        outs = product(lstage[s], block, rstage[s], ops, base, wdev, phys)
+        outs = right_rows(wides[s], rstage[s], ops, base, wdev, phys)
         for q in range(phys):
             keep[0, t, q] = outs[q][:part]
             keep[1, t, q] = outs[q][part : 2 * part]
             far_give[t, q] = outs[q][2 * part : 3 * part].astype(jnp.bfloat16)
             near_give[t, q] = outs[q][3 * part :].astype(jnp.bfloat16)
+    for s in range(len(EARLY) * SLOTS):
+        t = order[EARLY[s // SLOTS] * SLOTS + s % SLOTS]
+        for side in range(2):
+            keep[side, t] = early_keep[side, s]
+        far_give[t] = early_far[s]
+        near_give[t] = early_near[s]
 
 
 def late(order, ops, blocks, staged, nsec, wdev, sdev):
@@ -227,8 +237,13 @@
     return pl.pallas_call(
         functools.partial(late_kernel, nsec, wdev, sdev),
         out_shape=[jax.ShapeDtypeStruct((2, sdev, phys, part, blk), jnp.float32), give, give],
-        in_specs=[space(pltpu.SMEM)] * 2 + [space(pltpu.VMEM)] * (len(blocks) + 5),
+        in_specs=[space(pl.ANY)] * 2 + [space(pltpu.VMEM)] * (len(blocks) + 5),
         out_specs=[space(pltpu.VMEM)] * 3,
+        scratch_shapes=[
+            pltpu.SMEM(order.shape, order.dtype),
+            pltpu.SMEM(ops.shape, ops.dtype),
+            pltpu.SemaphoreType.DMA((2,)),
+        ],
         compiler_params=params(),
         cost_estimate=pl.CostEstimate(
             flops=n * wdev * phys * blk**3 * 4,
@@ -280,21 +295,19 @@
     blocks = jnp.transpose(psi, (0, 2, 1, 3))
     ops = site_op.astype(jnp.float32).reshape(-1)
     table = pltpu.with_memory_space_constraint(source, pltpu.HBM)
-    outgoing = route(
-        tuple(range(1, nsec)), table, pltpu.with_memory_space_constraint(blocks, pltpu.HBM)
-    )
-    order = receive_order(table, outgoing[0], nsec, sdev)
-    arrived = []
+    held = route(table, pltpu.with_memory_space_constraint(blocks, pltpu.HBM), nsec)
+    order = receive_order(table, held[0], nsec, sdev)
+    arrived = [held[0]]
     for k in range(1, nsec):
-        arrived.append(lax.ppermute(outgoing[k - 1], "sec", [(i, i ^ k) for i in range(nsec)]))
+        arrived.append(lax.ppermute(held[k], "sec", [(i, i ^ k) for i in range(nsec)]))
 
     def across(value, m):
         return lax.ppermute(value, "mpo", [(i, i ^ m) for i in range(nmpo)])
 
-    staged = early(order, ops, blocks, arrived[0], left_env, right_env, nsec, nmpo)
-    keep, far_give, near_give = late(order, ops, arrived[1:], staged, nsec, wdev, sdev)
-    over = across(pair(keep, across(far_give, 1)), 2)
-    out = finish(keep, across(near_give, 1), over)
+    staged = early(order, ops, [arrived[k] for k in EARLY], left_env, right_env, nsec, nmpo)
+    keep, far_give, near_give = late(order, ops, [arrived[k] for k in LATE], staged, nsec, wdev, sdev)
+    far = across(pair(keep, across(far_give, 1)), 2)
+    out = finish(keep, across(near_give, 1), far)
     return jnp.transpose(out, (0, 2, 1, 3))
 
 

time: 34 us -> 32.5 us (0.956)
  the two profiles are of different devices: /device:TPU:10 before, /device:TPU:18 now
where the time goes in v4:
time: 32.5 us; the launch traced here: 32.4 us
  waiting for transfers between devices  21.1 us (65%)
  Pallas kernels  6.23 us (19%)
  starting transfers between devices  4.73 us (15%)
    ppermute x3, waiting for transfers between devices, fast_shards(): lax.ppermute(held[k], 'sec', [(i, i ^ k) for i in range(nsec)])  13.8 us
    ppermute x3, waiting for transfers between devices, across(): return lax.ppermute(value, 'mpo', [(i, i ^ m) for i in range(nmpo)])  7.34 us
    ppermute x3, starting transfers between devices, fast_shards(): lax.ppermute(held[k], 'sec', [(i, i ^ k) for i in range(nsec)])  3.55 us
    pallas_call x1, Pallas kernels, route(): pl.pallas_call(functools.partial(route_kernel, nsec), out_shape=[jax.Shap...  1.43 us
    pallas_call x1, Pallas kernels, receive_order(): pl.pallas_call(functools.partial(order_kernel, nsec, sdev), out_shape=jax...  1.37 us
    pallas_call x1, Pallas kernels, late(): pl.pallas_call(functools.partial(late_kernel, nsec, wdev, sdev), out_shap...  1.31 us
    pallas_call x1, Pallas kernels, early(): pl.pallas_call(functools.partial(early_kernel, nsec, nmpo), out_shape=[ke...  1.26 us
    ppermute x3, starting transfers between devices, across(): return lax.ppermute(value, 'mpo', [(i, i ^ m) for i in range(nmpo)])  1.17 us
  transfers between devices with their start and end apart: 6, of which 5 were waited for; matrix products, arithmetic and copies ran while one was open for 1% of the time, Pallas kernels for 8%

profile of v4, /device:TPU:18, one launch (start us, length us, event | category | flops | bytes accessed | tf_op | source)
XLA Modules:
  0.0 32.4 jit_solution(5463022479045147846)
XLA Ops:
  0.0 0.0 copy-start.2
  0.0 0.0 copy-start
  0.0 0.0 copy-start.1
  0.0 1.4 %route.1 = (bf16[2,3,128,128]{3,2,1,0:T(8,128)(2,1)S(1)}, bf16[2,3,128,128]{3,2,1,0:T(8,128)(2,1)S(1)}, bf16[2,3,128,128]{3,2,1,0:T(8,128)(2,1)S(1)}, bf16[2,3,128,128]{3,2,1,0:T(8,128)(2,1)S(1)}) custom-call(s32[1,32]{1,0:T(1,128)} %source.3, bf16[8,3,128,128]{3,2,1,0:T(8,128)(2,1)} %bitcast.2), custom_call_target="tpu_custom_call" | custom-call | tf_op jit(solution)/shard_map/route/pallas_call | solution.py:68
  1.4 0.4 %collective-permute-start = (bf16[2,3,128,128]{3,2,1,0:T(8,128)(2,1)S(1)}, bf16[2,3,128,128]{3,2,1,0:T(8,128)(2,1)S(1)}, u32[]{:S(2)}, u32[]{:S(2)}) collective-permute-start(bf16[2,3,128,128]{3,2,1,0:T(8,128)(2,1)S(1)} %get-tuple-element.18), channel_id=1, source_target_pairs={{0,8},{4,12},{8,0},{12,4},{1,9},{5,13},{9,1},{13,5},{2,10},{6,14},... | collective-permute-start | bytes 589832 | tf_op jit(solution)/shard_map/ppermute | solution.py:302
  1.8 1.6 %collective-permute-start.1 = (bf16[2,3,128,128]{3,2,1,0:T(8,128)(2,1)S(1)}, bf16[2,3,128,128]{3,2,1,0:T(8,128)(2,1)S(1)}, u32[]{:S(2)}, u32[]{:S(2)}) collective-permute-start(bf16[2,3,128,128]{3,2,1,0:T(8,128)(2,1)S(1)} %get-tuple-element.19), channel_id=1, source_target_pairs={{0,4},{4,0},{8,12},{12,8},{1,5},{5,1},{9,13},{13,9},{2,6},{6,2},{1... | collective-permute-start | bytes 589832 | tf_op jit(solution)/shard_map/ppermute | solution.py:302
  3.4 1.6 %collective-permute-start.2 = (bf16[2,3,128,128]{3,2,1,0:T(8,128)(2,1)S(1)}, bf16[2,3,128,128]{3,2,1,0:T(8,128)(2,1)S(1)}, u32[]{:S(2)}, u32[]{:S(2)}) collective-permute-start(bf16[2,3,128,128]{3,2,1,0:T(8,128)(2,1)S(1)} %get-tuple-element.20), channel_id=1, source_target_pairs={{0,12},{4,8},{8,4},{12,0},{1,13},{5,9},{9,5},{13,1},{2,14},{6,10},... | collective-permute-start | bytes 589832 | tf_op jit(solution)/shard_map/ppermute | solution.py:302
  5.0 0.0 copy-done.2
  5.0 0.1 copy.6
  5.1 0.1 reshape.8.ops.ops_in
  5.3 1.4 %order.1.order_in = s32[8]{0:T(128)S(1)} custom-call(s32[1,32]{1,0:T(1,128)} %source.3, bf16[2,3,128,128]{3,2,1,0:T(8,128)(2,1)S(1)} %get-tuple-element.17.after.refs_0_), custom_call_target="tpu_custom_call" | custom-call | tf_op jit(solution)/shard_map/order/pallas_call | solution.py:96
  6.6 0.0 copy-done
  6.6 0.0 copy-done.1
  6.6 1.3 %early.1 = (f32[2,2,3,32,128]{4,3,2,1,0:T(8,128)S(1)}, bf16[2,3,32,128]{3,2,1,0:T(8,128)(2,1)S(1)}, bf16[2,3,32,128]{3,2,1,0:T(8,128)(2,1)S(1)}, bf16[6,256,128]...) custom-call(s32[8]{0:T(128)S(1)} %order.1.order_in, f32[144]{0:T(256)S(1)} %reshape.8.ops.ops_in, ...), custom_call_target="tpu_custom_call" | custom-call | flops 100663296 | bytes 8388608 | tf_op jit(solution)/shard_map/early/pallas_call | solution.py:183
  7.9 4.1 %collective-permute-done.refs_0_ = bf16[2,3,128,128]{3,2,1,0:T(8,128)(2,1)S(1)} collective-permute-done((bf16[2,3,128,128]{3,2,1,0:T(8,128)(2,1)S(1)}, bf16[2,3,128,128]{3,2,1,0:T(8,128)(2,1)S(1)}, u32[]{:S(2)}, u32[]{:S(2)}) %collective-permute-start) | collective-permute-done | bytes 196640 | tf_op jit(solution)/shard_map/ppermute | solution.py:302
  12.0 1.4 %collective-permute-done.1.refs_1_ = bf16[2,3,128,128]{3,2,1,0:T(8,128)(2,1)S(1)} collective-permute-done((bf16[2,3,128,128]{3,2,1,0:T(8,128)(2,1)S(1)}, bf16[2,3,128,128]{3,2,1,0:T(8,128)(2,1)S(1)}, u32[]{:S(2)}, u32[]{:S(2)}) %collective-permute-start.1) | collective-permute-done | bytes 196640 | tf_op jit(solution)/shard_map/ppermute | solution.py:302
  13.4 8.3 %collective-permute-done.2.refs_2_ = bf16[2,3,128,128]{3,2,1,0:T(8,128)(2,1)S(1)} collective-permute-done((bf16[2,3,128,128]{3,2,1,0:T(8,128)(2,1)S(1)}, bf16[2,3,128,128]{3,2,1,0:T(8,128)(2,1)S(1)}, u32[]{:S(2)}, u32[]{:S(2)}) %collective-permute-start.2) | collective-permute-done | bytes 196640 | tf_op jit(solution)/shard_map/ppermute | solution.py:302
  21.7 1.3 %late.1 = (f32[2,8,3,32,128]{4,3,2,1,0:T(8,128)S(1)}, bf16[8,3,32,128]{3,2,1,0:T(8,128)(2,1)S(1)}, bf16[8,3,32,128]{3,2,1,0:T(8,128)(2,1)S(1)}) custom-call(s32[8]{0:T(128)S(1)} %order.1.order_in, f32[144]{0:T(256)S(1)} %reshape.8.ops.ops_in, bf16[2,3,128,128]{3,2,1,0:T(8,128)(2,1)S(1)} %collective-permute-done.refs_0_, ...), custom_call_target="tpu_custom_call" | custom-call | flops 301989888 | bytes 8388608 | tf_op jit(solution)/shard_map/late/pallas_call | solution.py:237
  23.0 0.1 collective-permute-start.4
  23.1 0.5 %collective-permute-start.3 = (bf16[8,3,32,128]{3,2,1,0:T(8,128)(2,1)S(1)}, bf16[8,3,32,128]{3,2,1,0:T(8,128)(2,1)S(1)}, u32[]{:S(2)}, u32[]{:S(2)}) collective-permute-start(bf16[8,3,32,128]{3,2,1,0:T(8,128)(2,1)S(1)} %get-tuple-element.27), channel_id=1, source_target_pairs={{0,1},{1,0},{2,3},{3,2},{4,5},{5,4},{6,7},{7,6},{8,9},{9,8},{10,11... | collective-permute-start | bytes 589832 | tf_op jit(solution)/shard_map/ppermute | solution.py:305
  23.6 0.9 %collective-permute-done.4.got = bf16[8,3,32,128]{3,2,1,0:T(8,128)(2,1)S(1)} collective-permute-done((bf16[8,3,32,128]{3,2,1,0:T(8,128)(2,1)S(1)}, bf16[8,3,32,128]{3,2,1,0:T(8,128)(2,1)S(1)}, u32[]{:S(2)}, u32[]{:S(2)}) %collective-permute-start.4) | collective-permute-done | bytes 196640 | tf_op jit(solution)/shard_map/ppermute | solution.py:305
  24.6 0.6 %collective-permute-start.5 = (bf16[8,3,32,128]{3,2,1,0:T(8,128)(2,1)S(1)}, bf16[8,3,32,128]{3,2,1,0:T(8,128)(2,1)S(1)}, u32[]{:S(2)}, u32[]{:S(2)}) collective-permute-start(bf16[8,3,32,128]{3,2,1,0:T(8,128)(2,1)S(1)} %pair.1), channel_id=1, source_target_pairs={{0,2},{1,3},{2,0},{3,1},{4,6},{5,7},{6,4},{7,5},{8,10},{9,11},{10,... | collective-permute-start | bytes 589832 | tf_op jit(solution)/shard_map/ppermute | solution.py:305
  25.2 0.0 collective-permute-done.3.near
  25.2 6.4 %collective-permute-done.5.far = bf16[8,3,32,128]{3,2,1,0:T(8,128)(2,1)S(1)} collective-permute-done((bf16[8,3,32,128]{3,2,1,0:T(8,128)(2,1)S(1)}, bf16[8,3,32,128]{3,2,1,0:T(8,128)(2,1)S(1)}, u32[]{:S(2)}, u32[]{:S(2)}) %collective-permute-start.5) | collective-permute-done | bytes 196640 | tf_op jit(solution)/shard_map/ppermute | solution.py:305
  31.6 0.8 %finish.1 = bf16[32,3,8,128]{3,2,1,0:T(8,128)(2,1)} custom-call(f32[2,8,3,32,128]{4,3,2,1,0:T(8,128)S(1)} %get-tuple-element.26.keep, bf16[8,3,32,128]{3,2,1,0:T(8,128)(2,1)S(1)} %collective-permute-done.3.near, bf16[8,3,32,128]{3,2,1,0:T(8,128)(2,1)S(1)} %collective-permute-done.5.far), custom_call_target="tpu_custom_call" | custom-call | tf_op jit(solution)/shard_map/finish/pallas_call | solution.py:280
  (1 shorter events, 0.0 us)
Async XLA Ops:
  0.0 5.0 %copy-start.2 = (bf16[2,8,3,3]{1,0,3,2:T(2,128)(2,1)S(1)}, bf16[2,8,3,3]{1,0,3,2:T(2,128)(2,1)}, u32[]{:S(2)}) copy-start(bf16[2,8,3,3]{1,0,3,2:T(2,128)(2,1)} %param.8) | copy-start | bytes 868
  0.0 6.6 %copy-start = (bf16[2,8,128,128]{3,2,1,0:T(8,128)(2,1)S(1)}, bf16[2,8,128,128]{3,2,1,0:T(8,128)(2,1)}, u32[]{:S(2)}) copy-start(bf16[2,8,128,128]{3,2,1,0:T(8,128)(2,1)} %refs_1_.1) | copy-start | bytes 1572868
  0.0 6.6 %copy-start.1 = (bf16[2,8,128,128]{3,2,1,0:T(8,128)(2,1)S(1)}, bf16[2,8,128,128]{3,2,1,0:T(8,128)(2,1)}, u32[]{:S(2)}) copy-start(bf16[2,8,128,128]{3,2,1,0:T(8,128)(2,1)} %refs_2_.1) | copy-start | bytes 1572868
  1.4 10.6 %collective-permute-start = (bf16[2,3,128,128]{3,2,1,0:T(8,128)(2,1)S(1)}, bf16[2,3,128,128]{3,2,1,0:T(8,128)(2,1)S(1)}, u32[]{:S(2)}, u32[]{:S(2)}) collective-permute-start(bf16[2,3,128,128]{3,2,1,0:T(8,128)(2,1)S(1)} %get-tuple-element.18), channel_id=1, source_target_pairs={{0,8},{4,12},{8,0},{12,4},{1,9},{5,13},{9,1},{13,5},{2,10},{6,14},... | collective-permute-start | bytes 589832 | tf_op jit(solution)/shard_map/ppermute | solution.py:302
  1.8 11.6 %collective-permute-start.1 = (bf16[2,3,128,128]{3,2,1,0:T(8,128)(2,1)S(1)}, bf16[2,3,128,128]{3,2,1,0:T(8,128)(2,1)S(1)}, u32[]{:S(2)}, u32[]{:S(2)}) collective-permute-start(bf16[2,3,128,128]{3,2,1,0:T(8,128)(2,1)S(1)} %get-tuple-element.19), channel_id=1, source_target_pairs={{0,4},{4,0},{8,12},{12,8},{1,5},{5,1},{9,13},{13,9},{2,6},{6,2},{1... | collective-permute-start | bytes 589832 | tf_op jit(solution)/shard_map/ppermute | solution.py:302
  3.4 18.3 %collective-permute-start.2 = (bf16[2,3,128,128]{3,2,1,0:T(8,128)(2,1)S(1)}, bf16[2,3,128,128]{3,2,1,0:T(8,128)(2,1)S(1)}, u32[]{:S(2)}, u32[]{:S(2)}) collective-permute-start(bf16[2,3,128,128]{3,2,1,0:T(8,128)(2,1)S(1)} %get-tuple-element.20), channel_id=1, source_target_pairs={{0,12},{4,8},{8,4},{12,0},{1,13},{5,9},{9,5},{13,1},{2,14},{6,10},... | collective-permute-start | bytes 589832 | tf_op jit(solution)/shard_map/ppermute | solution.py:302
  23.0 1.5 %collective-permute-start.4 = (bf16[8,3,32,128]{3,2,1,0:T(8,128)(2,1)S(1)}, bf16[8,3,32,128]{3,2,1,0:T(8,128)(2,1)S(1)}, u32[]{:S(2)}, u32[]{:S(2)}) collective-permute-start(bf16[8,3,32,128]{3,2,1,0:T(8,128)(2,1)S(1)} %get-tuple-element.28), channel_id=1, source_target_pairs={{0,1},{1,0},{2,3},{3,2},{4,5},{5,4},{6,7},{7,6},{8,9},{9,8},{10,11... | collective-permute-start | bytes 589832 | tf_op jit(solution)/shard_map/ppermute | solution.py:305
  23.1 2.1 %collective-permute-start.3 = (bf16[8,3,32,128]{3,2,1,0:T(8,128)(2,1)S(1)}, bf16[8,3,32,128]{3,2,1,0:T(8,128)(2,1)S(1)}, u32[]{:S(2)}, u32[]{:S(2)}) collective-permute-start(bf16[8,3,32,128]{3,2,1,0:T(8,128)(2,1)S(1)} %get-tuple-element.27), channel_id=1, source_target_pairs={{0,1},{1,0},{2,3},{3,2},{4,5},{5,4},{6,7},{7,6},{8,9},{9,8},{10,11... | collective-permute-start | bytes 589832 | tf_op jit(solution)/shard_map/ppermute | solution.py:305
  24.6 7.0 %collective-permute-start.5 = (bf16[8,3,32,128]{3,2,1,0:T(8,128)(2,1)S(1)}, bf16[8,3,32,128]{3,2,1,0:T(8,128)(2,1)S(1)}, u32[]{:S(2)}, u32[]{:S(2)}) collective-permute-start(bf16[8,3,32,128]{3,2,1,0:T(8,128)(2,1)S(1)} %pair.1), channel_id=1, source_target_pairs={{0,2},{1,3},{2,0},{3,1},{4,6},{5,7},{6,4},{7,5},{8,10},{9,11},{10,... | collective-permute-start | bytes 589832 | tf_op jit(solution)/shard_map/ppermute | solution.py:305

commit v5 on v4

--- a/solution.py
+++ b/solution.py
@@ -9,7 +9,10 @@
 
 SLOTS = 2
 EARLY = (0,)
-LATE = (2, 1, 3)
+MID = (2, 1)
+LAST = 3
+LATE = MID + (LAST,)
+NAME_ROWS = 16
 VMEM_BYTES = 16 * 1024 * 1024
 
 
@@ -43,8 +46,8 @@
     return places, rows
 
 
-def route_kernel(nsec, source, psi, *refs):
-    outs, (table, held, load, sems) = refs[:nsec], refs[nsec:]
+def route_kernel(classes, source, psi, *refs):
+    outs, (table, held, load, sems) = refs[: len(classes)], refs[len(classes) :]
     sdev = psi.shape[0]
     me = lax.axis_index("sec")
     fetch = pltpu.make_async_copy(source, table, load)
@@ -55,21 +58,21 @@
         copy.start()
         copies.append(copy)
     fetch.wait()
-    rows = [pick(table, jnp.bitwise_xor(me, k) * sdev, sdev, me)[1] for k in range(nsec)]
+    rows = [pick(table, jnp.bitwise_xor(me, k) * sdev, sdev, me)[1] for k in classes]
     for copy in copies:
         copy.wait()
-    for k in range(nsec):
+    for i in range(len(classes)):
         for j in range(SLOTS):
-            outs[k][j] = held[rows[k][j]]
-
-
-def route(source, psi, nsec):
+            outs[i][j] = held[rows[i][j]]
+
+
+def route(classes, source, psi):
     block = psi.shape[1:]
     return pl.pallas_call(
-        functools.partial(route_kernel, nsec),
-        out_shape=[jax.ShapeDtypeStruct((SLOTS,) + block, psi.dtype)] * nsec,
+        functools.partial(route_kernel, classes),
+        out_shape=[jax.ShapeDtypeStruct((SLOTS,) + block, psi.dtype)] * len(classes),
         in_specs=[space(pl.ANY)] * 2,
-        out_specs=[space(pltpu.VMEM)] * nsec,
+        out_specs=[space(pltpu.VMEM)] * len(classes),
         scratch_shapes=[
             pltpu.SMEM(source.shape, jnp.int32),
             pltpu.VMEM(psi.shape, psi.dtype),
@@ -79,6 +82,26 @@
         compiler_params=params(),
         name="route",
     )(source, psi)
+
+
+def double_kernel(block, out, sems):
+    copies = [pltpu.make_async_copy(block, out.at[i], sems.at[i]) for i in range(2)]
+    for copy in copies:
+        copy.start()
+    for copy in copies:
+        copy.wait()
+
+
+def double(block):
+    return pl.pallas_call(
+        double_kernel,
+        out_shape=jax.ShapeDtypeStruct((2,) + block.shape, block.dtype),
+        in_specs=[space(pltpu.VMEM)],
+        out_specs=space(pl.ANY),
+        scratch_shapes=[pltpu.SemaphoreType.DMA((2,))],
+        compiler_params=params(),
+        name="double",
+    )(block)
 
 
 def order_kernel(nsec, sdev, source, after, order, table, load):
@@ -109,7 +132,7 @@
     return wide.astype(jnp.bfloat16)
 
 
-def right_rows(wide, rhs, ops, base, wdev, phys):
+def right_rows(wide, rhs, op, wdev, phys):
     rows = wide.shape[0] // wdev
     blk = rhs.shape[1]
     outs = []
@@ -119,7 +142,7 @@
             total = None
             for p in range(phys):
                 part = wide[w * rows : (w + 1) * rows, p * blk : (p + 1) * blk]
-                term = part.astype(jnp.float32) * ops[base[w] + p * phys + q]
+                term = part.astype(jnp.float32) * op(w, p, q)
                 total = term if total is None else total + term
             across.append(total.astype(jnp.bfloat16))
         mixed = jnp.concatenate(across, axis=1)
@@ -127,12 +150,16 @@
     return outs
 
 
-def product(lhs, block, rhs, ops, base, wdev, phys):
-    return right_rows(left_rows(lhs, block), rhs, ops, base, wdev, phys)
-
-
-def op_base(t, wdev, sdev, phys):
-    return [(w * sdev + t) * (phys * phys) for w in range(wdev)]
+def scalar_op(ops, t, sdev, phys):
+    return lambda w, p, q: ops[(w * sdev + t) * (phys * phys) + p * phys + q]
+
+
+def row_op(rows, s, phys):
+    def op(w, p, q):
+        i = (w * phys + p) * phys + q
+        return rows[s, i : i + 1, :]
+
+    return op
 
 
 QUARTERS = (2, 0, 3, 1)
@@ -140,7 +167,7 @@
 
 def early_kernel(nsec, nmpo, order, ops, *refs):
     blocks, refs = refs[: len(EARLY)], refs[len(EARLY) :]
-    left, right, keep, far_give, near_give, lstage, rstage = refs
+    left, right, keep, far_give, near_give, lstage, rstage, oprows, named = refs
     wdev, sdev, blk = left.shape[:3]
     phys = blocks[0].shape[1]
     part = blk // nmpo
@@ -158,13 +185,23 @@
         t = order[LATE[s // SLOTS] * SLOTS + s % SLOTS]
         lstage[s] = side(t)
         rstage[s] = right[:, t].reshape(wdev * blk, blk)
+    for s in range(SLOTS):
+        t = order[LAST * SLOTS + s]
+        named[s] = jnp.full(named.shape[1:], t.astype(jnp.float32), jnp.float32).astype(named.dtype)
+        op = scalar_op(ops, t, sdev, phys)
+        for w in range(wdev):
+            for p in range(phys):
+                for q in range(phys):
+                    i = (w * phys + p) * phys + q
+                    oprows[s, i : i + 1, :] = jnp.full((1, blk), op(w, p, q), jnp.float32)
     for i, k in enumerate(EARLY):
         for j in range(SLOTS):
             s = i * SLOTS + j
             t = order[k * SLOTS + j]
             rhs = right[:, t].reshape(wdev * blk, blk)
             block = [blocks[i][j, p] for p in range(phys)]
-            outs = product(side(t), block, rhs, ops, op_base(t, wdev, sdev, phys), wdev, phys)
+            op = scalar_op(ops, t, sdev, phys)
+            outs = right_rows(left_rows(side(t), block), rhs, op, wdev, phys)
             for q in range(phys):
                 keep[0, s, q] = outs[q][:part]
                 keep[1, s, q] = outs[q][part : 2 * part]
@@ -179,12 +216,14 @@
     n, late_n = len(EARLY) * SLOTS, len(LATE) * SLOTS
     keep = jax.ShapeDtypeStruct((2, n, phys, part, blk), jnp.float32)
     give = jax.ShapeDtypeStruct((n, phys, part, blk), jnp.bfloat16)
+    rows = jax.ShapeDtypeStruct((SLOTS, wdev * phys * phys, blk), jnp.float32)
+    name = jax.ShapeDtypeStruct((SLOTS, NAME_ROWS, blk), jnp.bfloat16)
     whole = jax.ShapeDtypeStruct((late_n, wdev * blk, blk), jnp.bfloat16)
     return pl.pallas_call(
         functools.partial(early_kernel, nsec, nmpo),
-        out_shape=[keep, give, give, whole, whole],
+        out_shape=[keep, give, give, whole, whole, rows, name],
         in_specs=[space(pltpu.SMEM)] * 2 + [space(pltpu.VMEM)] * (len(EARLY) + 2),
-        out_specs=[space(pltpu.VMEM)] * 5,
+        out_specs=[space(pltpu.VMEM)] * 7,
         compiler_params=params(),
         cost_estimate=pl.CostEstimate(
             flops=n * wdev * phys * blk**3 * 4,
@@ -195,9 +234,9 @@
     )(order, ops, *blocks, left, right)
 
 
-def late_kernel(nsec, wdev, sdev, order_in, ops_in, *refs):
-    nlate = len(LATE)
-    blocks, refs = refs[:nlate], refs[nlate:]
+def mid_kernel(wdev, sdev, order_in, ops_in, *refs):
+    nmid = len(MID)
+    blocks, refs = refs[:nmid], refs[nmid:]
     lstage, rstage, early_keep, early_far, early_near, keep, far_give, near_give = refs[:8]
     order, ops, sems = refs[8:]
     phys, part = far_give.shape[1], far_give.shape[2]
@@ -208,34 +247,43 @@
     for load in loads:
         load.start()
     wides = []
-    for s in range(nlate * SLOTS):
+    for s in range(nmid * SLOTS):
         block = [blocks[s // SLOTS][s % SLOTS, p] for p in range(phys)]
         wides.append(left_rows(lstage[s], block))
     for load in loads:
         load.wait()
-    for s in range(nlate * SLOTS):
-        t = order[LATE[s // SLOTS] * SLOTS + s % SLOTS]
-        base = op_base(t, wdev, sdev, phys)
-        outs = right_rows(wides[s], rstage[s], ops, base, wdev, phys)
+
+    def place(classes, s):
+        return order[classes[s // SLOTS] * SLOTS + s % SLOTS]
+
+    for s in range(nmid * SLOTS):
+        t = place(MID, s)
+        outs = right_rows(wides[s], rstage[s], scalar_op(ops, t, sdev, phys), wdev, phys)
         for q in range(phys):
             keep[0, t, q] = outs[q][:part]
             keep[1, t, q] = outs[q][part : 2 * part]
             far_give[t, q] = outs[q][2 * part : 3 * part].astype(jnp.bfloat16)
             near_give[t, q] = outs[q][3 * part :].astype(jnp.bfloat16)
     for s in range(len(EARLY) * SLOTS):
-        t = order[EARLY[s // SLOTS] * SLOTS + s % SLOTS]
+        t = place(EARLY, s)
         for side in range(2):
             keep[side, t] = early_keep[side, s]
         far_give[t] = early_far[s]
         near_give[t] = early_near[s]
-
-
-def late(order, ops, blocks, staged, nsec, wdev, sdev):
+    for s in range(SLOTS):
+        t = order[LAST * SLOTS + s]
+        for side in range(2):
+            keep[side, t] = jnp.zeros(keep.shape[2:], keep.dtype)
+        far_give[t] = jnp.zeros(far_give.shape[1:], far_give.dtype)
+        near_give[t] = jnp.zeros(near_give.shape[1:], near_give.dtype)
+
+
+def mid(order, ops, blocks, staged, wdev, sdev):
     phys, part, blk = staged[0].shape[2:]
     n = len(blocks) * SLOTS
     give = jax.ShapeDtypeStruct((sdev, phys, part, blk), jnp.bfloat16)
     return pl.pallas_call(
-        functools.partial(late_kernel, nsec, wdev, sdev),
+        functools.partial(mid_kernel, wdev, sdev),
         out_shape=[jax.ShapeDtypeStruct((2, sdev, phys, part, blk), jnp.float32), give, give],
         in_specs=[space(pl.ANY)] * 2 + [space(pltpu.VMEM)] * (len(blocks) + 5),
         out_specs=[space(pltpu.VMEM)] * 3,
@@ -250,8 +298,45 @@
             bytes_accessed=8 * 1024 * 1024,
             transcendentals=0,
         ),
-        name="late",
-    )(order, ops, *blocks, *staged[3:], *staged[:3])
+        name="mid",
+    )(order, ops, *blocks, *staged[3:5], *staged[:3])
+
+
+def last_kernel(wdev, after, block, lstage, rstage, oprows, named, *gives):
+    phys, blk = block.shape[2], block.shape[4]
+    part = blk // len(gives)
+    first = len(MID) * SLOTS
+    me = lax.axis_index("sec")
+    other = (jnp.bitwise_xor(me, LAST) > me).astype(jnp.int32)
+    wides = []
+    for s in range(SLOTS):
+        wides.append(left_rows(lstage[first + s], [block[other, s, p] for p in range(phys)]))
+    for s in range(SLOTS):
+        outs = right_rows(wides[s], rstage[first + s], row_op(oprows, s, phys), wdev, phys)
+        for i, m in enumerate(QUARTERS):
+            for q in range(phys):
+                rows = outs[q][i * part : (i + 1) * part].astype(gives[m].dtype)
+                gives[m][s, q * part : (q + 1) * part] = rows
+            gives[m][s, phys * part :] = named[s].astype(gives[m].dtype)
+
+
+def last(after, block, staged, wdev):
+    phys, part, blk = staged[0].shape[2:]
+    shape = (SLOTS, phys * part + NAME_ROWS, blk)
+    give = jax.ShapeDtypeStruct(shape, jnp.bfloat16)
+    return pl.pallas_call(
+        functools.partial(last_kernel, wdev),
+        out_shape=[jax.ShapeDtypeStruct(shape, jnp.float32)] + [give] * 3,
+        in_specs=[space(pl.ANY)] + [space(pltpu.VMEM)] * 5,
+        out_specs=[space(pltpu.VMEM)] * 4,
+        compiler_params=params(),
+        cost_estimate=pl.CostEstimate(
+            flops=SLOTS * wdev * phys * blk**3 * 4,
+            bytes_accessed=4 * 1024 * 1024,
+            transcendentals=0,
+        ),
+        name="last",
+    )(after, block, *staged[3:])
 
 
 def pair_kernel(keep, got, out):
@@ -269,22 +354,54 @@
     )(keep, got)
 
 
-def finish_kernel(keep, near, far, out):
-    for q in range(out.shape[1]):
-        total = keep[1, :, q] + near[:, q].astype(jnp.float32) + far[:, q].astype(jnp.float32)
-        out[:, q] = jnp.swapaxes(total, 0, 1).astype(out.dtype)
-
-
-def finish(keep, near, far):
-    sdev, phys, part, blk = far.shape
+def tail_sum(tails, t):
+    total = None
+    for tail in tails:
+        rows = tail.shape[1] - NAME_ROWS
+        for s in range(SLOTS):
+            here = tail[s, rows:, :].astype(jnp.float32)[:1] == t
+            value = jnp.where(here, tail[s, :rows, :].astype(jnp.float32), 0.0)
+            total = value if total is None else total + value
+    return total
+
+
+def base_kernel(keep, near, far, own, mate, acc):
+    phys, part, blk = acc.shape[1:]
+    for t in range(acc.shape[0]):
+        total = keep[1, t] + near[t].astype(jnp.float32) + far[t].astype(jnp.float32)
+        acc[t] = total + tail_sum((own, mate), t).reshape(phys, part, blk)
+
+
+def base(keep, near, far, own, mate):
+    return pl.pallas_call(
+        base_kernel,
+        out_shape=jax.ShapeDtypeStruct(far.shape, jnp.float32),
+        in_specs=[space(pltpu.VMEM)] * 5,
+        out_specs=space(pltpu.VMEM),
+        compiler_params=params(),
+        name="base",
+    )(keep, near, far, own, mate)
+
+
+def finish_kernel(total, tail2, tail3, out, acc):
+    sdev, phys, part, blk = acc.shape
+    for t in range(sdev):
+        acc[t] = total[t] + tail_sum((tail2, tail3), t).reshape(phys, part, blk)
+    for q in range(phys):
+        out[:, q] = jnp.swapaxes(acc[:, q], 0, 1).astype(out.dtype)
+
+
+def finish(total, tail2, tail3):
+    sdev, phys, part, blk = total.shape
     return pl.pallas_call(
         finish_kernel,
         out_shape=jax.ShapeDtypeStruct((part, phys, sdev, blk), jnp.bfloat16),
         in_specs=[space(pltpu.VMEM)] * 3,
         out_specs=space(pltpu.VMEM),
+        scratch_shapes=[pltpu.VMEM(total.shape, total.dtype)],
         compiler_params=params(),
         name="finish",
-    )(keep, near, far)
+    )(total, tail2, tail3)
 
 
 def fast_shards(psi, left_env, right_env, site_op, source):
@@ -295,19 +412,27 @@
     blocks = jnp.transpose(psi, (0, 2, 1, 3))
     ops = site_op.astype(jnp.float32).reshape(-1)
     table = pltpu.with_memory_space_constraint(source, pltpu.HBM)
-    held = route(table, pltpu.with_memory_space_constraint(blocks, pltpu.HBM), nsec)
-    order = receive_order(table, held[0], nsec, sdev)
-    arrived = [held[0]]
-    for k in range(1, nsec):
-        arrived.append(lax.ppermute(held[k], "sec", [(i, i ^ k) for i in range(nsec)]))
+    pinned = pltpu.with_memory_space_constraint(blocks, pltpu.HBM)
+    held = route(EARLY + MID + (LAST,), table, pinned)
+    arrived = {0: held[0]}
+    for k, value in zip(MID, held[len(EARLY) :]):
+        arrived[k] = lax.ppermute(value, "sec", [(i, i ^ k) for i in range(nsec)])
+    both = double(held[-1])
+    order = receive_order(table, both, nsec, sdev)
+    pairs = [[i, i ^ LAST] for i in range(nsec) if i < i ^ LAST]
+    final = lax.all_to_all(both, "sec", 0, 0, axis_index_groups=pairs, tiled=True)
 
     def across(value, m):
         return lax.ppermute(value, "mpo", [(i, i ^ m) for i in range(nmpo)])
 
     staged = early(order, ops, [arrived[k] for k in EARLY], left_env, right_env, nsec, nmpo)
-    keep, far_give, near_give = late(order, ops, [arrived[k] for k in LATE], staged, nsec, wdev, sdev)
-    far = across(pair(keep, across(far_give, 1)), 2)
-    out = finish(keep, across(near_give, 1), far)
+    keep, far_give, near_give = mid(order, ops, [arrived[k] for k in MID], staged, wdev, sdev)
+    summed = pair(keep, across(far_give, 1))
+    far = across(summed, 2)
+    near = across(near_give, 1)
+    own, give1, give2, give3 = last(summed, final, staged, wdev)
+    total = base(keep, near, far, own, across(give1, 1))
+    out = finish(total, across(give2, 2), across(give3, 3))
     return jnp.transpose(out, (0, 2, 1, 3))
 
 

time: 32.5 us -> 29.1 us (0.90)
  the two profiles are of different devices: /device:TPU:18 before, /device:TPU:17 now
where the time goes in v5:
time: 29.1 us; the launch traced here: 28.9 us
  starting transfers between devices  11.6 us (40%)
  waiting for transfers between devices  9.2 us (32%)
  Pallas kernels  7.66 us (26%)
    ppermute x6, starting transfers between devices, across(): return lax.ppermute(value, 'mpo', [(i, i ^ m) for i in range(nmpo)])  5.31 us
    all_to_all x1, waiting for transfers between devices, fast_shards(): lax.all_to_all(both, 'sec', 0, 0, axis_index_groups=pairs, tiled=True)  5.03 us
    all_to_all x1, starting transfers between devices, fast_shards(): lax.all_to_all(both, 'sec', 0, 0, axis_index_groups=pairs, tiled=True)  4.87 us
    ppermute x6, waiting for transfers between devices, across(): return lax.ppermute(value, 'mpo', [(i, i ^ m) for i in range(nmpo)])  4.16 us
    pallas_call x1, Pallas kernels, receive_order(): pl.pallas_call(functools.partial(order_kernel, nsec, sdev), out_shape=jax...  1.49 us
    ppermute x2, starting transfers between devices, fast_shards(): arrived[k] = lax.ppermute(value, 'sec', [(i, i ^ k) for i in range(nsec)])  1.43 us
    pallas_call x1, Pallas kernels, route(): pl.pallas_call(functools.partial(route_kernel, classes), out_shape=[jax.S...  1.34 us
    pallas_call x1, Pallas kernels, early(): pl.pallas_call(functools.partial(early_kernel, nsec, nmpo), out_shape=[ke...  1.27 us
  transfers between devices with their start and end apart: 9, of which 4 were waited for; matrix products, arithmetic and copies ran while one was open for 1% of the time, Pallas kernels for 19%

profile of v5, /device:TPU:17, one launch (start us, length us, event | category | flops | bytes accessed | tf_op | source)
XLA Modules:
  0.0 28.9 jit_solution(16428896235510939109)
XLA Ops:
  0.0 1.3 %route.1 = (bf16[2,3,128,128]{3,2,1,0:T(8,128)(2,1)S(1)}, bf16[2,3,128,128]{3,2,1,0:T(8,128)(2,1)S(1)}, bf16[2,3,128,128]{3,2,1,0:T(8,128)(2,1)S(1)}, bf16[2,3,128,128]{3,2,1,0:T(8,128)(2,1)S(1)}) custom-call(s32[1,32]{1,0:T(1,128)} %source.3, bf16[8,3,128,128]{3,2,1,0:T(8,128)(2,1)} %bitcast.2), custom_call_target="tpu_custom_call" | custom-call | tf_op jit(solution)/shard_map/route/pallas_call | solution.py:71
  1.3 0.1 collective-permute-start
  1.4 1.4 %collective-permute-start.1 = (bf16[2,3,128,128]{3,2,1,0:T(8,128)(2,1)S(1)}, bf16[2,3,128,128]{3,2,1,0:T(8,128)(2,1)S(1)}, u32[]{:S(2)}, u32[]{:S(2)}) collective-permute-start(bf16[2,3,128,128]{3,2,1,0:T(8,128)(2,1)S(1)} %get-tuple-element.25), channel_id=1, source_target_pairs={{0,4},{4,0},{8,12},{12,8},{1,5},{5,1},{9,13},{13,9},{2,6},{6,2},{1... | collective-permute-start | bytes 589832 | tf_op jit(solution)/shard_map/ppermute | solution.py:419
  2.8 0.8 %double.1.after = bf16[2,2,3,128,128]{4,3,2,1,0:T(8,128)(2,1)} custom-call(bf16[2,3,128,128]{3,2,1,0:T(8,128)(2,1)S(1)} %get-tuple-element.23.block), custom_call_target="tpu_custom_call" | custom-call | tf_op jit(solution)/shard_map/double/pallas_call | solution.py:96
  3.6 0.0 copy-start
  3.6 0.0 copy-start.1
  3.6 4.9 %all-to-all-start = ((bf16[2,2,3,128,128]{4,3,2,1,0:T(8,128)(2,1)}), bf16[2,2,3,128,128]{4,3,2,1,0:T(8,128)(2,1)S(1)}, u32[]{:S(2)}, u32[]{:S(2)}) async-start(bf16[2,2,3,128,128]{4,3,2,1,0:T(8,128)(2,1)} %double.1.after), calls=%async_computation | async-start | bytes 786432 | tf_op jit(solution)/shard_map/all_to_all | solution.py:423
  8.5 0.0 copy-start.2
  8.5 1.5 %order.1.order_in = s32[8]{0:T(128)S(1)} custom-call(s32[1,32]{1,0:T(1,128)} %source.3, bf16[2,2,3,128,128]{4,3,2,1,0:T(8,128)(2,1)} %double.1.after), custom_call_target="tpu_custom_call" | custom-call | tf_op jit(solution)/shard_map/order/pallas_call | solution.py:119
  10.0 0.0 copy-done.2
  10.0 0.1 copy.6
  10.1 0.1 reshape.8.ops.ops_in
  10.2 0.0 copy-done
  10.2 0.0 copy-done.1
  10.2 1.3 %early.1 = (f32[2,2,3,32,128]{4,3,2,1,0:T(8,128)S(1)}, bf16[2,3,32,128]{3,2,1,0:T(8,128)(2,1)S(1)}, bf16[2,3,32,128]{3,2,1,0:T(8,128)(2,1)S(1)}, bf16[6,256,128]...) custom-call(s32[8]{0:T(128)S(1)} %order.1.order_in, ...), custom_call_target="tpu_custom_call" | custom-call | flops 100663296 | bytes 8388608 | tf_op jit(solution)/shard_map/early/pallas_call | solution.py:222
  11.5 0.0 collective-permute-done.refs_0_
  11.5 0.0 collective-permute-done.1.refs_1_
  11.5 1.1 %mid.1 = (f32[2,8,3,32,128]{4,3,2,1,0:T(8,128)S(1)}, bf16[8,3,32,128]{3,2,1,0:T(8,128)(2,1)S(1)}, bf16[8,3,32,128]{3,2,1,0:T(8,128)(2,1)S(1)}) custom-call(s32[8]{0:T(128)S(1)} %order.1.order_in, f32[144]{0:T(256)S(1)} %reshape.8.ops.ops_in, bf16[2,3,128,128]{3,2,1,0:T(8,128)(2,1)S(1)} %collective-permute-done.refs_0_, ...), custom_call_target="tpu_custom_call" | custom-call | flops 201326592 | bytes 8388608 | tf_op jit(solution)/shard_map/mid/pallas_call | solution.py:285
  12.7 1.7 %collective-permute-start.3 = (bf16[8,3,32,128]{3,2,1,0:T(8,128)(2,1)S(1)}, bf16[8,3,32,128]{3,2,1,0:T(8,128)(2,1)S(1)}, u32[]{:S(2)}, u32[]{:S(2)}) collective-permute-start(bf16[8,3,32,128]{3,2,1,0:T(8,128)(2,1)S(1)} %get-tuple-element.34), channel_id=1, source_target_pairs={{0,1},{1,0},{2,3},{3,2},{4,5},{5,4},{6,7},{7,6},{8,9},{9,8},{10,11... | collective-permute-start | bytes 589832 | tf_op jit(solution)/shard_map/ppermute | solution.py:426
  14.4 0.1 collective-permute-start.2
  14.4 1.0 %collective-permute-done.3.got = bf16[8,3,32,128]{3,2,1,0:T(8,128)(2,1)S(1)} collective-permute-done((bf16[8,3,32,128]{3,2,1,0:T(8,128)(2,1)S(1)}, bf16[8,3,32,128]{3,2,1,0:T(8,128)(2,1)S(1)}, u32[]{:S(2)}, u32[]{:S(2)}) %collective-permute-start.3) | collective-permute-done | bytes 196640 | tf_op jit(solution)/shard_map/ppermute | solution.py:426
  15.5 1.3 %collective-permute-start.4 = (bf16[8,3,32,128]{3,2,1,0:T(8,128)(2,1)S(1)}, bf16[8,3,32,128]{3,2,1,0:T(8,128)(2,1)S(1)}, u32[]{:S(2)}, u32[]{:S(2)}) collective-permute-start(bf16[8,3,32,128]{3,2,1,0:T(8,128)(2,1)S(1)} %pair.1.after), channel_id=1, source_target_pairs={{0,2},{1,3},{2,0},{3,1},{4,6},{5,7},{6,4},{7,5},{8,10},{9,11},{10,... | collective-permute-start | bytes 589832 | tf_op jit(solution)/shard_map/ppermute | solution.py:426
  16.7 5.0 %all-to-all-done.block = bf16[2,2,3,128,128]{4,3,2,1,0:T(8,128)(2,1)S(1)} async-done(((bf16[2,2,3,128,128]{4,3,2,1,0:T(8,128)(2,1)}), bf16[2,2,3,128,128]{4,3,2,1,0:T(8,128)(2,1)S(1)}, u32[]{:S(2)}, u32[]{:S(2)}) %all-to-all-start) | async-done | bytes 393248 | tf_op jit(solution)/shard_map/all_to_all | solution.py:423
  21.8 0.5 %last.1 = (f32[2,112,128]{2,1,0:T(8,128)S(1)}, bf16[2,112,128]{2,1,0:T(8,128)(2,1)S(1)}, bf16[2,112,128]{2,1,0:T(8,128)(2,1)S(1)}, bf16[2,112,128]{2,1,0:T(8,128)(2,1)S(1)}) custom-call(bf16[8,3,32,128]{3,2,1,0:T(8,128)(2,1)S(1)} %pair.1.after, bf16[2,2,3,128,128]{4,3,2,1,0:T(8,128)(2,1)S(1)} %all-to-all-done.block, ...), custom_call_target="tpu_custom_call" | custom-call | flops 100663296 | bytes 4194304 | tf_op jit(solution)/shard_map/last/pallas_call | solution.py:327
  22.3 0.6 %collective-permute-start.5 = (bf16[2,112,128]{2,1,0:T(8,128)(2,1)S(1)}, bf16[2,112,128]{2,1,0:T(8,128)(2,1)S(1)}, u32[]{:S(2)}, u32[]{:S(2)}) collective-permute-start(bf16[2,112,128]{2,1,0:T(8,128)(2,1)S(1)} %get-tuple-element.38), channel_id=1, source_target_pairs={{0,1},{1,0},{2,3},{3,2},{4,5},{5,4},{6,7},{7,6},{8,9},{9,8},{10,11... | collective-permute-start | bytes 172040 | tf_op jit(solution)/shard_map/ppermute | solution.py:426
  22.8 1.2 %collective-permute-start.6 = (bf16[2,112,128]{2,1,0:T(8,128)(2,1)S(1)}, bf16[2,112,128]{2,1,0:T(8,128)(2,1)S(1)}, u32[]{:S(2)}, u32[]{:S(2)}) collective-permute-start(bf16[2,112,128]{2,1,0:T(8,128)(2,1)S(1)} %get-tuple-element.39), channel_id=1, source_target_pairs={{0,2},{1,3},{2,0},{3,1},{4,6},{5,7},{6,4},{7,5},{8,10},{9,11},{10,... | collective-permute-start | bytes 172040 | tf_op jit(solution)/shard_map/ppermute | solution.py:426
  24.1 0.5 %collective-permute-start.7 = (bf16[2,112,128]{2,1,0:T(8,128)(2,1)S(1)}, bf16[2,112,128]{2,1,0:T(8,128)(2,1)S(1)}, u32[]{:S(2)}, u32[]{:S(2)}) collective-permute-start(bf16[2,112,128]{2,1,0:T(8,128)(2,1)S(1)} %get-tuple-element.40), channel_id=1, source_target_pairs={{0,3},{1,2},{2,1},{3,0},{4,7},{5,6},{6,5},{7,4},{8,11},{9,10},{10,... | collective-permute-start | bytes 172040 | tf_op jit(solution)/shard_map/ppermute | solution.py:426
  24.6 0.0 collective-permute-done.2.near
  24.6 0.0 collective-permute-done.5.mate
  24.6 0.0 collective-permute-done.4.far
  24.6 0.2 base.1.total
  24.8 1.6 %collective-permute-done.6.tail2 = bf16[2,112,128]{2,1,0:T(8,128)(2,1)S(1)} collective-permute-done((bf16[2,112,128]{2,1,0:T(8,128)(2,1)S(1)}, bf16[2,112,128]{2,1,0:T(8,128)(2,1)S(1)}, u32[]{:S(2)}, u32[]{:S(2)}) %collective-permute-start.6) | collective-permute-done | bytes 57376 | tf_op jit(solution)/shard_map/ppermute | solution.py:426
  26.3 1.6 %collective-permute-done.7.tail3 = bf16[2,112,128]{2,1,0:T(8,128)(2,1)S(1)} collective-permute-done((bf16[2,112,128]{2,1,0:T(8,128)(2,1)S(1)}, bf16[2,112,128]{2,1,0:T(8,128)(2,1)S(1)}, u32[]{:S(2)}, u32[]{:S(2)}) %collective-permute-start.7) | collective-permute-done | bytes 57376 | tf_op jit(solution)/shard_map/ppermute | solution.py:426
  27.9 0.9 %finish.1 = bf16[32,3,8,128]{3,2,1,0:T(8,128)(2,1)} custom-call(f32[8,3,32,128]{3,2,1,0:T(8,128)S(1)} %base.1.total, bf16[2,112,128]{2,1,0:T(8,128)(2,1)S(1)} %collective-permute-done.6.tail2, bf16[2,112,128]{2,1,0:T(8,128)(2,1)S(1)} %collective-permute-done.7.tail3), custom_call_target="tpu_custom_call" | custom-call | tf_op jit(solution)/shard_map/finish/pallas_call | solution.py:396
  (1 shorter events, 0.0 us)
Async XLA Ops:
  1.3 10.2 %collective-permute-start = (bf16[2,3,128,128]{3,2,1,0:T(8,128)(2,1)S(1)}, bf16[2,3,128,128]{3,2,1,0:T(8,128)(2,1)S(1)}, u32[]{:S(2)}, u32[]{:S(2)}) collective-permute-start(bf16[2,3,128,128]{3,2,1,0:T(8,128)(2,1)S(1)} %get-tuple-element.24), channel_id=1, source_target_pairs={{0,8},{4,12},{8,0},{12,4},{1,9},{5,13},{9,1},{13,5},{2,10},{6,14},... | collective-permute-start | bytes 589832 | tf_op jit(solution)/shard_map/ppermute | solution.py:419
  1.4 10.1 %collective-permute-start.1 = (bf16[2,3,128,128]{3,2,1,0:T(8,128)(2,1)S(1)}, bf16[2,3,128,128]{3,2,1,0:T(8,128)(2,1)S(1)}, u32[]{:S(2)}, u32[]{:S(2)}) collective-permute-start(bf16[2,3,128,128]{3,2,1,0:T(8,128)(2,1)S(1)} %get-tuple-element.25), channel_id=1, source_target_pairs={{0,4},{4,0},{8,12},{12,8},{1,5},{5,1},{9,13},{13,9},{2,6},{6,2},{1... | collective-permute-start | bytes 589832 | tf_op jit(solution)/shard_map/ppermute | solution.py:419
  3.6 6.7 %copy-start = (bf16[2,8,128,128]{3,2,1,0:T(8,128)(2,1)S(1)}, bf16[2,8,128,128]{3,2,1,0:T(8,128)(2,1)}, u32[]{:S(2)}) copy-start(bf16[2,8,128,128]{3,2,1,0:T(8,128)(2,1)} %refs_1_.1) | copy-start | bytes 1572868
  3.6 6.7 %copy-start.1 = (bf16[2,8,128,128]{3,2,1,0:T(8,128)(2,1)S(1)}, bf16[2,8,128,128]{3,2,1,0:T(8,128)(2,1)}, u32[]{:S(2)}) copy-start(bf16[2,8,128,128]{3,2,1,0:T(8,128)(2,1)} %refs_2_.1) | copy-start | bytes 1572868
  3.6 18.2 %all-to-all-start = ((bf16[2,2,3,128,128]{4,3,2,1,0:T(8,128)(2,1)}), bf16[2,2,3,128,128]{4,3,2,1,0:T(8,128)(2,1)S(1)}, u32[]{:S(2)}, u32[]{:S(2)}) async-start(bf16[2,2,3,128,128]{4,3,2,1,0:T(8,128)(2,1)} %double.1.after), calls=%async_computation | async-start | bytes 786432 | tf_op jit(solution)/shard_map/all_to_all | solution.py:423
  8.5 1.5 %copy-start.2 = (bf16[2,8,3,3]{1,0,3,2:T(2,128)(2,1)S(1)}, bf16[2,8,3,3]{1,0,3,2:T(2,128)(2,1)}, u32[]{:S(2)}) copy-start(bf16[2,8,3,3]{1,0,3,2:T(2,128)(2,1)} %param.8) | copy-start | bytes 868
  12.7 2.8 %collective-permute-start.3 = (bf16[8,3,32,128]{3,2,1,0:T(8,128)(2,1)S(1)}, bf16[8,3,32,128]{3,2,1,0:T(8,128)(2,1)S(1)}, u32[]{:S(2)}, u32[]{:S(2)}) collective-permute-start(bf16[8,3,32,128]{3,2,1,0:T(8,128)(2,1)S(1)} %get-tuple-element.34), channel_id=1, source_target_pairs={{0,1},{1,0},{2,3},{3,2},{4,5},{5,4},{6,7},{7,6},{8,9},{9,8},{10,11... | collective-permute-start | bytes 589832 | tf_op jit(solution)/shard_map/ppermute | solution.py:426
  14.4 10.2 %collective-permute-start.2 = (bf16[8,3,32,128]{3,2,1,0:T(8,128)(2,1)S(1)}, bf16[8,3,32,128]{3,2,1,0:T(8,128)(2,1)S(1)}, u32[]{:S(2)}, u32[]{:S(2)}) collective-permute-start(bf16[8,3,32,128]{3,2,1,0:T(8,128)(2,1)S(1)} %get-tuple-element.33), channel_id=1, source_target_pairs={{0,1},{1,0},{2,3},{3,2},{4,5},{5,4},{6,7},{7,6},{8,9},{9,8},{10,11... | collective-permute-start | bytes 589832 | tf_op jit(solution)/shard_map/ppermute | solution.py:426
  15.5 9.1 %collective-permute-start.4 = (bf16[8,3,32,128]{3,2,1,0:T(8,128)(2,1)S(1)}, bf16[8,3,32,128]{3,2,1,0:T(8,128)(2,1)S(1)}, u32[]{:S(2)}, u32[]{:S(2)}) collective-permute-start(bf16[8,3,32,128]{3,2,1,0:T(8,128)(2,1)S(1)} %pair.1.after), channel_id=1, source_target_pairs={{0,2},{1,3},{2,0},{3,1},{4,6},{5,7},{6,4},{7,5},{8,10},{9,11},{10,... | collective-permute-start | bytes 589832 | tf_op jit(solution)/shard_map/ppermute | solution.py:426
  22.3 2.3 %collective-permute-start.5 = (bf16[2,112,128]{2,1,0:T(8,128)(2,1)S(1)}, bf16[2,112,128]{2,1,0:T(8,128)(2,1)S(1)}, u32[]{:S(2)}, u32[]{:S(2)}) collective-permute-start(bf16[2,112,128]{2,1,0:T(8,128)(2,1)S(1)} %get-tuple-element.38), channel_id=1, source_target_pairs={{0,1},{1,0},{2,3},{3,2},{4,5},{5,4},{6,7},{7,6},{8,9},{9,8},{10,11... | collective-permute-start | bytes 172040 | tf_op jit(solution)/shard_map/ppermute | solution.py:426
  22.8 3.5 %collective-permute-start.6 = (bf16[2,112,128]{2,1,0:T(8,128)(2,1)S(1)}, bf16[2,112,128]{2,1,0:T(8,128)(2,1)S(1)}, u32[]{:S(2)}, u32[]{:S(2)}) collective-permute-start(bf16[2,112,128]{2,1,0:T(8,128)(2,1)S(1)} %get-tuple-element.39), channel_id=1, source_target_pairs={{0,2},{1,3},{2,0},{3,1},{4,6},{5,7},{6,4},{7,5},{8,10},{9,11},{10,... | collective-permute-start | bytes 172040 | tf_op jit(solution)/shard_map/ppermute | solution.py:426
  24.1 3.9 %collective-permute-start.7 = (bf16[2,112,128]{2,1,0:T(8,128)(2,1)S(1)}, bf16[2,112,128]{2,1,0:T(8,128)(2,1)S(1)}, u32[]{:S(2)}, u32[]{:S(2)}) collective-permute-start(bf16[2,112,128]{2,1,0:T(8,128)(2,1)S(1)} %get-tuple-element.40), channel_id=1, source_target_pairs={{0,3},{1,2},{2,1},{3,0},{4,7},{5,6},{6,5},{7,4},{8,11},{9,10},{10,... | collective-permute-start | bytes 172040 | tf_op jit(solution)/shard_map/ppermute | solution.py:426

commit v6 on v5

--- a/solution.py
+++ b/solution.py
@@ -185,15 +185,18 @@
         t = order[LATE[s // SLOTS] * SLOTS + s % SLOTS]
         lstage[s] = side(t)
         rstage[s] = right[:, t].reshape(wdev * blk, blk)
+    line = lax.broadcasted_iota(jnp.int32, named.shape, 0)
+    names = jnp.zeros(named.shape, jnp.float32)
     for s in range(SLOTS):
         t = order[LAST * SLOTS + s]
-        named[s] = jnp.full(named.shape[1:], t.astype(jnp.float32), jnp.float32).astype(named.dtype)
+        names = jnp.where(line == s, t.astype(jnp.float32), names)
         op = scalar_op(ops, t, sdev, phys)
         for w in range(wdev):
             for p in range(phys):
                 for q in range(phys):
                     i = (w * phys + p) * phys + q
                     oprows[s, i : i + 1, :] = jnp.full((1, blk), op(w, p, q), jnp.float32)
+    named[...] = names.astype(named.dtype)
     for i, k in enumerate(EARLY):
         for j in range(SLOTS):
             s = i * SLOTS + j
@@ -217,7 +220,7 @@
     keep = jax.ShapeDtypeStruct((2, n, phys, part, blk), jnp.float32)
     give = jax.ShapeDtypeStruct((n, phys, part, blk), jnp.bfloat16)
     rows = jax.ShapeDtypeStruct((SLOTS, wdev * phys * phys, blk), jnp.float32)
-    name = jax.ShapeDtypeStruct((SLOTS, NAME_ROWS, blk), jnp.bfloat16)
+    name = jax.ShapeDtypeStruct((NAME_ROWS, blk), jnp.bfloat16)
     whole = jax.ShapeDtypeStruct((late_n, wdev * blk, blk), jnp.bfloat16)
     return pl.pallas_call(
         functools.partial(early_kernel, nsec, nmpo),
@@ -305,6 +308,7 @@
 def last_kernel(wdev, after, block, lstage, rstage, oprows, named, *gives):
     phys, blk = block.shape[2], block.shape[4]
     part = blk // len(gives)
+    size = phys * part
     first = len(MID) * SLOTS
     me = lax.axis_index("sec")
     other = (jnp.bitwise_xor(me, LAST) > me).astype(jnp.int32)
@@ -316,13 +320,15 @@
         for i, m in enumerate(QUARTERS):
             for q in range(phys):
                 rows = outs[q][i * part : (i + 1) * part].astype(gives[m].dtype)
-                gives[m][s, q * part : (q + 1) * part] = rows
-            gives[m][s, phys * part :] = named[s].astype(gives[m].dtype)
+                at = s * size + q * part
+                gives[m][at : at + part] = rows
+    for give in gives:
+        give[SLOTS * size :] = named[...].astype(give.dtype)
 
 
 def last(after, block, staged, wdev):
     phys, part, blk = staged[0].shape[2:]
-    shape = (SLOTS, phys * part + NAME_ROWS, blk)
+    shape = (SLOTS * phys * part + NAME_ROWS, blk)
     give = jax.ShapeDtypeStruct(shape, jnp.bfloat16)
     return pl.pallas_call(
         functools.partial(last_kernel, wdev),
@@ -354,22 +360,25 @@
     )(keep, got)
 
 
-def tail_sum(tails, t):
+def tail_sum(tails, t, first, count):
     total = None
     for tail in tails:
-        rows = tail.shape[1] - NAME_ROWS
+        end = tail.shape[0] - NAME_ROWS
+        size = end // SLOTS
+        names = tail[end:, :].astype(jnp.float32)
         for s in range(SLOTS):
-            here = tail[s, rows:, :].astype(jnp.float32)[:1] == t
-            value = jnp.where(here, tail[s, :rows, :].astype(jnp.float32), 0.0)
+            at = s * size + first
+            rows = tail[at : at + count, :].astype(jnp.float32)
+            value = jnp.where(names[s : s + 1] == t, rows, 0.0)
             total = value if total is None else total + value
     return total
 
 
 def base_kernel(keep, near, far, own, mate, acc):
-    phys, part, blk = acc.shape[1:]
-    for t in range(acc.shape[0]):
+    sdev, phys, part, blk = acc.shape
+    for t in range(sdev):
         total = keep[1, t] + near[t].astype(jnp.float32) + far[t].astype(jnp.float32)
-        acc[t] = total + tail_sum((own, mate), t).reshape(phys, part, blk)
+        acc[t] = total + tail_sum((own, mate), t, 0, phys * part).reshape(phys, part, blk)
 
 
 def base(keep, near, far, own, mate):
@@ -383,12 +392,18 @@
     )(keep, near, far, own, mate)
 
 
-def finish_kernel(total, tail2, tail3, out, acc):
-    sdev, phys, part, blk = acc.shape
-    for t in range(sdev):
-        acc[t] = total[t] + tail_sum((tail2, tail3), t).reshape(phys, part, blk)
+def finish_kernel(total, tail2, tail3, out, acc, turned, sems):
+    sdev, phys, part, blk = total.shape
+    copies = []
     for q in range(phys):
-        out[:, q] = jnp.swapaxes(acc[:, q], 0, 1).astype(out.dtype)
+        for t in range(sdev):
+            acc[q, t] = total[t, q] + tail_sum((tail2, tail3), t, q * part, part)
+        turned[q] = jnp.swapaxes(acc[q], 0, 1).astype(turned.dtype)
+        copy = pltpu.make_async_copy(turned.at[q], out.at[:, q], sems.at[q])
+        copy.start()
+        copies.append(copy)
+    for copy in copies:
+        copy.wait()
 
 
 def finish(total, tail2, tail3):
@@ -397,8 +412,12 @@
         finish_kernel,
         out_shape=jax.ShapeDtypeStruct((part, phys, sdev, blk), jnp.bfloat16),
         in_specs=[space(pltpu.VMEM)] * 3,
-        out_specs=space(pltpu.VMEM),
-        scratch_shapes=[pltpu.VMEM(total.shape, total.dtype)],
+        out_specs=space(pl.ANY),
+        scratch_shapes=[
+            pltpu.VMEM((phys, sdev, part, blk), jnp.float32),
+            pltpu.VMEM((phys, part, sdev, blk), jnp.bfloat16),
+            pltpu.SemaphoreType.DMA((phys,)),
+        ],
         compiler_params=params(),
         name="finish",
     )(total, tail2, tail3)

time: 29.1 us -> 29 us (level)
  no operation moved by 1% of the time
where the time goes in v6:
time: 29 us; the launch traced here: 28.8 us
  starting transfers between devices  11.6 us (40%)
  waiting for transfers between devices  9.12 us (31%)
  Pallas kernels  7.65 us (26%)
    ppermute x6, starting transfers between devices, across(): return lax.ppermute(value, 'mpo', [(i, i ^ m) for i in range(nmpo)])  5.31 us
    all_to_all x1, waiting for transfers between devices, fast_shards(): lax.all_to_all(both, 'sec', 0, 0, axis_index_groups=pairs, tiled=True)  5.03 us
    all_to_all x1, starting transfers between devices, fast_shards(): lax.all_to_all(both, 'sec', 0, 0, axis_index_groups=pairs, tiled=True)  4.87 us
    ppermute x6, waiting for transfers between devices, across(): return lax.ppermute(value, 'mpo', [(i, i ^ m) for i in range(nmpo)])  4.09 us
    pallas_call x1, Pallas kernels, receive_order(): pl.pallas_call(functools.partial(order_kernel, nsec, sdev), out_shape=jax...  1.49 us
    ppermute x2, starting transfers between devices, fast_shards(): arrived[k] = lax.ppermute(value, 'sec', [(i, i ^ k) for i in range(nsec)])  1.43 us
    pallas_call x1, Pallas kernels, route(): pl.pallas_call(functools.partial(route_kernel, classes), out_shape=[jax.S...  1.34 us
    pallas_call x1, Pallas kernels, early(): pl.pallas_call(functools.partial(early_kernel, nsec, nmpo), out_shape=[ke...  1.27 us
  transfers between devices with their start and end apart: 9, of which 4 were waited for; matrix products, arithmetic and copies ran while one was open for 1% of the time, Pallas kernels for 19%

profile of v6, /device:TPU:17, one launch (start us, length us, event | category | flops | bytes accessed | tf_op | source)
XLA Modules:
  0.0 28.8 jit_solution(12355567788240340425)
XLA Ops:
  0.0 1.3 %route.1 = (bf16[2,3,128,128]{3,2,1,0:T(8,128)(2,1)S(1)}, bf16[2,3,128,128]{3,2,1,0:T(8,128)(2,1)S(1)}, bf16[2,3,128,128]{3,2,1,0:T(8,128)(2,1)S(1)}, bf16[2,3,128,128]{3,2,1,0:T(8,128)(2,1)S(1)}) custom-call(s32[1,32]{1,0:T(1,128)} %source.3, bf16[8,3,128,128]{3,2,1,0:T(8,128)(2,1)} %bitcast.2), custom_call_target="tpu_custom_call" | custom-call | tf_op jit(solution)/shard_map/route/pallas_call | solution.py:71
  1.3 0.1 collective-permute-start
  1.4 1.4 %collective-permute-start.1 = (bf16[2,3,128,128]{3,2,1,0:T(8,128)(2,1)S(1)}, bf16[2,3,128,128]{3,2,1,0:T(8,128)(2,1)S(1)}, u32[]{:S(2)}, u32[]{:S(2)}) collective-permute-start(bf16[2,3,128,128]{3,2,1,0:T(8,128)(2,1)S(1)} %get-tuple-element.25), channel_id=1, source_target_pairs={{0,4},{4,0},{8,12},{12,8},{1,5},{5,1},{9,13},{13,9},{2,6},{6,2},{1... | collective-permute-start | bytes 589832 | tf_op jit(solution)/shard_map/ppermute | solution.py:438
  2.8 0.8 %double.1.after = bf16[2,2,3,128,128]{4,3,2,1,0:T(8,128)(2,1)} custom-call(bf16[2,3,128,128]{3,2,1,0:T(8,128)(2,1)S(1)} %get-tuple-element.23.block), custom_call_target="tpu_custom_call" | custom-call | tf_op jit(solution)/shard_map/double/pallas_call | solution.py:96
  3.6 0.0 copy-start
  3.6 0.0 copy-start.1
  3.6 4.9 %all-to-all-start = ((bf16[2,2,3,128,128]{4,3,2,1,0:T(8,128)(2,1)}), bf16[2,2,3,128,128]{4,3,2,1,0:T(8,128)(2,1)S(1)}, u32[]{:S(2)}, u32[]{:S(2)}) async-start(bf16[2,2,3,128,128]{4,3,2,1,0:T(8,128)(2,1)} %double.1.after), calls=%async_computation | async-start | bytes 786432 | tf_op jit(solution)/shard_map/all_to_all | solution.py:442
  8.5 0.0 copy-start.2
  8.5 1.5 %order.1.order_in = s32[8]{0:T(128)S(1)} custom-call(s32[1,32]{1,0:T(1,128)} %source.3, bf16[2,2,3,128,128]{4,3,2,1,0:T(8,128)(2,1)} %double.1.after), custom_call_target="tpu_custom_call" | custom-call | tf_op jit(solution)/shard_map/order/pallas_call | solution.py:119
  10.0 0.0 copy-done.2
  10.0 0.1 copy.6
  10.1 0.1 reshape.8.ops.ops_in
  10.2 0.0 copy-done
  10.2 0.0 copy-done.1
  10.2 1.3 %early.1 = (f32[2,2,3,32,128]{4,3,2,1,0:T(8,128)S(1)}, bf16[2,3,32,128]{3,2,1,0:T(8,128)(2,1)S(1)}, bf16[2,3,32,128]{3,2,1,0:T(8,128)(2,1)S(1)}, bf16[6,256,128]...) custom-call(s32[8]{0:T(128)S(1)} %order.1.order_in, ...), custom_call_target="tpu_custom_call" | custom-call | flops 100663296 | bytes 8388608 | tf_op jit(solution)/shard_map/early/pallas_call | solution.py:225
  11.5 0.0 collective-permute-done.refs_0_
  11.5 0.0 collective-permute-done.1.refs_1_
  11.5 1.1 %mid.1 = (f32[2,8,3,32,128]{4,3,2,1,0:T(8,128)S(1)}, bf16[8,3,32,128]{3,2,1,0:T(8,128)(2,1)S(1)}, bf16[8,3,32,128]{3,2,1,0:T(8,128)(2,1)S(1)}) custom-call(s32[8]{0:T(128)S(1)} %order.1.order_in, f32[144]{0:T(256)S(1)} %reshape.8.ops.ops_in, bf16[2,3,128,128]{3,2,1,0:T(8,128)(2,1)S(1)} %collective-permute-done.refs_0_, ...), custom_call_target="tpu_custom_call" | custom-call | flops 201326592 | bytes 8388608 | tf_op jit(solution)/shard_map/mid/pallas_call | solution.py:288
  12.7 1.7 %collective-permute-start.3 = (bf16[8,3,32,128]{3,2,1,0:T(8,128)(2,1)S(1)}, bf16[8,3,32,128]{3,2,1,0:T(8,128)(2,1)S(1)}, u32[]{:S(2)}, u32[]{:S(2)}) collective-permute-start(bf16[8,3,32,128]{3,2,1,0:T(8,128)(2,1)S(1)} %get-tuple-element.34), channel_id=1, source_target_pairs={{0,1},{1,0},{2,3},{3,2},{4,5},{5,4},{6,7},{7,6},{8,9},{9,8},{10,11... | collective-permute-start | bytes 589832 | tf_op jit(solution)/shard_map/ppermute | solution.py:445
  14.4 0.1 collective-permute-start.2
  14.4 1.0 %collective-permute-done.3.got = bf16[8,3,32,128]{3,2,1,0:T(8,128)(2,1)S(1)} collective-permute-done((bf16[8,3,32,128]{3,2,1,0:T(8,128)(2,1)S(1)}, bf16[8,3,32,128]{3,2,1,0:T(8,128)(2,1)S(1)}, u32[]{:S(2)}, u32[]{:S(2)}) %collective-permute-start.3) | collective-permute-done | bytes 196640 | tf_op jit(solution)/shard_map/ppermute | solution.py:445
  15.5 1.3 %collective-permute-start.4 = (bf16[8,3,32,128]{3,2,1,0:T(8,128)(2,1)S(1)}, bf16[8,3,32,128]{3,2,1,0:T(8,128)(2,1)S(1)}, u32[]{:S(2)}, u32[]{:S(2)}) collective-permute-start(bf16[8,3,32,128]{3,2,1,0:T(8,128)(2,1)S(1)} %pair.1.after), channel_id=1, source_target_pairs={{0,2},{1,3},{2,0},{3,1},{4,6},{5,7},{6,4},{7,5},{8,10},{9,11},{10,... | collective-permute-start | bytes 589832 | tf_op jit(solution)/shard_map/ppermute | solution.py:445
  16.7 5.0 %all-to-all-done.block = bf16[2,2,3,128,128]{4,3,2,1,0:T(8,128)(2,1)S(1)} async-done(((bf16[2,2,3,128,128]{4,3,2,1,0:T(8,128)(2,1)}), bf16[2,2,3,128,128]{4,3,2,1,0:T(8,128)(2,1)S(1)}, u32[]{:S(2)}, u32[]{:S(2)}) %all-to-all-start) | async-done | bytes 393248 | tf_op jit(solution)/shard_map/all_to_all | solution.py:442
  21.8 0.5 %last.1 = (f32[208,128]{1,0:T(8,128)S(1)}, bf16[208,128]{1,0:T(8,128)(2,1)S(1)}, bf16[208,128]{1,0:T(8,128)(2,1)S(1)}, bf16[208,128]{1,0:T(8,128)(2,1)S(1)}) custom-call(bf16[8,3,32,128]{3,2,1,0:T(8,128)(2,1)S(1)} %pair.1.after, bf16[2,2,3,128,128]{4,3,2,1,0:T(8,128)(2,1)S(1)} %all-to-all-done.block, ...), custom_call_target="tpu_custom_call" | custom-call | flops 100663296 | bytes 4194304 | tf_op jit(solution)/shard_map/last/pallas_call | solution.py:333
  22.3 0.6 %collective-permute-start.5 = (bf16[208,128]{1,0:T(8,128)(2,1)S(1)}, bf16[208,128]{1,0:T(8,128)(2,1)S(1)}, u32[]{:S(2)}, u32[]{:S(2)}) collective-permute-start(bf16[208,128]{1,0:T(8,128)(2,1)S(1)} %get-tuple-element.38), channel_id=1, source_target_pairs={{0,1},{1,0},{2,3},{3,2},{4,5},{5,4},{6,7},{7,6},{8,9},{9,8},{10,11... | collective-permute-start | bytes 159752 | tf_op jit(solution)/shard_map/ppermute | solution.py:445
  22.8 1.2 %collective-permute-start.6 = (bf16[208,128]{1,0:T(8,128)(2,1)S(1)}, bf16[208,128]{1,0:T(8,128)(2,1)S(1)}, u32[]{:S(2)}, u32[]{:S(2)}) collective-permute-start(bf16[208,128]{1,0:T(8,128)(2,1)S(1)} %get-tuple-element.39), channel_id=1, source_target_pairs={{0,2},{1,3},{2,0},{3,1},{4,6},{5,7},{6,4},{7,5},{8,10},{9,11},{10,... | collective-permute-start | bytes 159752 | tf_op jit(solution)/shard_map/ppermute | solution.py:445
  24.1 0.5 %collective-permute-start.7 = (bf16[208,128]{1,0:T(8,128)(2,1)S(1)}, bf16[208,128]{1,0:T(8,128)(2,1)S(1)}, u32[]{:S(2)}, u32[]{:S(2)}) collective-permute-start(bf16[208,128]{1,0:T(8,128)(2,1)S(1)} %get-tuple-element.40), channel_id=1, source_target_pairs={{0,3},{1,2},{2,1},{3,0},{4,7},{5,6},{6,5},{7,4},{8,11},{9,10},{10,... | collective-permute-start | bytes 159752 | tf_op jit(solution)/shard_map/ppermute | solution.py:445
  24.6 0.0 collective-permute-done.2.near
  24.6 0.0 collective-permute-done.5.mate
  24.6 0.0 collective-permute-done.4.far
  24.6 0.2 base.1.total
  24.8 1.5 %collective-permute-done.6.tail2 = bf16[208,128]{1,0:T(8,128)(2,1)S(1)} collective-permute-done((bf16[208,128]{1,0:T(8,128)(2,1)S(1)}, bf16[208,128]{1,0:T(8,128)(2,1)S(1)}, u32[]{:S(2)}, u32[]{:S(2)}) %collective-permute-start.6) | collective-permute-done | bytes 53280 | tf_op jit(solution)/shard_map/ppermute | solution.py:445
  26.3 1.6 %collective-permute-done.7.tail3 = bf16[208,128]{1,0:T(8,128)(2,1)S(1)} collective-permute-done((bf16[208,128]{1,0:T(8,128)(2,1)S(1)}, bf16[208,128]{1,0:T(8,128)(2,1)S(1)}, u32[]{:S(2)}, u32[]{:S(2)}) %collective-permute-start.7) | collective-permute-done | bytes 53280 | tf_op jit(solution)/shard_map/ppermute | solution.py:445
  27.9 0.9 %finish.1 = bf16[32,3,8,128]{3,2,1,0:T(8,128)(2,1)} custom-call(f32[8,3,32,128]{3,2,1,0:T(8,128)S(1)} %base.1.total, bf16[208,128]{1,0:T(8,128)(2,1)S(1)} %collective-permute-done.6.tail2, bf16[208,128]{1,0:T(8,128)(2,1)S(1)} %collective-permute-done.7.tail3), custom_call_target="tpu_custom_call" | custom-call | tf_op jit(solution)/shard_map/finish/pallas_call | solution.py:411
  (1 shorter events, 0.0 us)
Async XLA Ops:
  1.3 10.2 %collective-permute-start = (bf16[2,3,128,128]{3,2,1,0:T(8,128)(2,1)S(1)}, bf16[2,3,128,128]{3,2,1,0:T(8,128)(2,1)S(1)}, u32[]{:S(2)}, u32[]{:S(2)}) collective-permute-start(bf16[2,3,128,128]{3,2,1,0:T(8,128)(2,1)S(1)} %get-tuple-element.24), channel_id=1, source_target_pairs={{0,8},{4,12},{8,0},{12,4},{1,9},{5,13},{9,1},{13,5},{2,10},{6,14},... | collective-permute-start | bytes 589832 | tf_op jit(solution)/shard_map/ppermute | solution.py:438
  1.4 10.1 %collective-permute-start.1 = (bf16[2,3,128,128]{3,2,1,0:T(8,128)(2,1)S(1)}, bf16[2,3,128,128]{3,2,1,0:T(8,128)(2,1)S(1)}, u32[]{:S(2)}, u32[]{:S(2)}) collective-permute-start(bf16[2,3,128,128]{3,2,1,0:T(8,128)(2,1)S(1)} %get-tuple-element.25), channel_id=1, source_target_pairs={{0,4},{4,0},{8,12},{12,8},{1,5},{5,1},{9,13},{13,9},{2,6},{6,2},{1... | collective-permute-start | bytes 589832 | tf_op jit(solution)/shard_map/ppermute | solution.py:438
  3.6 6.7 %copy-start = (bf16[2,8,128,128]{3,2,1,0:T(8,128)(2,1)S(1)}, bf16[2,8,128,128]{3,2,1,0:T(8,128)(2,1)}, u32[]{:S(2)}) copy-start(bf16[2,8,128,128]{3,2,1,0:T(8,128)(2,1)} %refs_1_.1) | copy-start | bytes 1572868
  3.6 6.7 %copy-start.1 = (bf16[2,8,128,128]{3,2,1,0:T(8,128)(2,1)S(1)}, bf16[2,8,128,128]{3,2,1,0:T(8,128)(2,1)}, u32[]{:S(2)}) copy-start(bf16[2,8,128,128]{3,2,1,0:T(8,128)(2,1)} %refs_2_.1) | copy-start | bytes 1572868
  3.6 18.2 %all-to-all-start = ((bf16[2,2,3,128,128]{4,3,2,1,0:T(8,128)(2,1)}), bf16[2,2,3,128,128]{4,3,2,1,0:T(8,128)(2,1)S(1)}, u32[]{:S(2)}, u32[]{:S(2)}) async-start(bf16[2,2,3,128,128]{4,3,2,1,0:T(8,128)(2,1)} %double.1.after), calls=%async_computation | async-start | bytes 786432 | tf_op jit(solution)/shard_map/all_to_all | solution.py:442
  8.5 1.5 %copy-start.2 = (bf16[2,8,3,3]{1,0,3,2:T(2,128)(2,1)S(1)}, bf16[2,8,3,3]{1,0,3,2:T(2,128)(2,1)}, u32[]{:S(2)}) copy-start(bf16[2,8,3,3]{1,0,3,2:T(2,128)(2,1)} %param.8) | copy-start | bytes 868
  12.7 2.8 %collective-permute-start.3 = (bf16[8,3,32,128]{3,2,1,0:T(8,128)(2,1)S(1)}, bf16[8,3,32,128]{3,2,1,0:T(8,128)(2,1)S(1)}, u32[]{:S(2)}, u32[]{:S(2)}) collective-permute-start(bf16[8,3,32,128]{3,2,1,0:T(8,128)(2,1)S(1)} %get-tuple-element.34), channel_id=1, source_target_pairs={{0,1},{1,0},{2,3},{3,2},{4,5},{5,4},{6,7},{7,6},{8,9},{9,8},{10,11... | collective-permute-start | bytes 589832 | tf_op jit(solution)/shard_map/ppermute | solution.py:445
  14.4 10.2 %collective-permute-start.2 = (bf16[8,3,32,128]{3,2,1,0:T(8,128)(2,1)S(1)}, bf16[8,3,32,128]{3,2,1,0:T(8,128)(2,1)S(1)}, u32[]{:S(2)}, u32[]{:S(2)}) collective-permute-start(bf16[8,3,32,128]{3,2,1,0:T(8,128)(2,1)S(1)} %get-tuple-element.33), channel_id=1, source_target_pairs={{0,1},{1,0},{2,3},{3,2},{4,5},{5,4},{6,7},{7,6},{8,9},{9,8},{10,11... | collective-permute-start | bytes 589832 | tf_op jit(solution)/shard_map/ppermute | solution.py:445
  15.5 9.1 %collective-permute-start.4 = (bf16[8,3,32,128]{3,2,1,0:T(8,128)(2,1)S(1)}, bf16[8,3,32,128]{3,2,1,0:T(8,128)(2,1)S(1)}, u32[]{:S(2)}, u32[]{:S(2)}) collective-permute-start(bf16[8,3,32,128]{3,2,1,0:T(8,128)(2,1)S(1)} %pair.1.after), channel_id=1, source_target_pairs={{0,2},{1,3},{2,0},{3,1},{4,6},{5,7},{6,4},{7,5},{8,10},{9,11},{10,... | collective-permute-start | bytes 589832 | tf_op jit(solution)/shard_map/ppermute | solution.py:445
  22.3 2.3 %collective-permute-start.5 = (bf16[208,128]{1,0:T(8,128)(2,1)S(1)}, bf16[208,128]{1,0:T(8,128)(2,1)S(1)}, u32[]{:S(2)}, u32[]{:S(2)}) collective-permute-start(bf16[208,128]{1,0:T(8,128)(2,1)S(1)} %get-tuple-element.38), channel_id=1, source_target_pairs={{0,1},{1,0},{2,3},{3,2},{4,5},{5,4},{6,7},{7,6},{8,9},{9,8},{10,11... | collective-permute-start | bytes 159752 | tf_op jit(solution)/shard_map/ppermute | solution.py:445
  22.8 3.4 %collective-permute-start.6 = (bf16[208,128]{1,0:T(8,128)(2,1)S(1)}, bf16[208,128]{1,0:T(8,128)(2,1)S(1)}, u32[]{:S(2)}, u32[]{:S(2)}) collective-permute-start(bf16[208,128]{1,0:T(8,128)(2,1)S(1)} %get-tuple-element.39), channel_id=1, source_target_pairs={{0,2},{1,3},{2,0},{3,1},{4,6},{5,7},{6,4},{7,5},{8,10},{9,11},{10,... | collective-permute-start | bytes 159752 | tf_op jit(solution)/shard_map/ppermute | solution.py:445
  24.1 3.8 %collective-permute-start.7 = (bf16[208,128]{1,0:T(8,128)(2,1)S(1)}, bf16[208,128]{1,0:T(8,128)(2,1)S(1)}, u32[]{:S(2)}, u32[]{:S(2)}) collective-permute-start(bf16[208,128]{1,0:T(8,128)(2,1)S(1)} %get-tuple-element.40), channel_id=1, source_target_pairs={{0,3},{1,2},{2,1},{3,0},{4,7},{5,6},{6,5},{7,4},{8,11},{9,10},{10,... | collective-permute-start | bytes 159752 | tf_op jit(solution)/shard_map/ppermute | solution.py:445

commit v7 on v6

--- a/solution.py
+++ b/solution.py
@@ -53,10 +53,9 @@
     fetch = pltpu.make_async_copy(source, table, load)
     fetch.start()
     copies = []
-    for row in range(sdev):
-        copy = pltpu.make_async_copy(psi.at[row], held.at[row], sems.at[row])
-        copy.start()
-        copies.append(copy)
+    copy = pltpu.make_async_copy(psi, held, sems.at[0])
+    copy.start()
+    copies.append(copy)
     fetch.wait()
     rows = [pick(table, jnp.bitwise_xor(me, k) * sdev, sdev, me)[1] for k in classes]
     for copy in copies:
@@ -77,7 +76,7 @@
             pltpu.SMEM(source.shape, jnp.int32),
             pltpu.VMEM(psi.shape, psi.dtype),
             pltpu.SemaphoreType.DMA,
-            pltpu.SemaphoreType.DMA((psi.shape[0],)),
+            pltpu.SemaphoreType.DMA((1,)),
         ],
         compiler_params=params(),
         name="route",

time: 29 us -> 28.9 us (level)
  no operation moved by 1% of the time
where the time goes in v7:
time: 28.9 us; the launch traced here: 28.6 us
  starting transfers between devices  11.6 us (40%)
  waiting for transfers between devices  9.13 us (32%)
  Pallas kernels  7.51 us (26%)
    ppermute x6, starting transfers between devices, across(): return lax.ppermute(value, 'mpo', [(i, i ^ m) for i in range(nmpo)])  5.31 us
    all_to_all x1, waiting for transfers between devices, fast_shards(): lax.all_to_all(both, 'sec', 0, 0, axis_index_groups=pairs, tiled=True)  5.03 us
    all_to_all x1, starting transfers between devices, fast_shards(): lax.all_to_all(both, 'sec', 0, 0, axis_index_groups=pairs, tiled=True)  4.87 us
    ppermute x6, waiting for transfers between devices, across(): return lax.ppermute(value, 'mpo', [(i, i ^ m) for i in range(nmpo)])  4.09 us
    pallas_call x1, Pallas kernels, receive_order(): pl.pallas_call(functools.partial(order_kernel, nsec, sdev), out_shape=jax...  1.49 us
    ppermute x2, starting transfers between devices, fast_shards(): arrived[k] = lax.ppermute(value, 'sec', [(i, i ^ k) for i in range(nsec)])  1.43 us
    pallas_call x1, Pallas kernels, early(): pl.pallas_call(functools.partial(early_kernel, nsec, nmpo), out_shape=[ke...  1.27 us
    pallas_call x1, Pallas kernels, route(): pl.pallas_call(functools.partial(route_kernel, classes), out_shape=[jax.S...  1.2 us
  transfers between devices with their start and end apart: 9, of which 4 were waited for; matrix products, arithmetic and copies ran while one was open for 1% of the time, Pallas kernels for 19%

profile of v7, /device:TPU:17, one launch (start us, length us, event | category | flops | bytes accessed | tf_op | source)
XLA Modules:
  0.0 28.6 jit_solution(735590202379929150)
XLA Ops:
  0.0 1.2 %route.1 = (bf16[2,3,128,128]{3,2,1,0:T(8,128)(2,1)S(1)}, bf16[2,3,128,128]{3,2,1,0:T(8,128)(2,1)S(1)}, bf16[2,3,128,128]{3,2,1,0:T(8,128)(2,1)S(1)}, bf16[2,3,128,128]{3,2,1,0:T(8,128)(2,1)S(1)}) custom-call(s32[1,32]{1,0:T(1,128)} %source.3, bf16[8,3,128,128]{3,2,1,0:T(8,128)(2,1)} %bitcast.2), custom_call_target="tpu_custom_call" | custom-call | tf_op jit(solution)/shard_map/route/pallas_call | solution.py:70
  1.2 0.1 collective-permute-start
  1.3 1.4 %collective-permute-start.1 = (bf16[2,3,128,128]{3,2,1,0:T(8,128)(2,1)S(1)}, bf16[2,3,128,128]{3,2,1,0:T(8,128)(2,1)S(1)}, u32[]{:S(2)}, u32[]{:S(2)}) collective-permute-start(bf16[2,3,128,128]{3,2,1,0:T(8,128)(2,1)S(1)} %get-tuple-element.25), channel_id=1, source_target_pairs={{0,4},{4,0},{8,12},{12,8},{1,5},{5,1},{9,13},{13,9},{2,6},{6,2},{1... | collective-permute-start | bytes 589832 | tf_op jit(solution)/shard_map/ppermute | solution.py:437
  2.7 0.8 %double.1.after = bf16[2,2,3,128,128]{4,3,2,1,0:T(8,128)(2,1)} custom-call(bf16[2,3,128,128]{3,2,1,0:T(8,128)(2,1)S(1)} %get-tuple-element.23.block), custom_call_target="tpu_custom_call" | custom-call | tf_op jit(solution)/shard_map/double/pallas_call | solution.py:95
  3.4 0.0 copy-start
  3.4 0.0 copy-start.1
  3.5 4.9 %all-to-all-start = ((bf16[2,2,3,128,128]{4,3,2,1,0:T(8,128)(2,1)}), bf16[2,2,3,128,128]{4,3,2,1,0:T(8,128)(2,1)S(1)}, u32[]{:S(2)}, u32[]{:S(2)}) async-start(bf16[2,2,3,128,128]{4,3,2,1,0:T(8,128)(2,1)} %double.1.after), calls=%async_computation | async-start | bytes 786432 | tf_op jit(solution)/shard_map/all_to_all | solution.py:441
  8.3 0.0 copy-start.2
  8.3 1.5 %order.1.order_in = s32[8]{0:T(128)S(1)} custom-call(s32[1,32]{1,0:T(1,128)} %source.3, bf16[2,2,3,128,128]{4,3,2,1,0:T(8,128)(2,1)} %double.1.after), custom_call_target="tpu_custom_call" | custom-call | tf_op jit(solution)/shard_map/order/pallas_call | solution.py:118
  9.8 0.0 copy-done.2
  9.8 0.1 copy.6
  10.0 0.1 reshape.8.ops.ops_in
  10.1 0.0 copy-done
  10.1 0.0 copy-done.1
  10.1 1.3 %early.1 = (f32[2,2,3,32,128]{4,3,2,1,0:T(8,128)S(1)}, bf16[2,3,32,128]{3,2,1,0:T(8,128)(2,1)S(1)}, bf16[2,3,32,128]{3,2,1,0:T(8,128)(2,1)S(1)}, bf16[6,256,128]...) custom-call(s32[8]{0:T(128)S(1)} %order.1.order_in, ...), custom_call_target="tpu_custom_call" | custom-call | flops 100663296 | bytes 8388608 | tf_op jit(solution)/shard_map/early/pallas_call | solution.py:224
  11.4 0.0 collective-permute-done.refs_0_
  11.4 0.0 collective-permute-done.1.refs_1_
  11.4 1.1 %mid.1 = (f32[2,8,3,32,128]{4,3,2,1,0:T(8,128)S(1)}, bf16[8,3,32,128]{3,2,1,0:T(8,128)(2,1)S(1)}, bf16[8,3,32,128]{3,2,1,0:T(8,128)(2,1)S(1)}) custom-call(s32[8]{0:T(128)S(1)} %order.1.order_in, f32[144]{0:T(256)S(1)} %reshape.8.ops.ops_in, bf16[2,3,128,128]{3,2,1,0:T(8,128)(2,1)S(1)} %collective-permute-done.refs_0_, ...), custom_call_target="tpu_custom_call" | custom-call | flops 201326592 | bytes 8388608 | tf_op jit(solution)/shard_map/mid/pallas_call | solution.py:287
  12.5 1.7 %collective-permute-start.3 = (bf16[8,3,32,128]{3,2,1,0:T(8,128)(2,1)S(1)}, bf16[8,3,32,128]{3,2,1,0:T(8,128)(2,1)S(1)}, u32[]{:S(2)}, u32[]{:S(2)}) collective-permute-start(bf16[8,3,32,128]{3,2,1,0:T(8,128)(2,1)S(1)} %get-tuple-element.34), channel_id=1, source_target_pairs={{0,1},{1,0},{2,3},{3,2},{4,5},{5,4},{6,7},{7,6},{8,9},{9,8},{10,11... | collective-permute-start | bytes 589832 | tf_op jit(solution)/shard_map/ppermute | solution.py:444
  14.2 0.1 collective-permute-start.2
  14.3 1.0 %collective-permute-done.3.got = bf16[8,3,32,128]{3,2,1,0:T(8,128)(2,1)S(1)} collective-permute-done((bf16[8,3,32,128]{3,2,1,0:T(8,128)(2,1)S(1)}, bf16[8,3,32,128]{3,2,1,0:T(8,128)(2,1)S(1)}, u32[]{:S(2)}, u32[]{:S(2)}) %collective-permute-start.3) | collective-permute-done | bytes 196640 | tf_op jit(solution)/shard_map/ppermute | solution.py:444
  15.3 1.3 %collective-permute-start.4 = (bf16[8,3,32,128]{3,2,1,0:T(8,128)(2,1)S(1)}, bf16[8,3,32,128]{3,2,1,0:T(8,128)(2,1)S(1)}, u32[]{:S(2)}, u32[]{:S(2)}) collective-permute-start(bf16[8,3,32,128]{3,2,1,0:T(8,128)(2,1)S(1)} %pair.1.after), channel_id=1, source_target_pairs={{0,2},{1,3},{2,0},{3,1},{4,6},{5,7},{6,4},{7,5},{8,10},{9,11},{10,... | collective-permute-start | bytes 589832 | tf_op jit(solution)/shard_map/ppermute | solution.py:444
  16.6 5.0 %all-to-all-done.block = bf16[2,2,3,128,128]{4,3,2,1,0:T(8,128)(2,1)S(1)} async-done(((bf16[2,2,3,128,128]{4,3,2,1,0:T(8,128)(2,1)}), bf16[2,2,3,128,128]{4,3,2,1,0:T(8,128)(2,1)S(1)}, u32[]{:S(2)}, u32[]{:S(2)}) %all-to-all-start) | async-done | bytes 393248 | tf_op jit(solution)/shard_map/all_to_all | solution.py:441
  21.6 0.5 %last.1 = (f32[208,128]{1,0:T(8,128)S(1)}, bf16[208,128]{1,0:T(8,128)(2,1)S(1)}, bf16[208,128]{1,0:T(8,128)(2,1)S(1)}, bf16[208,128]{1,0:T(8,128)(2,1)S(1)}) custom-call(bf16[8,3,32,128]{3,2,1,0:T(8,128)(2,1)S(1)} %pair.1.after, bf16[2,2,3,128,128]{4,3,2,1,0:T(8,128)(2,1)S(1)} %all-to-all-done.block, ...), custom_call_target="tpu_custom_call" | custom-call | flops 100663296 | bytes 4194304 | tf_op jit(solution)/shard_map/last/pallas_call | solution.py:332
  22.1 0.6 %collective-permute-start.5 = (bf16[208,128]{1,0:T(8,128)(2,1)S(1)}, bf16[208,128]{1,0:T(8,128)(2,1)S(1)}, u32[]{:S(2)}, u32[]{:S(2)}) collective-permute-start(bf16[208,128]{1,0:T(8,128)(2,1)S(1)} %get-tuple-element.38), channel_id=1, source_target_pairs={{0,1},{1,0},{2,3},{3,2},{4,5},{5,4},{6,7},{7,6},{8,9},{9,8},{10,11... | collective-permute-start | bytes 159752 | tf_op jit(solution)/shard_map/ppermute | solution.py:444
  22.7 1.2 %collective-permute-start.6 = (bf16[208,128]{1,0:T(8,128)(2,1)S(1)}, bf16[208,128]{1,0:T(8,128)(2,1)S(1)}, u32[]{:S(2)}, u32[]{:S(2)}) collective-permute-start(bf16[208,128]{1,0:T(8,128)(2,1)S(1)} %get-tuple-element.39), channel_id=1, source_target_pairs={{0,2},{1,3},{2,0},{3,1},{4,6},{5,7},{6,4},{7,5},{8,10},{9,11},{10,... | collective-permute-start | bytes 159752 | tf_op jit(solution)/shard_map/ppermute | solution.py:444
  23.9 0.5 %collective-permute-start.7 = (bf16[208,128]{1,0:T(8,128)(2,1)S(1)}, bf16[208,128]{1,0:T(8,128)(2,1)S(1)}, u32[]{:S(2)}, u32[]{:S(2)}) collective-permute-start(bf16[208,128]{1,0:T(8,128)(2,1)S(1)} %get-tuple-element.40), channel_id=1, source_target_pairs={{0,3},{1,2},{2,1},{3,0},{4,7},{5,6},{6,5},{7,4},{8,11},{9,10},{10,... | collective-permute-start | bytes 159752 | tf_op jit(solution)/shard_map/ppermute | solution.py:444
  24.4 0.0 collective-permute-done.2.near
  24.4 0.0 collective-permute-done.5.mate
  24.4 0.0 collective-permute-done.4.far
  24.4 0.2 base.1.total
  24.6 1.5 %collective-permute-done.6.tail2 = bf16[208,128]{1,0:T(8,128)(2,1)S(1)} collective-permute-done((bf16[208,128]{1,0:T(8,128)(2,1)S(1)}, bf16[208,128]{1,0:T(8,128)(2,1)S(1)}, u32[]{:S(2)}, u32[]{:S(2)}) %collective-permute-start.6) | collective-permute-done | bytes 53280 | tf_op jit(solution)/shard_map/ppermute | solution.py:444
  26.1 1.6 %collective-permute-done.7.tail3 = bf16[208,128]{1,0:T(8,128)(2,1)S(1)} collective-permute-done((bf16[208,128]{1,0:T(8,128)(2,1)S(1)}, bf16[208,128]{1,0:T(8,128)(2,1)S(1)}, u32[]{:S(2)}, u32[]{:S(2)}) %collective-permute-start.7) | collective-permute-done | bytes 53280 | tf_op jit(solution)/shard_map/ppermute | solution.py:444
  27.7 0.9 %finish.1 = bf16[32,3,8,128]{3,2,1,0:T(8,128)(2,1)} custom-call(f32[8,3,32,128]{3,2,1,0:T(8,128)S(1)} %base.1.total, bf16[208,128]{1,0:T(8,128)(2,1)S(1)} %collective-permute-done.6.tail2, bf16[208,128]{1,0:T(8,128)(2,1)S(1)} %collective-permute-done.7.tail3), custom_call_target="tpu_custom_call" | custom-call | tf_op jit(solution)/shard_map/finish/pallas_call | solution.py:410
  (1 shorter events, 0.0 us)
Async XLA Ops:
  1.2 10.2 %collective-permute-start = (bf16[2,3,128,128]{3,2,1,0:T(8,128)(2,1)S(1)}, bf16[2,3,128,128]{3,2,1,0:T(8,128)(2,1)S(1)}, u32[]{:S(2)}, u32[]{:S(2)}) collective-permute-start(bf16[2,3,128,128]{3,2,1,0:T(8,128)(2,1)S(1)} %get-tuple-element.24), channel_id=1, source_target_pairs={{0,8},{4,12},{8,0},{12,4},{1,9},{5,13},{9,1},{13,5},{2,10},{6,14},... | collective-permute-start | bytes 589832 | tf_op jit(solution)/shard_map/ppermute | solution.py:437
  1.3 10.1 %collective-permute-start.1 = (bf16[2,3,128,128]{3,2,1,0:T(8,128)(2,1)S(1)}, bf16[2,3,128,128]{3,2,1,0:T(8,128)(2,1)S(1)}, u32[]{:S(2)}, u32[]{:S(2)}) collective-permute-start(bf16[2,3,128,128]{3,2,1,0:T(8,128)(2,1)S(1)} %get-tuple-element.25), channel_id=1, source_target_pairs={{0,4},{4,0},{8,12},{12,8},{1,5},{5,1},{9,13},{13,9},{2,6},{6,2},{1... | collective-permute-start | bytes 589832 | tf_op jit(solution)/shard_map/ppermute | solution.py:437
  3.4 6.7 %copy-start = (bf16[2,8,128,128]{3,2,1,0:T(8,128)(2,1)S(1)}, bf16[2,8,128,128]{3,2,1,0:T(8,128)(2,1)}, u32[]{:S(2)}) copy-start(bf16[2,8,128,128]{3,2,1,0:T(8,128)(2,1)} %refs_1_.1) | copy-start | bytes 1572868
  3.4 6.7 %copy-start.1 = (bf16[2,8,128,128]{3,2,1,0:T(8,128)(2,1)S(1)}, bf16[2,8,128,128]{3,2,1,0:T(8,128)(2,1)}, u32[]{:S(2)}) copy-start(bf16[2,8,128,128]{3,2,1,0:T(8,128)(2,1)} %refs_2_.1) | copy-start | bytes 1572868
  3.5 18.2 %all-to-all-start = ((bf16[2,2,3,128,128]{4,3,2,1,0:T(8,128)(2,1)}), bf16[2,2,3,128,128]{4,3,2,1,0:T(8,128)(2,1)S(1)}, u32[]{:S(2)}, u32[]{:S(2)}) async-start(bf16[2,2,3,128,128]{4,3,2,1,0:T(8,128)(2,1)} %double.1.after), calls=%async_computation | async-start | bytes 786432 | tf_op jit(solution)/shard_map/all_to_all | solution.py:441
  8.3 1.5 %copy-start.2 = (bf16[2,8,3,3]{1,0,3,2:T(2,128)(2,1)S(1)}, bf16[2,8,3,3]{1,0,3,2:T(2,128)(2,1)}, u32[]{:S(2)}) copy-start(bf16[2,8,3,3]{1,0,3,2:T(2,128)(2,1)} %param.8) | copy-start | bytes 868
  12.5 2.8 %collective-permute-start.3 = (bf16[8,3,32,128]{3,2,1,0:T(8,128)(2,1)S(1)}, bf16[8,3,32,128]{3,2,1,0:T(8,128)(2,1)S(1)}, u32[]{:S(2)}, u32[]{:S(2)}) collective-permute-start(bf16[8,3,32,128]{3,2,1,0:T(8,128)(2,1)S(1)} %get-tuple-element.34), channel_id=1, source_target_pairs={{0,1},{1,0},{2,3},{3,2},{4,5},{5,4},{6,7},{7,6},{8,9},{9,8},{10,11... | collective-permute-start | bytes 589832 | tf_op jit(solution)/shard_map/ppermute | solution.py:444
  14.2 10.2 %collective-permute-start.2 = (bf16[8,3,32,128]{3,2,1,0:T(8,128)(2,1)S(1)}, bf16[8,3,32,128]{3,2,1,0:T(8,128)(2,1)S(1)}, u32[]{:S(2)}, u32[]{:S(2)}) collective-permute-start(bf16[8,3,32,128]{3,2,1,0:T(8,128)(2,1)S(1)} %get-tuple-element.33), channel_id=1, source_target_pairs={{0,1},{1,0},{2,3},{3,2},{4,5},{5,4},{6,7},{7,6},{8,9},{9,8},{10,11... | collective-permute-start | bytes 589832 | tf_op jit(solution)/shard_map/ppermute | solution.py:444
  15.3 9.1 %collective-permute-start.4 = (bf16[8,3,32,128]{3,2,1,0:T(8,128)(2,1)S(1)}, bf16[8,3,32,128]{3,2,1,0:T(8,128)(2,1)S(1)}, u32[]{:S(2)}, u32[]{:S(2)}) collective-permute-start(bf16[8,3,32,128]{3,2,1,0:T(8,128)(2,1)S(1)} %pair.1.after), channel_id=1, source_target_pairs={{0,2},{1,3},{2,0},{3,1},{4,6},{5,7},{6,4},{7,5},{8,10},{9,11},{10,... | collective-permute-start | bytes 589832 | tf_op jit(solution)/shard_map/ppermute | solution.py:444
  22.1 2.3 %collective-permute-start.5 = (bf16[208,128]{1,0:T(8,128)(2,1)S(1)}, bf16[208,128]{1,0:T(8,128)(2,1)S(1)}, u32[]{:S(2)}, u32[]{:S(2)}) collective-permute-start(bf16[208,128]{1,0:T(8,128)(2,1)S(1)} %get-tuple-element.38), channel_id=1, source_target_pairs={{0,1},{1,0},{2,3},{3,2},{4,5},{5,4},{6,7},{7,6},{8,9},{9,8},{10,11... | collective-permute-start | bytes 159752 | tf_op jit(solution)/shard_map/ppermute | solution.py:444
  22.7 3.4 %collective-permute-start.6 = (bf16[208,128]{1,0:T(8,128)(2,1)S(1)}, bf16[208,128]{1,0:T(8,128)(2,1)S(1)}, u32[]{:S(2)}, u32[]{:S(2)}) collective-permute-start(bf16[208,128]{1,0:T(8,128)(2,1)S(1)} %get-tuple-element.39), channel_id=1, source_target_pairs={{0,2},{1,3},{2,0},{3,1},{4,6},{5,7},{6,4},{7,5},{8,10},{9,11},{10,... | collective-permute-start | bytes 159752 | tf_op jit(solution)/shard_map/ppermute | solution.py:444
  23.9 3.8 %collective-permute-start.7 = (bf16[208,128]{1,0:T(8,128)(2,1)S(1)}, bf16[208,128]{1,0:T(8,128)(2,1)S(1)}, u32[]{:S(2)}, u32[]{:S(2)}) collective-permute-start(bf16[208,128]{1,0:T(8,128)(2,1)S(1)} %get-tuple-element.40), channel_id=1, source_target_pairs={{0,3},{1,2},{2,1},{3,0},{4,7},{5,6},{6,5},{7,4},{8,11},{9,10},{10,... | collective-permute-start | bytes 159752 | tf_op jit(solution)/shard_map/ppermute | solution.py:444

commit v8 on v7

--- a/solution.py
+++ b/solution.py
@@ -391,18 +391,13 @@
     )(keep, near, far, own, mate)
 
 
-def finish_kernel(total, tail2, tail3, out, acc, turned, sems):
+def finish_kernel(total, tail2, tail3, out, acc):
     sdev, phys, part, blk = total.shape
-    copies = []
+    for t in range(sdev):
+        late = tail_sum((tail2, tail3), t, 0, phys * part).reshape(phys, part, blk)
+        acc[t] = total[t] + late
     for q in range(phys):
-        for t in range(sdev):
-            acc[q, t] = total[t, q] + tail_sum((tail2, tail3), t, q * part, part)
-        turned[q] = jnp.swapaxes(acc[q], 0, 1).astype(turned.dtype)
-        copy = pltpu.make_async_copy(turned.at[q], out.at[:, q], sems.at[q])
-        copy.start()
-        copies.append(copy)
-    for copy in copies:
-        copy.wait()
+        out[:, q] = jnp.swapaxes(acc[:, q], 0, 1).astype(out.dtype)
 
 
 def finish(total, tail2, tail3):
@@ -411,12 +406,8 @@
         finish_kernel,
         out_shape=jax.ShapeDtypeStruct((part, phys, sdev, blk), jnp.bfloat16),
         in_specs=[space(pltpu.VMEM)] * 3,
-        out_specs=space(pl.ANY),
-        scratch_shapes=[
-            pltpu.VMEM((phys, sdev, part, blk), jnp.float32),
-            pltpu.VMEM((phys, part, sdev, blk), jnp.bfloat16),
-            pltpu.SemaphoreType.DMA((phys,)),
-        ],
+        out_specs=space(pltpu.VMEM),
+        scratch_shapes=[pltpu.VMEM(total.shape, total.dtype)],
         compiler_params=params(),
         name="finish",
     )(total, tail2, tail3)

time: 28.9 us -> 28.9 us (level)
  no operation moved by 1% of the time
where the time goes in v8:
time: 28.9 us; the launch traced here: 28.6 us
  starting transfers between devices  11.6 us (40%)
  waiting for transfers between devices  9.13 us (32%)
  Pallas kernels  7.51 us (26%)
    ppermute x6, starting transfers between devices, across(): return lax.ppermute(value, 'mpo', [(i, i ^ m) for i in range(nmpo)])  5.31 us
    all_to_all x1, waiting for transfers between devices, fast_shards(): lax.all_to_all(both, 'sec', 0, 0, axis_index_groups=pairs, tiled=True)  5.03 us
    all_to_all x1, starting transfers between devices, fast_shards(): lax.all_to_all(both, 'sec', 0, 0, axis_index_groups=pairs, tiled=True)  4.87 us
    ppermute x6, waiting for transfers between devices, across(): return lax.ppermute(value, 'mpo', [(i, i ^ m) for i in range(nmpo)])  4.09 us
    pallas_call x1, Pallas kernels, receive_order(): pl.pallas_call(functools.partial(order_kernel, nsec, sdev), out_shape=jax...  1.49 us
    ppermute x2, starting transfers between devices, fast_shards(): arrived[k] = lax.ppermute(value, 'sec', [(i, i ^ k) for i in range(nsec)])  1.43 us
    pallas_call x1, Pallas kernels, early(): pl.pallas_call(functools.partial(early_kernel, nsec, nmpo), out_shape=[ke...  1.27 us
    pallas_call x1, Pallas kernels, route(): pl.pallas_call(functools.partial(route_kernel, classes), out_shape=[jax.S...  1.2 us
  transfers between devices with their start and end apart: 9, of which 4 were waited for; matrix products, arithmetic and copies ran while one was open for 1% of the time, Pallas kernels for 19%

profile of v8, /device:TPU:17, one launch (start us, length us, event | category | flops | bytes accessed | tf_op | source)
XLA Modules:
  0.0 28.6 jit_solution(8445633637057462796)
XLA Ops:
  0.0 1.2 %route.1 = (bf16[2,3,128,128]{3,2,1,0:T(8,128)(2,1)S(1)}, bf16[2,3,128,128]{3,2,1,0:T(8,128)(2,1)S(1)}, bf16[2,3,128,128]{3,2,1,0:T(8,128)(2,1)S(1)}, bf16[2,3,128,128]{3,2,1,0:T(8,128)(2,1)S(1)}) custom-call(s32[1,32]{1,0:T(1,128)} %source.3, bf16[8,3,128,128]{3,2,1,0:T(8,128)(2,1)} %bitcast.2), custom_call_target="tpu_custom_call" | custom-call | tf_op jit(solution)/shard_map/route/pallas_call | solution.py:70
  1.2 0.1 collective-permute-start
  1.3 1.4 %collective-permute-start.1 = (bf16[2,3,128,128]{3,2,1,0:T(8,128)(2,1)S(1)}, bf16[2,3,128,128]{3,2,1,0:T(8,128)(2,1)S(1)}, u32[]{:S(2)}, u32[]{:S(2)}) collective-permute-start(bf16[2,3,128,128]{3,2,1,0:T(8,128)(2,1)S(1)} %get-tuple-element.25), channel_id=1, source_target_pairs={{0,4},{4,0},{8,12},{12,8},{1,5},{5,1},{9,13},{13,9},{2,6},{6,2},{1... | collective-permute-start | bytes 589832 | tf_op jit(solution)/shard_map/ppermute | solution.py:428
  2.7 0.8 %double.1.after = bf16[2,2,3,128,128]{4,3,2,1,0:T(8,128)(2,1)} custom-call(bf16[2,3,128,128]{3,2,1,0:T(8,128)(2,1)S(1)} %get-tuple-element.23.block), custom_call_target="tpu_custom_call" | custom-call | tf_op jit(solution)/shard_map/double/pallas_call | solution.py:95
  3.4 0.0 copy-start
  3.4 0.0 copy-start.1
  3.5 4.9 %all-to-all-start = ((bf16[2,2,3,128,128]{4,3,2,1,0:T(8,128)(2,1)}), bf16[2,2,3,128,128]{4,3,2,1,0:T(8,128)(2,1)S(1)}, u32[]{:S(2)}, u32[]{:S(2)}) async-start(bf16[2,2,3,128,128]{4,3,2,1,0:T(8,128)(2,1)} %double.1.after), calls=%async_computation | async-start | bytes 786432 | tf_op jit(solution)/shard_map/all_to_all | solution.py:432
  8.3 0.0 copy-start.2
  8.3 1.5 %order.1.order_in = s32[8]{0:T(128)S(1)} custom-call(s32[1,32]{1,0:T(1,128)} %source.3, bf16[2,2,3,128,128]{4,3,2,1,0:T(8,128)(2,1)} %double.1.after), custom_call_target="tpu_custom_call" | custom-call | tf_op jit(solution)/shard_map/order/pallas_call | solution.py:118
  9.8 0.0 copy-done.2
  9.8 0.1 copy.6
  10.0 0.1 reshape.8.ops.ops_in
  10.1 0.0 copy-done
  10.1 0.0 copy-done.1
  10.1 1.3 %early.1 = (f32[2,2,3,32,128]{4,3,2,1,0:T(8,128)S(1)}, bf16[2,3,32,128]{3,2,1,0:T(8,128)(2,1)S(1)}, bf16[2,3,32,128]{3,2,1,0:T(8,128)(2,1)S(1)}, bf16[6,256,128]...) custom-call(s32[8]{0:T(128)S(1)} %order.1.order_in, ...), custom_call_target="tpu_custom_call" | custom-call | flops 100663296 | bytes 8388608 | tf_op jit(solution)/shard_map/early/pallas_call | solution.py:224
  11.4 0.0 collective-permute-done.refs_0_
  11.4 0.0 collective-permute-done.1.refs_1_
  11.4 1.1 %mid.1 = (f32[2,8,3,32,128]{4,3,2,1,0:T(8,128)S(1)}, bf16[8,3,32,128]{3,2,1,0:T(8,128)(2,1)S(1)}, bf16[8,3,32,128]{3,2,1,0:T(8,128)(2,1)S(1)}) custom-call(s32[8]{0:T(128)S(1)} %order.1.order_in, f32[144]{0:T(256)S(1)} %reshape.8.ops.ops_in, bf16[2,3,128,128]{3,2,1,0:T(8,128)(2,1)S(1)} %collective-permute-done.refs_0_, ...), custom_call_target="tpu_custom_call" | custom-call | flops 201326592 | bytes 8388608 | tf_op jit(solution)/shard_map/mid/pallas_call | solution.py:287
  12.5 1.7 %collective-permute-start.3 = (bf16[8,3,32,128]{3,2,1,0:T(8,128)(2,1)S(1)}, bf16[8,3,32,128]{3,2,1,0:T(8,128)(2,1)S(1)}, u32[]{:S(2)}, u32[]{:S(2)}) collective-permute-start(bf16[8,3,32,128]{3,2,1,0:T(8,128)(2,1)S(1)} %get-tuple-element.34), channel_id=1, source_target_pairs={{0,1},{1,0},{2,3},{3,2},{4,5},{5,4},{6,7},{7,6},{8,9},{9,8},{10,11... | collective-permute-start | bytes 589832 | tf_op jit(solution)/shard_map/ppermute | solution.py:435
  14.2 0.1 collective-permute-start.2
  14.3 1.0 %collective-permute-done.3.got = bf16[8,3,32,128]{3,2,1,0:T(8,128)(2,1)S(1)} collective-permute-done((bf16[8,3,32,128]{3,2,1,0:T(8,128)(2,1)S(1)}, bf16[8,3,32,128]{3,2,1,0:T(8,128)(2,1)S(1)}, u32[]{:S(2)}, u32[]{:S(2)}) %collective-permute-start.3) | collective-permute-done | bytes 196640 | tf_op jit(solution)/shard_map/ppermute | solution.py:435
  15.3 1.3 %collective-permute-start.4 = (bf16[8,3,32,128]{3,2,1,0:T(8,128)(2,1)S(1)}, bf16[8,3,32,128]{3,2,1,0:T(8,128)(2,1)S(1)}, u32[]{:S(2)}, u32[]{:S(2)}) collective-permute-start(bf16[8,3,32,128]{3,2,1,0:T(8,128)(2,1)S(1)} %pair.1.after), channel_id=1, source_target_pairs={{0,2},{1,3},{2,0},{3,1},{4,6},{5,7},{6,4},{7,5},{8,10},{9,11},{10,... | collective-permute-start | bytes 589832 | tf_op jit(solution)/shard_map/ppermute | solution.py:435
  16.6 5.0 %all-to-all-done.block = bf16[2,2,3,128,128]{4,3,2,1,0:T(8,128)(2,1)S(1)} async-done(((bf16[2,2,3,128,128]{4,3,2,1,0:T(8,128)(2,1)}), bf16[2,2,3,128,128]{4,3,2,1,0:T(8,128)(2,1)S(1)}, u32[]{:S(2)}, u32[]{:S(2)}) %all-to-all-start) | async-done | bytes 393248 | tf_op jit(solution)/shard_map/all_to_all | solution.py:432
  21.6 0.5 %last.1 = (f32[208,128]{1,0:T(8,128)S(1)}, bf16[208,128]{1,0:T(8,128)(2,1)S(1)}, bf16[208,128]{1,0:T(8,128)(2,1)S(1)}, bf16[208,128]{1,0:T(8,128)(2,1)S(1)}) custom-call(bf16[8,3,32,128]{3,2,1,0:T(8,128)(2,1)S(1)} %pair.1.after, bf16[2,2,3,128,128]{4,3,2,1,0:T(8,128)(2,1)S(1)} %all-to-all-done.block, ...), custom_call_target="tpu_custom_call" | custom-call | flops 100663296 | bytes 4194304 | tf_op jit(solution)/shard_map/last/pallas_call | solution.py:332
  22.1 0.6 %collective-permute-start.5 = (bf16[208,128]{1,0:T(8,128)(2,1)S(1)}, bf16[208,128]{1,0:T(8,128)(2,1)S(1)}, u32[]{:S(2)}, u32[]{:S(2)}) collective-permute-start(bf16[208,128]{1,0:T(8,128)(2,1)S(1)} %get-tuple-element.38), channel_id=1, source_target_pairs={{0,1},{1,0},{2,3},{3,2},{4,5},{5,4},{6,7},{7,6},{8,9},{9,8},{10,11... | collective-permute-start | bytes 159752 | tf_op jit(solution)/shard_map/ppermute | solution.py:435
  22.7 1.2 %collective-permute-start.6 = (bf16[208,128]{1,0:T(8,128)(2,1)S(1)}, bf16[208,128]{1,0:T(8,128)(2,1)S(1)}, u32[]{:S(2)}, u32[]{:S(2)}) collective-permute-start(bf16[208,128]{1,0:T(8,128)(2,1)S(1)} %get-tuple-element.39), channel_id=1, source_target_pairs={{0,2},{1,3},{2,0},{3,1},{4,6},{5,7},{6,4},{7,5},{8,10},{9,11},{10,... | collective-permute-start | bytes 159752 | tf_op jit(solution)/shard_map/ppermute | solution.py:435
  23.9 0.5 %collective-permute-start.7 = (bf16[208,128]{1,0:T(8,128)(2,1)S(1)}, bf16[208,128]{1,0:T(8,128)(2,1)S(1)}, u32[]{:S(2)}, u32[]{:S(2)}) collective-permute-start(bf16[208,128]{1,0:T(8,128)(2,1)S(1)} %get-tuple-element.40), channel_id=1, source_target_pairs={{0,3},{1,2},{2,1},{3,0},{4,7},{5,6},{6,5},{7,4},{8,11},{9,10},{10,... | collective-permute-start | bytes 159752 | tf_op jit(solution)/shard_map/ppermute | solution.py:435
  24.4 0.0 collective-permute-done.2.near
  24.4 0.0 collective-permute-done.5.mate
  24.4 0.0 collective-permute-done.4.far
  24.4 0.2 base.1.total
  24.6 1.5 %collective-permute-done.6.tail2 = bf16[208,128]{1,0:T(8,128)(2,1)S(1)} collective-permute-done((bf16[208,128]{1,0:T(8,128)(2,1)S(1)}, bf16[208,128]{1,0:T(8,128)(2,1)S(1)}, u32[]{:S(2)}, u32[]{:S(2)}) %collective-permute-start.6) | collective-permute-done | bytes 53280 | tf_op jit(solution)/shard_map/ppermute | solution.py:435
  26.1 1.6 %collective-permute-done.7.tail3 = bf16[208,128]{1,0:T(8,128)(2,1)S(1)} collective-permute-done((bf16[208,128]{1,0:T(8,128)(2,1)S(1)}, bf16[208,128]{1,0:T(8,128)(2,1)S(1)}, u32[]{:S(2)}, u32[]{:S(2)}) %collective-permute-start.7) | collective-permute-done | bytes 53280 | tf_op jit(solution)/shard_map/ppermute | solution.py:435
  27.7 0.9 %finish.1 = bf16[32,3,8,128]{3,2,1,0:T(8,128)(2,1)} custom-call(f32[8,3,32,128]{3,2,1,0:T(8,128)S(1)} %base.1.total, bf16[208,128]{1,0:T(8,128)(2,1)S(1)} %collective-permute-done.6.tail2, bf16[208,128]{1,0:T(8,128)(2,1)S(1)} %collective-permute-done.7.tail3), custom_call_target="tpu_custom_call" | custom-call | tf_op jit(solution)/shard_map/finish/pallas_call | solution.py:405
  (1 shorter events, 0.0 us)
Async XLA Ops:
  1.2 10.2 %collective-permute-start = (bf16[2,3,128,128]{3,2,1,0:T(8,128)(2,1)S(1)}, bf16[2,3,128,128]{3,2,1,0:T(8,128)(2,1)S(1)}, u32[]{:S(2)}, u32[]{:S(2)}) collective-permute-start(bf16[2,3,128,128]{3,2,1,0:T(8,128)(2,1)S(1)} %get-tuple-element.24), channel_id=1, source_target_pairs={{0,8},{4,12},{8,0},{12,4},{1,9},{5,13},{9,1},{13,5},{2,10},{6,14},... | collective-permute-start | bytes 589832 | tf_op jit(solution)/shard_map/ppermute | solution.py:428
  1.3 10.1 %collective-permute-start.1 = (bf16[2,3,128,128]{3,2,1,0:T(8,128)(2,1)S(1)}, bf16[2,3,128,128]{3,2,1,0:T(8,128)(2,1)S(1)}, u32[]{:S(2)}, u32[]{:S(2)}) collective-permute-start(bf16[2,3,128,128]{3,2,1,0:T(8,128)(2,1)S(1)} %get-tuple-element.25), channel_id=1, source_target_pairs={{0,4},{4,0},{8,12},{12,8},{1,5},{5,1},{9,13},{13,9},{2,6},{6,2},{1... | collective-permute-start | bytes 589832 | tf_op jit(solution)/shard_map/ppermute | solution.py:428
  3.4 6.7 %copy-start = (bf16[2,8,128,128]{3,2,1,0:T(8,128)(2,1)S(1)}, bf16[2,8,128,128]{3,2,1,0:T(8,128)(2,1)}, u32[]{:S(2)}) copy-start(bf16[2,8,128,128]{3,2,1,0:T(8,128)(2,1)} %refs_1_.1) | copy-start | bytes 1572868
  3.4 6.7 %copy-start.1 = (bf16[2,8,128,128]{3,2,1,0:T(8,128)(2,1)S(1)}, bf16[2,8,128,128]{3,2,1,0:T(8,128)(2,1)}, u32[]{:S(2)}) copy-start(bf16[2,8,128,128]{3,2,1,0:T(8,128)(2,1)} %refs_2_.1) | copy-start | bytes 1572868
  3.5 18.2 %all-to-all-start = ((bf16[2,2,3,128,128]{4,3,2,1,0:T(8,128)(2,1)}), bf16[2,2,3,128,128]{4,3,2,1,0:T(8,128)(2,1)S(1)}, u32[]{:S(2)}, u32[]{:S(2)}) async-start(bf16[2,2,3,128,128]{4,3,2,1,0:T(8,128)(2,1)} %double.1.after), calls=%async_computation | async-start | bytes 786432 | tf_op jit(solution)/shard_map/all_to_all | solution.py:432
  8.3 1.5 %copy-start.2 = (bf16[2,8,3,3]{1,0,3,2:T(2,128)(2,1)S(1)}, bf16[2,8,3,3]{1,0,3,2:T(2,128)(2,1)}, u32[]{:S(2)}) copy-start(bf16[2,8,3,3]{1,0,3,2:T(2,128)(2,1)} %param.8) | copy-start | bytes 868
  12.5 2.8 %collective-permute-start.3 = (bf16[8,3,32,128]{3,2,1,0:T(8,128)(2,1)S(1)}, bf16[8,3,32,128]{3,2,1,0:T(8,128)(2,1)S(1)}, u32[]{:S(2)}, u32[]{:S(2)}) collective-permute-start(bf16[8,3,32,128]{3,2,1,0:T(8,128)(2,1)S(1)} %get-tuple-element.34), channel_id=1, source_target_pairs={{0,1},{1,0},{2,3},{3,2},{4,5},{5,4},{6,7},{7,6},{8,9},{9,8},{10,11... | collective-permute-start | bytes 589832 | tf_op jit(solution)/shard_map/ppermute | solution.py:435
  14.2 10.2 %collective-permute-start.2 = (bf16[8,3,32,128]{3,2,1,0:T(8,128)(2,1)S(1)}, bf16[8,3,32,128]{3,2,1,0:T(8,128)(2,1)S(1)}, u32[]{:S(2)}, u32[]{:S(2)}) collective-permute-start(bf16[8,3,32,128]{3,2,1,0:T(8,128)(2,1)S(1)} %get-tuple-element.33), channel_id=1, source_target_pairs={{0,1},{1,0},{2,3},{3,2},{4,5},{5,4},{6,7},{7,6},{8,9},{9,8},{10,11... | collective-permute-start | bytes 589832 | tf_op jit(solution)/shard_map/ppermute | solution.py:435
  15.3 9.1 %collective-permute-start.4 = (bf16[8,3,32,128]{3,2,1,0:T(8,128)(2,1)S(1)}, bf16[8,3,32,128]{3,2,1,0:T(8,128)(2,1)S(1)}, u32[]{:S(2)}, u32[]{:S(2)}) collective-permute-start(bf16[8,3,32,128]{3,2,1,0:T(8,128)(2,1)S(1)} %pair.1.after), channel_id=1, source_target_pairs={{0,2},{1,3},{2,0},{3,1},{4,6},{5,7},{6,4},{7,5},{8,10},{9,11},{10,... | collective-permute-start | bytes 589832 | tf_op jit(solution)/shard_map/ppermute | solution.py:435
  22.1 2.3 %collective-permute-start.5 = (bf16[208,128]{1,0:T(8,128)(2,1)S(1)}, bf16[208,128]{1,0:T(8,128)(2,1)S(1)}, u32[]{:S(2)}, u32[]{:S(2)}) collective-permute-start(bf16[208,128]{1,0:T(8,128)(2,1)S(1)} %get-tuple-element.38), channel_id=1, source_target_pairs={{0,1},{1,0},{2,3},{3,2},{4,5},{5,4},{6,7},{7,6},{8,9},{9,8},{10,11... | collective-permute-start | bytes 159752 | tf_op jit(solution)/shard_map/ppermute | solution.py:435
  22.7 3.4 %collective-permute-start.6 = (bf16[208,128]{1,0:T(8,128)(2,1)S(1)}, bf16[208,128]{1,0:T(8,128)(2,1)S(1)}, u32[]{:S(2)}, u32[]{:S(2)}) collective-permute-start(bf16[208,128]{1,0:T(8,128)(2,1)S(1)} %get-tuple-element.39), channel_id=1, source_target_pairs={{0,2},{1,3},{2,0},{3,1},{4,6},{5,7},{6,4},{7,5},{8,10},{9,11},{10,... | collective-permute-start | bytes 159752 | tf_op jit(solution)/shard_map/ppermute | solution.py:435
  23.9 3.8 %collective-permute-start.7 = (bf16[208,128]{1,0:T(8,128)(2,1)S(1)}, bf16[208,128]{1,0:T(8,128)(2,1)S(1)}, u32[]{:S(2)}, u32[]{:S(2)}) collective-permute-start(bf16[208,128]{1,0:T(8,128)(2,1)S(1)} %get-tuple-element.40), channel_id=1, source_target_pairs={{0,3},{1,2},{2,1},{3,0},{4,7},{5,6},{6,5},{7,4},{8,11},{9,10},{10,... | collective-permute-start | bytes 159752 | tf_op jit(solution)/shard_map/ppermute | solution.py:435

commit v9 on v8

--- a/solution.py
+++ b/solution.py
@@ -83,7 +83,7 @@
     )(source, psi)
 
 
-def double_kernel(block, out, sems):
+def double_kernel(block, after, out, sems):
     copies = [pltpu.make_async_copy(block, out.at[i], sems.at[i]) for i in range(2)]
     for copy in copies:
         copy.start()
@@ -91,16 +91,16 @@
         copy.wait()
 
 
-def double(block):
+def double(block, after):
     return pl.pallas_call(
         double_kernel,
         out_shape=jax.ShapeDtypeStruct((2,) + block.shape, block.dtype),
-        in_specs=[space(pltpu.VMEM)],
+        in_specs=[space(pltpu.VMEM), space(pl.ANY)],
         out_specs=space(pl.ANY),
         scratch_shapes=[pltpu.SemaphoreType.DMA((2,))],
         compiler_params=params(),
         name="double",
-    )(block)
+    )(block, after)
 
 
 def order_kernel(nsec, sdev, source, after, order, table, load):
@@ -426,8 +426,8 @@
     arrived = {0: held[0]}
     for k, value in zip(MID, held[len(EARLY) :]):
         arrived[k] = lax.ppermute(value, "sec", [(i, i ^ k) for i in range(nsec)])
-    both = double(held[-1])
-    order = receive_order(table, both, nsec, sdev)
+    order = receive_order(table, held[0], nsec, sdev)
+    both = double(held[-1], order)
     pairs = [[i, i ^ LAST] for i in range(nsec) if i < i ^ LAST]
     final = lax.all_to_all(both, "sec", 0, 0, axis_index_groups=pairs, tiled=True)
 

time: 28.9 us -> 28.8 us (level)
  transfers between devices with their start and end apart: 9 -> 9, of which waited for: 4 -> 4; matrix products, arithmetic and copies ran while one was open for 1% -> 1% of each run, Pallas kernels for 19% -> 18%
where the time goes in v9:
time: 28.8 us; the launch traced here: 28.6 us
  starting transfers between devices  11.5 us (40%)
  waiting for transfers between devices  9.36 us (32%)
  Pallas kernels  7.38 us (26%)
    all_to_all x1, waiting for transfers between devices, fast_shards(): lax.all_to_all(both, 'sec', 0, 0, axis_index_groups=pairs, tiled=True)  5.27 us
    ppermute x6, starting transfers between devices, across(): return lax.ppermute(value, 'mpo', [(i, i ^ m) for i in range(nmpo)])  5.2 us
    all_to_all x1, starting transfers between devices, fast_shards(): lax.all_to_all(both, 'sec', 0, 0, axis_index_groups=pairs, tiled=True)  4.87 us
    ppermute x6, waiting for transfers between devices, across(): return lax.ppermute(value, 'mpo', [(i, i ^ m) for i in range(nmpo)])  4.09 us
    ppermute x2, starting transfers between devices, fast_shards(): arrived[k] = lax.ppermute(value, 'sec', [(i, i ^ k) for i in range(nsec)])  1.43 us
    pallas_call x1, Pallas kernels, receive_order(): pl.pallas_call(functools.partial(order_kernel, nsec, sdev), out_shape=jax...  1.36 us
    pallas_call x1, Pallas kernels, early(): pl.pallas_call(functools.partial(early_kernel, nsec, nmpo), out_shape=[ke...  1.27 us
    pallas_call x1, Pallas kernels, route(): pl.pallas_call(functools.partial(route_kernel, classes), out_shape=[jax.S...  1.2 us
  transfers between devices with their start and end apart: 9, of which 4 were waited for; matrix products, arithmetic and copies ran while one was open for 1% of the time, Pallas kernels for 18%

profile of v9, /device:TPU:17, one launch (start us, length us, event | category | flops | bytes accessed | tf_op | source)
XLA Modules:
  0.0 28.6 jit_solution(15899441518092924656)
XLA Ops:
  0.0 1.2 %route.1 = (bf16[2,3,128,128]{3,2,1,0:T(8,128)(2,1)S(1)}, bf16[2,3,128,128]{3,2,1,0:T(8,128)(2,1)S(1)}, bf16[2,3,128,128]{3,2,1,0:T(8,128)(2,1)S(1)}, bf16[2,3,128,128]{3,2,1,0:T(8,128)(2,1)S(1)}) custom-call(s32[1,32]{1,0:T(1,128)} %source.3, bf16[8,3,128,128]{3,2,1,0:T(8,128)(2,1)} %bitcast.2), custom_call_target="tpu_custom_call" | custom-call | tf_op jit(solution)/shard_map/route/pallas_call | solution.py:70
  1.2 0.1 collective-permute-start
  1.3 1.4 %collective-permute-start.1 = (bf16[2,3,128,128]{3,2,1,0:T(8,128)(2,1)S(1)}, bf16[2,3,128,128]{3,2,1,0:T(8,128)(2,1)S(1)}, u32[]{:S(2)}, u32[]{:S(2)}) collective-permute-start(bf16[2,3,128,128]{3,2,1,0:T(8,128)(2,1)S(1)} %get-tuple-element.25), channel_id=1, source_target_pairs={{0,4},{4,0},{8,12},{12,8},{1,5},{5,1},{9,13},{13,9},{2,6},{6,2},{1... | collective-permute-start | bytes 589832 | tf_op jit(solution)/shard_map/ppermute | solution.py:428
  2.7 1.4 %order.1.order_in.after = s32[8]{0:T(128)S(1)} custom-call(s32[1,32]{1,0:T(1,128)} %source.3, bf16[2,3,128,128]{3,2,1,0:T(8,128)(2,1)S(1)} %get-tuple-element.23.after.refs_0_), custom_call_target="tpu_custom_call" | custom-call | tf_op jit(solution)/shard_map/order/pallas_call | solution.py:118
  4.0 0.0 copy-start.1
  4.0 0.8 %double.1 = bf16[2,2,3,128,128]{4,3,2,1,0:T(8,128)(2,1)} custom-call(bf16[2,3,128,128]{3,2,1,0:T(8,128)(2,1)S(1)} %get-tuple-element.34.block, s32[8]{0:T(128)S(1)} %order.1.order_in.after), custom_call_target="tpu_custom_call" | custom-call | tf_op jit(solution)/shard_map/double/pallas_call | solution.py:95
  4.8 0.0 copy-start.2
  4.8 0.0 copy-start
  4.8 4.9 %all-to-all-start = ((bf16[2,2,3,128,128]{4,3,2,1,0:T(8,128)(2,1)}), bf16[2,2,3,128,128]{4,3,2,1,0:T(8,128)(2,1)S(1)}, u32[]{:S(2)}, u32[]{:S(2)}) async-start(bf16[2,2,3,128,128]{4,3,2,1,0:T(8,128)(2,1)} %double.1), calls=%async_computation | async-start | bytes 786432 | tf_op jit(solution)/shard_map/all_to_all | solution.py:432
  9.7 0.0 copy-done.2
  9.7 0.1 copy.6
  9.8 0.1 reshape.8.ops.ops_in
  10.0 0.0 copy-done.1
  10.0 0.0 copy-done
  10.0 1.3 %early.1 = (f32[2,2,3,32,128]{4,3,2,1,0:T(8,128)S(1)}, bf16[2,3,32,128]{3,2,1,0:T(8,128)(2,1)S(1)}, bf16[2,3,32,128]{3,2,1,0:T(8,128)(2,1)S(1)}, bf16[6,256,128]...) custom-call(s32[8]{0:T(128)S(1)} %order.1.order_in.after, ...), custom_call_target="tpu_custom_call" | custom-call | flops 100663296 | bytes 8388608 | tf_op jit(solution)/shard_map/early/pallas_call | solution.py:224
  11.3 0.0 collective-permute-done.refs_0_
  11.3 0.0 collective-permute-done.1.refs_1_
  11.3 1.1 %mid.1 = (f32[2,8,3,32,128]{4,3,2,1,0:T(8,128)S(1)}, bf16[8,3,32,128]{3,2,1,0:T(8,128)(2,1)S(1)}, bf16[8,3,32,128]{3,2,1,0:T(8,128)(2,1)S(1)}) custom-call(s32[8]{0:T(128)S(1)} %order.1.order_in.after, f32[144]{0:T(256)S(1)} %reshape.8.ops.ops_in, bf16[2,3,128,128]{3,2,1,0:T(8,128)(2,1)S(1)} %collective-permute-done.refs_0_, ...), custom_call_target="tpu_custom_call" | custom-call | flops 201326592 | bytes 8388608 | tf_op jit(solution)/shard_map/mid/pallas_call | solution.py:287
  12.4 1.6 %collective-permute-start.3 = (bf16[8,3,32,128]{3,2,1,0:T(8,128)(2,1)S(1)}, bf16[8,3,32,128]{3,2,1,0:T(8,128)(2,1)S(1)}, u32[]{:S(2)}, u32[]{:S(2)}) collective-permute-start(bf16[8,3,32,128]{3,2,1,0:T(8,128)(2,1)S(1)} %get-tuple-element.33), channel_id=1, source_target_pairs={{0,1},{1,0},{2,3},{3,2},{4,5},{5,4},{6,7},{7,6},{8,9},{9,8},{10,11... | collective-permute-start | bytes 589832 | tf_op jit(solution)/shard_map/ppermute | solution.py:435
  14.0 0.1 collective-permute-start.2
  14.1 1.0 %collective-permute-done.3.got = bf16[8,3,32,128]{3,2,1,0:T(8,128)(2,1)S(1)} collective-permute-done((bf16[8,3,32,128]{3,2,1,0:T(8,128)(2,1)S(1)}, bf16[8,3,32,128]{3,2,1,0:T(8,128)(2,1)S(1)}, u32[]{:S(2)}, u32[]{:S(2)}) %collective-permute-start.3) | collective-permute-done | bytes 196640 | tf_op jit(solution)/shard_map/ppermute | solution.py:435
  15.1 1.3 %collective-permute-start.4 = (bf16[8,3,32,128]{3,2,1,0:T(8,128)(2,1)S(1)}, bf16[8,3,32,128]{3,2,1,0:T(8,128)(2,1)S(1)}, u32[]{:S(2)}, u32[]{:S(2)}) collective-permute-start(bf16[8,3,32,128]{3,2,1,0:T(8,128)(2,1)S(1)} %pair.1.after), channel_id=1, source_target_pairs={{0,2},{1,3},{2,0},{3,1},{4,6},{5,7},{6,4},{7,5},{8,10},{9,11},{10,... | collective-permute-start | bytes 589832 | tf_op jit(solution)/shard_map/ppermute | solution.py:435
  16.4 5.3 %all-to-all-done.block = bf16[2,2,3,128,128]{4,3,2,1,0:T(8,128)(2,1)S(1)} async-done(((bf16[2,2,3,128,128]{4,3,2,1,0:T(8,128)(2,1)}), bf16[2,2,3,128,128]{4,3,2,1,0:T(8,128)(2,1)S(1)}, u32[]{:S(2)}, u32[]{:S(2)}) %all-to-all-start) | async-done | bytes 393248 | tf_op jit(solution)/shard_map/all_to_all | solution.py:432
  21.6 0.5 %last.1 = (f32[208,128]{1,0:T(8,128)S(1)}, bf16[208,128]{1,0:T(8,128)(2,1)S(1)}, bf16[208,128]{1,0:T(8,128)(2,1)S(1)}, bf16[208,128]{1,0:T(8,128)(2,1)S(1)}) custom-call(bf16[8,3,32,128]{3,2,1,0:T(8,128)(2,1)S(1)} %pair.1.after, bf16[2,2,3,128,128]{4,3,2,1,0:T(8,128)(2,1)S(1)} %all-to-all-done.block, ...), custom_call_target="tpu_custom_call" | custom-call | flops 100663296 | bytes 4194304 | tf_op jit(solution)/shard_map/last/pallas_call | solution.py:332
  22.1 0.6 %collective-permute-start.5 = (bf16[208,128]{1,0:T(8,128)(2,1)S(1)}, bf16[208,128]{1,0:T(8,128)(2,1)S(1)}, u32[]{:S(2)}, u32[]{:S(2)}) collective-permute-start(bf16[208,128]{1,0:T(8,128)(2,1)S(1)} %get-tuple-element.38), channel_id=1, source_target_pairs={{0,1},{1,0},{2,3},{3,2},{4,5},{5,4},{6,7},{7,6},{8,9},{9,8},{10,11... | collective-permute-start | bytes 159752 | tf_op jit(solution)/shard_map/ppermute | solution.py:435
  22.7 1.2 %collective-permute-start.6 = (bf16[208,128]{1,0:T(8,128)(2,1)S(1)}, bf16[208,128]{1,0:T(8,128)(2,1)S(1)}, u32[]{:S(2)}, u32[]{:S(2)}) collective-permute-start(bf16[208,128]{1,0:T(8,128)(2,1)S(1)} %get-tuple-element.39), channel_id=1, source_target_pairs={{0,2},{1,3},{2,0},{3,1},{4,6},{5,7},{6,4},{7,5},{8,10},{9,11},{10,... | collective-permute-start | bytes 159752 | tf_op jit(solution)/shard_map/ppermute | solution.py:435
  23.9 0.5 %collective-permute-start.7 = (bf16[208,128]{1,0:T(8,128)(2,1)S(1)}, bf16[208,128]{1,0:T(8,128)(2,1)S(1)}, u32[]{:S(2)}, u32[]{:S(2)}) collective-permute-start(bf16[208,128]{1,0:T(8,128)(2,1)S(1)} %get-tuple-element.40), channel_id=1, source_target_pairs={{0,3},{1,2},{2,1},{3,0},{4,7},{5,6},{6,5},{7,4},{8,11},{9,10},{10,... | collective-permute-start | bytes 159752 | tf_op jit(solution)/shard_map/ppermute | solution.py:435
  24.4 0.0 collective-permute-done.2.near
  24.4 0.0 collective-permute-done.5.mate
  24.4 0.0 collective-permute-done.4.far
  24.4 0.2 base.1.total
  24.6 1.5 %collective-permute-done.6.tail2 = bf16[208,128]{1,0:T(8,128)(2,1)S(1)} collective-permute-done((bf16[208,128]{1,0:T(8,128)(2,1)S(1)}, bf16[208,128]{1,0:T(8,128)(2,1)S(1)}, u32[]{:S(2)}, u32[]{:S(2)}) %collective-permute-start.6) | collective-permute-done | bytes 53280 | tf_op jit(solution)/shard_map/ppermute | solution.py:435
  26.1 1.6 %collective-permute-done.7.tail3 = bf16[208,128]{1,0:T(8,128)(2,1)S(1)} collective-permute-done((bf16[208,128]{1,0:T(8,128)(2,1)S(1)}, bf16[208,128]{1,0:T(8,128)(2,1)S(1)}, u32[]{:S(2)}, u32[]{:S(2)}) %collective-permute-start.7) | collective-permute-done | bytes 53280 | tf_op jit(solution)/shard_map/ppermute | solution.py:435
  27.7 0.9 %finish.1 = bf16[32,3,8,128]{3,2,1,0:T(8,128)(2,1)} custom-call(f32[8,3,32,128]{3,2,1,0:T(8,128)S(1)} %base.1.total, bf16[208,128]{1,0:T(8,128)(2,1)S(1)} %collective-permute-done.6.tail2, bf16[208,128]{1,0:T(8,128)(2,1)S(1)} %collective-permute-done.7.tail3), custom_call_target="tpu_custom_call" | custom-call | tf_op jit(solution)/shard_map/finish/pallas_call | solution.py:405
  (1 shorter events, 0.0 us)
Async XLA Ops:
  1.2 10.1 %collective-permute-start = (bf16[2,3,128,128]{3,2,1,0:T(8,128)(2,1)S(1)}, bf16[2,3,128,128]{3,2,1,0:T(8,128)(2,1)S(1)}, u32[]{:S(2)}, u32[]{:S(2)}) collective-permute-start(bf16[2,3,128,128]{3,2,1,0:T(8,128)(2,1)S(1)} %get-tuple-element.24), channel_id=1, source_target_pairs={{0,8},{4,12},{8,0},{12,4},{1,9},{5,13},{9,1},{13,5},{2,10},{6,14},... | collective-permute-start | bytes 589832 | tf_op jit(solution)/shard_map/ppermute | solution.py:428
  1.3 10.0 %collective-permute-start.1 = (bf16[2,3,128,128]{3,2,1,0:T(8,128)(2,1)S(1)}, bf16[2,3,128,128]{3,2,1,0:T(8,128)(2,1)S(1)}, u32[]{:S(2)}, u32[]{:S(2)}) collective-permute-start(bf16[2,3,128,128]{3,2,1,0:T(8,128)(2,1)S(1)} %get-tuple-element.25), channel_id=1, source_target_pairs={{0,4},{4,0},{8,12},{12,8},{1,5},{5,1},{9,13},{13,9},{2,6},{6,2},{1... | collective-permute-start | bytes 589832 | tf_op jit(solution)/shard_map/ppermute | solution.py:428
  4.0 5.9 %copy-start.1 = (bf16[2,8,128,128]{3,2,1,0:T(8,128)(2,1)S(1)}, bf16[2,8,128,128]{3,2,1,0:T(8,128)(2,1)}, u32[]{:S(2)}) copy-start(bf16[2,8,128,128]{3,2,1,0:T(8,128)(2,1)} %refs_2_.1) | copy-start | bytes 1572868
  4.8 4.9 %copy-start.2 = (bf16[2,8,3,3]{1,0,3,2:T(2,128)(2,1)S(1)}, bf16[2,8,3,3]{1,0,3,2:T(2,128)(2,1)}, u32[]{:S(2)}) copy-start(bf16[2,8,3,3]{1,0,3,2:T(2,128)(2,1)} %param.8) | copy-start | bytes 868
  4.8 5.1 %copy-start = (bf16[2,8,128,128]{3,2,1,0:T(8,128)(2,1)S(1)}, bf16[2,8,128,128]{3,2,1,0:T(8,128)(2,1)}, u32[]{:S(2)}) copy-start(bf16[2,8,128,128]{3,2,1,0:T(8,128)(2,1)} %refs_1_.1) | copy-start | bytes 1572868
  4.8 16.8 %all-to-all-start = ((bf16[2,2,3,128,128]{4,3,2,1,0:T(8,128)(2,1)}), bf16[2,2,3,128,128]{4,3,2,1,0:T(8,128)(2,1)S(1)}, u32[]{:S(2)}, u32[]{:S(2)}) async-start(bf16[2,2,3,128,128]{4,3,2,1,0:T(8,128)(2,1)} %double.1), calls=%async_computation | async-start | bytes 786432 | tf_op jit(solution)/shard_map/all_to_all | solution.py:432
  12.4 2.6 %collective-permute-start.3 = (bf16[8,3,32,128]{3,2,1,0:T(8,128)(2,1)S(1)}, bf16[8,3,32,128]{3,2,1,0:T(8,128)(2,1)S(1)}, u32[]{:S(2)}, u32[]{:S(2)}) collective-permute-start(bf16[8,3,32,128]{3,2,1,0:T(8,128)(2,1)S(1)} %get-tuple-element.33), channel_id=1, source_target_pairs={{0,1},{1,0},{2,3},{3,2},{4,5},{5,4},{6,7},{7,6},{8,9},{9,8},{10,11... | collective-permute-start | bytes 589832 | tf_op jit(solution)/shard_map/ppermute | solution.py:435
  14.0 10.4 %collective-permute-start.2 = (bf16[8,3,32,128]{3,2,1,0:T(8,128)(2,1)S(1)}, bf16[8,3,32,128]{3,2,1,0:T(8,128)(2,1)S(1)}, u32[]{:S(2)}, u32[]{:S(2)}) collective-permute-start(bf16[8,3,32,128]{3,2,1,0:T(8,128)(2,1)S(1)} %get-tuple-element.32), channel_id=1, source_target_pairs={{0,1},{1,0},{2,3},{3,2},{4,5},{5,4},{6,7},{7,6},{8,9},{9,8},{10,11... | collective-permute-start | bytes 589832 | tf_op jit(solution)/shard_map/ppermute | solution.py:435
  15.1 9.3 %collective-permute-start.4 = (bf16[8,3,32,128]{3,2,1,0:T(8,128)(2,1)S(1)}, bf16[8,3,32,128]{3,2,1,0:T(8,128)(2,1)S(1)}, u32[]{:S(2)}, u32[]{:S(2)}) collective-permute-start(bf16[8,3,32,128]{3,2,1,0:T(8,128)(2,1)S(1)} %pair.1.after), channel_id=1, source_target_pairs={{0,2},{1,3},{2,0},{3,1},{4,6},{5,7},{6,4},{7,5},{8,10},{9,11},{10,... | collective-permute-start | bytes 589832 | tf_op jit(solution)/shard_map/ppermute | solution.py:435
  22.1 2.3 %collective-permute-start.5 = (bf16[208,128]{1,0:T(8,128)(2,1)S(1)}, bf16[208,128]{1,0:T(8,128)(2,1)S(1)}, u32[]{:S(2)}, u32[]{:S(2)}) collective-permute-start(bf16[208,128]{1,0:T(8,128)(2,1)S(1)} %get-tuple-element.38), channel_id=1, source_target_pairs={{0,1},{1,0},{2,3},{3,2},{4,5},{5,4},{6,7},{7,6},{8,9},{9,8},{10,11... | collective-permute-start | bytes 159752 | tf_op jit(solution)/shard_map/ppermute | solution.py:435
  22.7 3.4 %collective-permute-start.6 = (bf16[208,128]{1,0:T(8,128)(2,1)S(1)}, bf16[208,128]{1,0:T(8,128)(2,1)S(1)}, u32[]{:S(2)}, u32[]{:S(2)}) collective-permute-start(bf16[208,128]{1,0:T(8,128)(2,1)S(1)} %get-tuple-element.39), channel_id=1, source_target_pairs={{0,2},{1,3},{2,0},{3,1},{4,6},{5,7},{6,4},{7,5},{8,10},{9,11},{10,... | collective-permute-start | bytes 159752 | tf_op jit(solution)/shard_map/ppermute | solution.py:435
  23.9 3.8 %collective-permute-start.7 = (bf16[208,128]{1,0:T(8,128)(2,1)S(1)}, bf16[208,128]{1,0:T(8,128)(2,1)S(1)}, u32[]{:S(2)}, u32[]{:S(2)}) collective-permute-start(bf16[208,128]{1,0:T(8,128)(2,1)S(1)} %get-tuple-element.40), channel_id=1, source_target_pairs={{0,3},{1,2},{2,1},{3,0},{4,7},{5,6},{6,5},{7,4},{8,11},{9,10},{10,... | collective-permute-start | bytes 159752 | tf_op jit(solution)/shard_map/ppermute | solution.py:435

commit v10 on v9

--- a/solution.py
+++ b/solution.py
@@ -239,9 +239,10 @@
 def mid_kernel(wdev, sdev, order_in, ops_in, *refs):
     nmid = len(MID)
     blocks, refs = refs[:nmid], refs[nmid:]
-    lstage, rstage, early_keep, early_far, early_near, keep, far_give, near_give = refs[:8]
-    order, ops, sems = refs[8:]
-    phys, part = far_give.shape[1], far_give.shape[2]
+    lstage, rstage, named, early_keep, early_far, early_near = refs[:6]
+    keep, far_give, near_give, order, ops, sems = refs[6:]
+    phys, part, blk = near_give.shape[1:]
+    size = phys * part
     loads = [
         pltpu.make_async_copy(order_in, order, sems.at[0]),
         pltpu.make_async_copy(ops_in, ops, sems.at[1]),
@@ -264,30 +265,35 @@
         for q in range(phys):
             keep[0, t, q] = outs[q][:part]
             keep[1, t, q] = outs[q][part : 2 * part]
-            far_give[t, q] = outs[q][2 * part : 3 * part].astype(jnp.bfloat16)
+            at = pl.multiple_of(t * size + q * part, part)
+            far_give[pl.ds(at, part), :] = outs[q][2 * part : 3 * part].astype(jnp.bfloat16)
             near_give[t, q] = outs[q][3 * part :].astype(jnp.bfloat16)
     for s in range(len(EARLY) * SLOTS):
         t = place(EARLY, s)
         for side in range(2):
             keep[side, t] = early_keep[side, s]
-        far_give[t] = early_far[s]
+        at = pl.multiple_of(t * size, size)
+        far_give[pl.ds(at, size), :] = early_far[s].reshape(size, blk)
         near_give[t] = early_near[s]
     for s in range(SLOTS):
         t = order[LAST * SLOTS + s]
         for side in range(2):
             keep[side, t] = jnp.zeros(keep.shape[2:], keep.dtype)
-        far_give[t] = jnp.zeros(far_give.shape[1:], far_give.dtype)
+        at = pl.multiple_of(t * size, size)
+        far_give[pl.ds(at, size), :] = jnp.zeros((size, blk), far_give.dtype)
         near_give[t] = jnp.zeros(near_give.shape[1:], near_give.dtype)
+    far_give[sdev * size :, :] = named[...]
 
 
 def mid(order, ops, blocks, staged, wdev, sdev):
     phys, part, blk = staged[0].shape[2:]
     n = len(blocks) * SLOTS
     give = jax.ShapeDtypeStruct((sdev, phys, part, blk), jnp.bfloat16)
+    flat = jax.ShapeDtypeStruct((sdev * phys * part + NAME_ROWS, blk), jnp.bfloat16)
     return pl.pallas_call(
         functools.partial(mid_kernel, wdev, sdev),
-        out_shape=[jax.ShapeDtypeStruct((2, sdev, phys, part, blk), jnp.float32), give, give],
-        in_specs=[space(pl.ANY)] * 2 + [space(pltpu.VMEM)] * (len(blocks) + 5),
+        out_shape=[jax.ShapeDtypeStruct((2, sdev, phys, part, blk), jnp.float32), flat, give],
+        in_specs=[space(pl.ANY)] * 2 + [space(pltpu.VMEM)] * (len(blocks) + 6),
         out_specs=[space(pltpu.VMEM)] * 3,
         scratch_shapes=[
             pltpu.SMEM(order.shape, order.dtype),
@@ -301,7 +307,7 @@
             transcendentals=0,
         ),
         name="mid",
-    )(order, ops, *blocks, *staged[3:5], *staged[:3])
+    )(order, ops, *blocks, *staged[3:5], staged[6], *staged[:3])
 
 
 def last_kernel(wdev, after, block, lstage, rstage, oprows, named, *gives):
@@ -321,17 +327,19 @@
                 rows = outs[q][i * part : (i + 1) * part].astype(gives[m].dtype)
                 at = s * size + q * part
                 gives[m][at : at + part] = rows
-    for give in gives:
+    for give in gives[:2]:
         give[SLOTS * size :] = named[...].astype(give.dtype)
 
 
 def last(after, block, staged, wdev):
     phys, part, blk = staged[0].shape[2:]
-    shape = (SLOTS * phys * part + NAME_ROWS, blk)
+    size = SLOTS * phys * part
+    shape = (size + NAME_ROWS, blk)
     give = jax.ShapeDtypeStruct(shape, jnp.bfloat16)
+    plain = jax.ShapeDtypeStruct((size, blk), jnp.bfloat16)
     return pl.pallas_call(
         functools.partial(last_kernel, wdev),
-        out_shape=[jax.ShapeDtypeStruct(shape, jnp.float32)] + [give] * 3,
+        out_shape=[jax.ShapeDtypeStruct(shape, jnp.float32), give, plain, plain],
         in_specs=[space(pl.ANY)] + [space(pltpu.VMEM)] * 5,
         out_specs=[space(pltpu.VMEM)] * 4,
         compiler_params=params(),
@@ -344,46 +352,51 @@
     )(after, block, *staged[3:])
 
 
-def pair_kernel(keep, got, out):
-    out[...] = (keep[0] + got[...].astype(jnp.float32)).astype(out.dtype)
-
-
-def pair(keep, got):
+def pair_kernel(keep, got, named, out):
+    rows = got.shape[0] - NAME_ROWS
+    own = keep[0].reshape(rows, out.shape[1])
+    out[:rows, :] = (own + got[:rows, :].astype(jnp.float32)).astype(out.dtype)
+    out[rows : rows + NAME_ROWS, :] = named[...]
+    out[rows + NAME_ROWS :, :] = got[rows:, :]
+
+
+def pair(keep, got, named):
     return pl.pallas_call(
         pair_kernel,
-        out_shape=jax.ShapeDtypeStruct(got.shape, got.dtype),
-        in_specs=[space(pltpu.VMEM)] * 2,
+        out_shape=jax.ShapeDtypeStruct((got.shape[0] + NAME_ROWS, got.shape[1]), got.dtype),
+        in_specs=[space(pltpu.VMEM)] * 3,
         out_specs=space(pltpu.VMEM),
         compiler_params=params(),
         name="pair",
-    )(keep, got)
-
-
-def tail_sum(tails, t, first, count):
+    )(keep, got, named)
+
+
+def tail_sum(tails, t):
     total = None
-    for tail in tails:
-        end = tail.shape[0] - NAME_ROWS
-        size = end // SLOTS
-        names = tail[end:, :].astype(jnp.float32)
+    for rows, names in tails:
+        size = rows.shape[0] // SLOTS
         for s in range(SLOTS):
-            at = s * size + first
-            rows = tail[at : at + count, :].astype(jnp.float32)
-            value = jnp.where(names[s : s + 1] == t, rows, 0.0)
+            part = rows[s * size : (s + 1) * size]
+            value = jnp.where(names[s : s + 1] == t, part.astype(jnp.float32), 0.0)
             total = value if total is None else total + value
     return total
 
 
 def base_kernel(keep, near, far, own, mate, acc):
     sdev, phys, part, blk = acc.shape
+    size = phys * part
+    end = SLOTS * size
+    tails = [(tail[:end, :], tail[end:, :].astype(jnp.float32)) for tail in (own, mate)]
     for t in range(sdev):
-        total = keep[1, t] + near[t].astype(jnp.float32) + far[t].astype(jnp.float32)
-        acc[t] = total + tail_sum((own, mate), t, 0, phys * part).reshape(phys, part, blk)
+        over = far[t * size : (t + 1) * size, :].astype(jnp.float32).reshape(phys, part, blk)
+        total = keep[1, t] + near[t].astype(jnp.float32) + over
+        acc[t] = total + tail_sum(tails, t).reshape(phys, part, blk)
 
 
 def base(keep, near, far, own, mate):
     return pl.pallas_call(
         base_kernel,
-        out_shape=jax.ShapeDtypeStruct(far.shape, jnp.float32),
+        out_shape=jax.ShapeDtypeStruct(near.shape, jnp.float32),
         in_specs=[space(pltpu.VMEM)] * 5,
         out_specs=space(pltpu.VMEM),
         compiler_params=params(),
@@ -391,26 +404,28 @@
     )(keep, near, far, own, mate)
 
 
-def finish_kernel(total, tail2, tail3, out, acc):
+def finish_kernel(total, far, tail2, tail3, out, acc):
     sdev, phys, part, blk = total.shape
+    at = sdev * phys * part
+    names = far[at:, :].astype(jnp.float32)
+    tails = [(tail2[...], names[:NAME_ROWS]), (tail3[...], names[NAME_ROWS:])]
     for t in range(sdev):
-        late = tail_sum((tail2, tail3), t, 0, phys * part).reshape(phys, part, blk)
-        acc[t] = total[t] + late
+        acc[t] = total[t] + tail_sum(tails, t).reshape(phys, part, blk)
     for q in range(phys):
         out[:, q] = jnp.swapaxes(acc[:, q], 0, 1).astype(out.dtype)
 
 
-def finish(total, tail2, tail3):
+def finish(total, far, tail2, tail3):
     sdev, phys, part, blk = total.shape
     return pl.pallas_call(
         finish_kernel,
         out_shape=jax.ShapeDtypeStruct((part, phys, sdev, blk), jnp.bfloat16),
-        in_specs=[space(pltpu.VMEM)] * 3,
+        in_specs=[space(pltpu.VMEM)] * 4,
         out_specs=space(pltpu.VMEM),
         scratch_shapes=[pltpu.VMEM(total.shape, total.dtype)],
         compiler_params=params(),
         name="finish",
-    )(total, tail2, tail3)
+    )(total, far, tail2, tail3)
 
 
 def fast_shards(psi, left_env, right_env, site_op, source):
@@ -436,12 +451,12 @@
 
     staged = early(order, ops, [arrived[k] for k in EARLY], left_env, right_env, nsec, nmpo)
     keep, far_give, near_give = mid(order, ops, [arrived[k] for k in MID], staged, wdev, sdev)
-    summed = pair(keep, across(far_give, 1))
+    summed = pair(keep, across(far_give, 1), staged[6])
     far = across(summed, 2)
     near = across(near_give, 1)
     own, give1, give2, give3 = last(summed, final, staged, wdev)
     total = base(keep, near, far, own, across(give1, 1))
-    out = finish(total, across(give2, 2), across(give3, 3))
+    out = finish(total, far, across(give2, 2), across(give3, 3))
     return jnp.transpose(out, (0, 2, 1, 3))
 
 

time: 28.8 us -> 28.8 us (level)
  waiting for transfers between devices: 9.36 us -> 8.71 us
  starting transfers between devices: 11.5 us -> 12.1 us
    all_to_all x1, waiting for transfers between devices: 5.27 us -> 4.61 us  [fast_shards(): lax.all_to_all(both, 'sec', 0, 0, axis_index_groups=pairs, tiled=True)]
    ppermute x6, starting transfers between devices: 5.2 us -> 5.77 us  [across(): return lax.ppermute(value, 'mpo', [(i, i ^ m) for i in range(nmpo)])]
where the time goes in v10:
time: 28.8 us; the launch traced here: 28.5 us
  starting transfers between devices  12.1 us (42%)
  waiting for transfers between devices  8.71 us (30%)
  Pallas kernels  7.37 us (26%)
    ppermute x6, starting transfers between devices, across(): return lax.ppermute(value, 'mpo', [(i, i ^ m) for i in range(nmpo)])  5.77 us
    all_to_all x1, starting transfers between devices, fast_shards(): lax.all_to_all(both, 'sec', 0, 0, axis_index_groups=pairs, tiled=True)  4.87 us
    all_to_all x1, waiting for transfers between devices, fast_shards(): lax.all_to_all(both, 'sec', 0, 0, axis_index_groups=pairs, tiled=True)  4.61 us
    ppermute x6, waiting for transfers between devices, across(): return lax.ppermute(value, 'mpo', [(i, i ^ m) for i in range(nmpo)])  4.1 us
    ppermute x2, starting transfers between devices, fast_shards(): arrived[k] = lax.ppermute(value, 'sec', [(i, i ^ k) for i in range(nsec)])  1.43 us
    pallas_call x1, Pallas kernels, receive_order(): pl.pallas_call(functools.partial(order_kernel, nsec, sdev), out_shape=jax...  1.36 us
    pallas_call x1, Pallas kernels, early(): pl.pallas_call(functools.partial(early_kernel, nsec, nmpo), out_shape=[ke...  1.27 us
    pallas_call x1, Pallas kernels, route(): pl.pallas_call(functools.partial(route_kernel, classes), out_shape=[jax.S...  1.2 us
  transfers between devices with their start and end apart: 9, of which 4 were waited for; matrix products, arithmetic and copies ran while one was open for 1% of the time, Pallas kernels for 18%

profile of v10, /device:TPU:17, one launch (start us, length us, event | category | flops | bytes accessed | tf_op | source)
XLA Modules:
  0.0 28.5 jit_solution(16684989315617016649)
XLA Ops:
  0.0 1.2 %route.1 = (bf16[2,3,128,128]{3,2,1,0:T(8,128)(2,1)S(1)}, bf16[2,3,128,128]{3,2,1,0:T(8,128)(2,1)S(1)}, bf16[2,3,128,128]{3,2,1,0:T(8,128)(2,1)S(1)}, bf16[2,3,128,128]{3,2,1,0:T(8,128)(2,1)S(1)}) custom-call(s32[1,32]{1,0:T(1,128)} %source.3, bf16[8,3,128,128]{3,2,1,0:T(8,128)(2,1)} %bitcast.2), custom_call_target="tpu_custom_call" | custom-call | tf_op jit(solution)/shard_map/route/pallas_call | solution.py:70
  1.2 0.1 collective-permute-start
  1.3 1.4 %collective-permute-start.1 = (bf16[2,3,128,128]{3,2,1,0:T(8,128)(2,1)S(1)}, bf16[2,3,128,128]{3,2,1,0:T(8,128)(2,1)S(1)}, u32[]{:S(2)}, u32[]{:S(2)}) collective-permute-start(bf16[2,3,128,128]{3,2,1,0:T(8,128)(2,1)S(1)} %get-tuple-element.25), channel_id=1, source_target_pairs={{0,4},{4,0},{8,12},{12,8},{1,5},{5,1},{9,13},{13,9},{2,6},{6,2},{1... | collective-permute-start | bytes 589832 | tf_op jit(solution)/shard_map/ppermute | solution.py:443
  2.7 1.4 %order.1.order_in.after = s32[8]{0:T(128)S(1)} custom-call(s32[1,32]{1,0:T(1,128)} %source.3, bf16[2,3,128,128]{3,2,1,0:T(8,128)(2,1)S(1)} %get-tuple-element.23.after.refs_0_), custom_call_target="tpu_custom_call" | custom-call | tf_op jit(solution)/shard_map/order/pallas_call | solution.py:118
  4.0 0.0 copy-start.1
  4.0 0.8 %double.1 = bf16[2,2,3,128,128]{4,3,2,1,0:T(8,128)(2,1)} custom-call(bf16[2,3,128,128]{3,2,1,0:T(8,128)(2,1)S(1)} %get-tuple-element.35.block, s32[8]{0:T(128)S(1)} %order.1.order_in.after), custom_call_target="tpu_custom_call" | custom-call | tf_op jit(solution)/shard_map/double/pallas_call | solution.py:95
  4.8 0.0 copy-start.2
  4.8 0.0 copy-start
  4.8 4.9 %all-to-all-start = ((bf16[2,2,3,128,128]{4,3,2,1,0:T(8,128)(2,1)}), bf16[2,2,3,128,128]{4,3,2,1,0:T(8,128)(2,1)S(1)}, u32[]{:S(2)}, u32[]{:S(2)}) async-start(bf16[2,2,3,128,128]{4,3,2,1,0:T(8,128)(2,1)} %double.1), calls=%async_computation | async-start | bytes 786432 | tf_op jit(solution)/shard_map/all_to_all | solution.py:447
  9.7 0.0 copy-done.2
  9.7 0.1 copy.6
  9.8 0.1 reshape.8.ops.ops_in
  10.0 0.0 copy-done.1
  10.0 0.0 copy-done
  10.0 1.3 %early.1 = (f32[2,2,3,32,128]{4,3,2,1,0:T(8,128)S(1)}, bf16[2,3,32,128]{3,2,1,0:T(8,128)(2,1)S(1)}, bf16[2,3,32,128]{3,2,1,0:T(8,128)(2,1)S(1)}, bf16[6,256,128]...) custom-call(s32[8]{0:T(128)S(1)} %order.1.order_in.after, ...), custom_call_target="tpu_custom_call" | custom-call | flops 100663296 | bytes 8388608 | tf_op jit(solution)/shard_map/early/pallas_call | solution.py:224
  11.3 0.0 collective-permute-done.refs_0_
  11.3 0.0 collective-permute-done.1.refs_1_
  11.3 1.1 %mid.1 = (f32[2,8,3,32,128]{4,3,2,1,0:T(8,128)S(1)}, bf16[784,128]{1,0:T(8,128)(2,1)S(1)}, bf16[8,3,32,128]{3,2,1,0:T(8,128)(2,1)S(1)}) custom-call(s32[8]{0:T(128)S(1)} %order.1.order_in.after, f32[144]{0:T(256)S(1)} %reshape.8.ops.ops_in, bf16[2,3,128,128]{3,2,1,0:T(8,128)(2,1)S(1)} %collective-permute-done.refs_0_, ...), custom_call_target="tpu_custom_call" | custom-call | flops 201326592 | bytes 8388608 | tf_op jit(solution)/shard_map/mid/pallas_call | solution.py:293
  12.4 1.6 %collective-permute-start.3 = (bf16[784,128]{1,0:T(8,128)(2,1)S(1)}, bf16[784,128]{1,0:T(8,128)(2,1)S(1)}, u32[]{:S(2)}, u32[]{:S(2)}) collective-permute-start(bf16[784,128]{1,0:T(8,128)(2,1)S(1)} %get-tuple-element.34), channel_id=1, source_target_pairs={{0,1},{1,0},{2,3},{3,2},{4,5},{5,4},{6,7},{7,6},{8,9},{9,8},{10,11... | collective-permute-start | bytes 602120 | tf_op jit(solution)/shard_map/ppermute | solution.py:450
  14.0 1.1 %collective-permute-done.3.got = bf16[784,128]{1,0:T(8,128)(2,1)S(1)} collective-permute-done((bf16[784,128]{1,0:T(8,128)(2,1)S(1)}, bf16[784,128]{1,0:T(8,128)(2,1)S(1)}, u32[]{:S(2)}, u32[]{:S(2)}) %collective-permute-start.3) | collective-permute-done | bytes 200736 | tf_op jit(solution)/shard_map/ppermute | solution.py:450
  15.1 1.3 %collective-permute-start.4 = (bf16[800,128]{1,0:T(8,128)(2,1)S(1)}, bf16[800,128]{1,0:T(8,128)(2,1)S(1)}, u32[]{:S(2)}, u32[]{:S(2)}) collective-permute-start(bf16[800,128]{1,0:T(8,128)(2,1)S(1)} %pair.1.after), channel_id=1, source_target_pairs={{0,2},{1,3},{2,0},{3,1},{4,6},{5,7},{6,4},{7,5},{8,10},{9,11},{10,... | collective-permute-start | bytes 614408 | tf_op jit(solution)/shard_map/ppermute | solution.py:450
  16.4 0.7 %collective-permute-start.2 = (bf16[8,3,32,128]{3,2,1,0:T(8,128)(2,1)S(1)}, bf16[8,3,32,128]{3,2,1,0:T(8,128)(2,1)S(1)}, u32[]{:S(2)}, u32[]{:S(2)}) collective-permute-start(bf16[8,3,32,128]{3,2,1,0:T(8,128)(2,1)S(1)} %get-tuple-element.33), channel_id=1, source_target_pairs={{0,1},{1,0},{2,3},{3,2},{4,5},{5,4},{6,7},{7,6},{8,9},{9,8},{10,11... | collective-permute-start | bytes 589832 | tf_op jit(solution)/shard_map/ppermute | solution.py:450
  17.0 4.6 %all-to-all-done.block = bf16[2,2,3,128,128]{4,3,2,1,0:T(8,128)(2,1)S(1)} async-done(((bf16[2,2,3,128,128]{4,3,2,1,0:T(8,128)(2,1)}), bf16[2,2,3,128,128]{4,3,2,1,0:T(8,128)(2,1)S(1)}, u32[]{:S(2)}, u32[]{:S(2)}) %all-to-all-start) | async-done | bytes 393248 | tf_op jit(solution)/shard_map/all_to_all | solution.py:447
  21.6 0.5 %last.1 = (f32[208,128]{1,0:T(8,128)S(1)}, bf16[208,128]{1,0:T(8,128)(2,1)S(1)}, bf16[192,128]{1,0:T(8,128)(2,1)S(1)}, bf16[192,128]{1,0:T(8,128)(2,1)S(1)}) custom-call(bf16[800,128]{1,0:T(8,128)(2,1)S(1)} %pair.1.after, bf16[2,2,3,128,128]{4,3,2,1,0:T(8,128)(2,1)S(1)} %all-to-all-done.block, bf16[6,256,128]{2,1,0:T(8,128)(2,1)S(1)} %get-tuple-element.26.refs_2_.lstage, ...), custom_call_target="tpu_custom_call" | custom-call | flops 100663296 | bytes 4194304 | tf_op jit(solution)/shard_map/last/pallas_call | solution.py:340
  22.1 0.6 %collective-permute-start.5 = (bf16[208,128]{1,0:T(8,128)(2,1)S(1)}, bf16[208,128]{1,0:T(8,128)(2,1)S(1)}, u32[]{:S(2)}, u32[]{:S(2)}) collective-permute-start(bf16[208,128]{1,0:T(8,128)(2,1)S(1)} %get-tuple-element.38), channel_id=1, source_target_pairs={{0,1},{1,0},{2,3},{3,2},{4,5},{5,4},{6,7},{7,6},{8,9},{9,8},{10,11... | collective-permute-start | bytes 159752 | tf_op jit(solution)/shard_map/ppermute | solution.py:450
  22.7 1.2 %collective-permute-start.6 = (bf16[192,128]{1,0:T(8,128)(2,1)S(1)}, bf16[192,128]{1,0:T(8,128)(2,1)S(1)}, u32[]{:S(2)}, u32[]{:S(2)}) collective-permute-start(bf16[192,128]{1,0:T(8,128)(2,1)S(1)} %get-tuple-element.39), channel_id=1, source_target_pairs={{0,2},{1,3},{2,0},{3,1},{4,6},{5,7},{6,4},{7,5},{8,10},{9,11},{10,... | collective-permute-start | bytes 147464 | tf_op jit(solution)/shard_map/ppermute | solution.py:450
  23.9 0.5 %collective-permute-start.7 = (bf16[192,128]{1,0:T(8,128)(2,1)S(1)}, bf16[192,128]{1,0:T(8,128)(2,1)S(1)}, u32[]{:S(2)}, u32[]{:S(2)}) collective-permute-start(bf16[192,128]{1,0:T(8,128)(2,1)S(1)} %get-tuple-element.40), channel_id=1, source_target_pairs={{0,3},{1,2},{2,1},{3,0},{4,7},{5,6},{6,5},{7,4},{8,11},{9,10},{10,... | collective-permute-start | bytes 147464 | tf_op jit(solution)/shard_map/ppermute | solution.py:450
  24.4 0.0 collective-permute-done.2.near
  24.4 0.0 collective-permute-done.5.mate
  24.4 0.0 collective-permute-done.4.far
  24.4 0.2 base.1.total
  24.6 1.0 %collective-permute-done.6.tail2 = bf16[192,128]{1,0:T(8,128)(2,1)S(1)} collective-permute-done((bf16[192,128]{1,0:T(8,128)(2,1)S(1)}, bf16[192,128]{1,0:T(8,128)(2,1)S(1)}, u32[]{:S(2)}, u32[]{:S(2)}) %collective-permute-start.6) | collective-permute-done | bytes 49184 | tf_op jit(solution)/shard_map/ppermute | solution.py:450
  25.7 2.0 %collective-permute-done.7.tail3 = bf16[192,128]{1,0:T(8,128)(2,1)S(1)} collective-permute-done((bf16[192,128]{1,0:T(8,128)(2,1)S(1)}, bf16[192,128]{1,0:T(8,128)(2,1)S(1)}, u32[]{:S(2)}, u32[]{:S(2)}) %collective-permute-start.7) | collective-permute-done | bytes 49184 | tf_op jit(solution)/shard_map/ppermute | solution.py:450
  27.6 0.9 %finish.1 = bf16[32,3,8,128]{3,2,1,0:T(8,128)(2,1)} custom-call(f32[8,3,32,128]{3,2,1,0:T(8,128)S(1)} %base.1.total, bf16[800,128]{1,0:T(8,128)(2,1)S(1)} %collective-permute-done.4.far, bf16[192,128]{1,0:T(8,128)(2,1)S(1)} %collective-permute-done.6.tail2, bf16[192,128]{1,0:T(8,128)(2,1)S(1)} %collective-permute-done.7.tail3), custom_call_target="tpu_custom_call" | custom-call | tf_op jit(solution)/shard_map/finish/pallas_call | solution.py:420
  (1 shorter events, 0.0 us)
Async XLA Ops:
  1.2 10.1 %collective-permute-start = (bf16[2,3,128,128]{3,2,1,0:T(8,128)(2,1)S(1)}, bf16[2,3,128,128]{3,2,1,0:T(8,128)(2,1)S(1)}, u32[]{:S(2)}, u32[]{:S(2)}) collective-permute-start(bf16[2,3,128,128]{3,2,1,0:T(8,128)(2,1)S(1)} %get-tuple-element.24), channel_id=1, source_target_pairs={{0,8},{4,12},{8,0},{12,4},{1,9},{5,13},{9,1},{13,5},{2,10},{6,14},... | collective-permute-start | bytes 589832 | tf_op jit(solution)/shard_map/ppermute | solution.py:443
  1.3 10.0 %collective-permute-start.1 = (bf16[2,3,128,128]{3,2,1,0:T(8,128)(2,1)S(1)}, bf16[2,3,128,128]{3,2,1,0:T(8,128)(2,1)S(1)}, u32[]{:S(2)}, u32[]{:S(2)}) collective-permute-start(bf16[2,3,128,128]{3,2,1,0:T(8,128)(2,1)S(1)} %get-tuple-element.25), channel_id=1, source_target_pairs={{0,4},{4,0},{8,12},{12,8},{1,5},{5,1},{9,13},{13,9},{2,6},{6,2},{1... | collective-permute-start | bytes 589832 | tf_op jit(solution)/shard_map/ppermute | solution.py:443
  4.0 5.9 %copy-start.1 = (bf16[2,8,128,128]{3,2,1,0:T(8,128)(2,1)S(1)}, bf16[2,8,128,128]{3,2,1,0:T(8,128)(2,1)}, u32[]{:S(2)}) copy-start(bf16[2,8,128,128]{3,2,1,0:T(8,128)(2,1)} %refs_2_.1) | copy-start | bytes 1572868
  4.8 4.9 %copy-start.2 = (bf16[2,8,3,3]{1,0,3,2:T(2,128)(2,1)S(1)}, bf16[2,8,3,3]{1,0,3,2:T(2,128)(2,1)}, u32[]{:S(2)}) copy-start(bf16[2,8,3,3]{1,0,3,2:T(2,128)(2,1)} %param.8) | copy-start | bytes 868
  4.8 5.1 %copy-start = (bf16[2,8,128,128]{3,2,1,0:T(8,128)(2,1)S(1)}, bf16[2,8,128,128]{3,2,1,0:T(8,128)(2,1)}, u32[]{:S(2)}) copy-start(bf16[2,8,128,128]{3,2,1,0:T(8,128)(2,1)} %refs_1_.1) | copy-start | bytes 1572868
  4.8 16.8 %all-to-all-start = ((bf16[2,2,3,128,128]{4,3,2,1,0:T(8,128)(2,1)}), bf16[2,2,3,128,128]{4,3,2,1,0:T(8,128)(2,1)S(1)}, u32[]{:S(2)}, u32[]{:S(2)}) async-start(bf16[2,2,3,128,128]{4,3,2,1,0:T(8,128)(2,1)} %double.1), calls=%async_computation | async-start | bytes 786432 | tf_op jit(solution)/shard_map/all_to_all | solution.py:447
  12.4 2.7 %collective-permute-start.3 = (bf16[784,128]{1,0:T(8,128)(2,1)S(1)}, bf16[784,128]{1,0:T(8,128)(2,1)S(1)}, u32[]{:S(2)}, u32[]{:S(2)}) collective-permute-start(bf16[784,128]{1,0:T(8,128)(2,1)S(1)} %get-tuple-element.34), channel_id=1, source_target_pairs={{0,1},{1,0},{2,3},{3,2},{4,5},{5,4},{6,7},{7,6},{8,9},{9,8},{10,11... | collective-permute-start | bytes 602120 | tf_op jit(solution)/shard_map/ppermute | solution.py:450
  15.1 9.3 %collective-permute-start.4 = (bf16[800,128]{1,0:T(8,128)(2,1)S(1)}, bf16[800,128]{1,0:T(8,128)(2,1)S(1)}, u32[]{:S(2)}, u32[]{:S(2)}) collective-permute-start(bf16[800,128]{1,0:T(8,128)(2,1)S(1)} %pair.1.after), channel_id=1, source_target_pairs={{0,2},{1,3},{2,0},{3,1},{4,6},{5,7},{6,4},{7,5},{8,10},{9,11},{10,... | collective-permute-start | bytes 614408 | tf_op jit(solution)/shard_map/ppermute | solution.py:450
  16.4 8.0 %collective-permute-start.2 = (bf16[8,3,32,128]{3,2,1,0:T(8,128)(2,1)S(1)}, bf16[8,3,32,128]{3,2,1,0:T(8,128)(2,1)S(1)}, u32[]{:S(2)}, u32[]{:S(2)}) collective-permute-start(bf16[8,3,32,128]{3,2,1,0:T(8,128)(2,1)S(1)} %get-tuple-element.33), channel_id=1, source_target_pairs={{0,1},{1,0},{2,3},{3,2},{4,5},{5,4},{6,7},{7,6},{8,9},{9,8},{10,11... | collective-permute-start | bytes 589832 | tf_op jit(solution)/shard_map/ppermute | solution.py:450
  22.1 2.3 %collective-permute-start.5 = (bf16[208,128]{1,0:T(8,128)(2,1)S(1)}, bf16[208,128]{1,0:T(8,128)(2,1)S(1)}, u32[]{:S(2)}, u32[]{:S(2)}) collective-permute-start(bf16[208,128]{1,0:T(8,128)(2,1)S(1)} %get-tuple-element.38), channel_id=1, source_target_pairs={{0,1},{1,0},{2,3},{3,2},{4,5},{5,4},{6,7},{7,6},{8,9},{9,8},{10,11... | collective-permute-start | bytes 159752 | tf_op jit(solution)/shard_map/ppermute | solution.py:450
  22.7 3.0 %collective-permute-start.6 = (bf16[192,128]{1,0:T(8,128)(2,1)S(1)}, bf16[192,128]{1,0:T(8,128)(2,1)S(1)}, u32[]{:S(2)}, u32[]{:S(2)}) collective-permute-start(bf16[192,128]{1,0:T(8,128)(2,1)S(1)} %get-tuple-element.39), channel_id=1, source_target_pairs={{0,2},{1,3},{2,0},{3,1},{4,6},{5,7},{6,4},{7,5},{8,10},{9,11},{10,... | collective-permute-start | bytes 147464 | tf_op jit(solution)/shard_map/ppermute | solution.py:450
  23.9 3.7 %collective-permute-start.7 = (bf16[192,128]{1,0:T(8,128)(2,1)S(1)}, bf16[192,128]{1,0:T(8,128)(2,1)S(1)}, u32[]{:S(2)}, u32[]{:S(2)}) collective-permute-start(bf16[192,128]{1,0:T(8,128)(2,1)S(1)} %get-tuple-element.40), channel_id=1, source_target_pairs={{0,3},{1,2},{2,1},{3,0},{4,7},{5,6},{6,5},{7,4},{8,11},{9,10},{10,... | collective-permute-start | bytes 147464 | tf_op jit(solution)/shard_map/ppermute | solution.py:450
